TPU v7x, 512 devices: a whole 4x4x16 slice. The times are simulated.
512 devices in a mesh: tile: 64 (over z, y_lo, core), seq: 8 (over x, y_hi).
Axes of the slice: x: 4, y: 4 (y_hi: 2, y_lo: 2; y = y_hi * 2 + y_lo), z: 16, core: 2. Of those that a mesh axis runs over, the one named last changes fastest.
Arguments:
- tokens: bfloat16 [64, 2048, 1152], P('tile', 'seq'), may hold values from -6 to 6
- mod_shift: float32 [64, 1152], P('tile'), may hold values from -3 to 3
- mod_scale: float32 [64, 1152], P('tile'), may hold values from -0.9 to 3.5
- mod_gate: float32 [64, 1152], P('tile'), may hold values from -6 to 6
- w_qkv: bfloat16 [3, 1152, 576], P(None, None, 'seq'), may hold values from -0.29882812 to 0.29882812
- w_out: bfloat16 [576, 1152], P('seq'), may hold values from -0.25 to 0.25
- east_rows: int32 [64, 256], P('tile', 'seq'), may hold values from 0 to 255, as said below
- west_rows: int32 [64, 256], P('tile', 'seq'), may hold values from 0 to 255, as said below
- blend_weight: int32 [64, 256], P(None, 'seq'), may hold values from 1 to 7
Outputs:
- blended: bfloat16 [64, 2048, 1152], P('tile', 'seq')
Inputs may be any that keep to these rules, and one draw needn't show every extreme that they name: In each tile and each block of 32 entries (one block of 256 tokens), the east_rows entries are distinct and none equals a west_rows entry of the same block. `west_rows`: distinct within each block of 32 entries, disjoint from east_rows of the same block.
All inputs are finite; a program needn't handle non-finite values.
Results may differ from a plain program's by a relative error of at most 0.02.
Values may be sent and summed in bfloat16 or wider, within the bound.
No kernel may reach another device: no remote copies, remote signals or barrier semaphores. Data moves between devices by JAX's collectives and lax.ppermute only.
A program may use at most 64 MiB of HBM per device.

v0:
```python
import jax
import jax.numpy as jnp
from jax import lax
from jax.sharding import PartitionSpec as P

HD = 72
HEADS = 8
HQ = 576


def shifted(value, axis, by):
    count = lax.axis_size(axis)
    return lax.ppermute(value, axis, [(i, (i + by) % count) for i in range(count)])


def layer_norm(values):
    mean = jnp.mean(values, axis=-1, keepdims=True)
    centered = values - mean
    var = jnp.mean(centered * centered, axis=-1, keepdims=True)
    return centered * lax.rsqrt(var + 1e-06)


def attend_block(carry, query, keys, values):
    best, total, summed = carry
    count = keys.shape[0]
    head_count = query.shape[1]
    keys = keys.reshape(count, head_count, HD)
    values = values.reshape(count, head_count, HD)
    scores = jnp.einsum("qhd,khd->hqk", query, keys, preferred_element_type=jnp.float32) * HD ** (
        -0.5
    )
    peak = jnp.maximum(best, jnp.max(scores, axis=-1))
    factor = jnp.exp(best - peak)
    expo = jnp.exp(scores - peak[:, :, None])
    total = total * factor + jnp.sum(expo, axis=-1)
    summed = summed * jnp.transpose(factor)[:, :, None] + jnp.einsum(
        "hqk,khd->qhd", expo.astype(jnp.bfloat16), values, preferred_element_type=jnp.float32
    )
    return (peak, total, summed)


def fold_keys(carry, query, key_rows, value_rows):
    count = key_rows.shape[0]
    width = key_rows.shape[1]
    key_blocks = key_rows.reshape(count // 512, 512, width)
    value_blocks = value_rows.reshape(count // 512, 512, width)

    def step(inner, blocks):
        return (attend_block(inner, query, blocks[0], blocks[1]), None)

    carry, unused = lax.scan(step, carry, (key_blocks, value_blocks))
    return carry


def start_state(head_count, query_rows):
    return (
        jnp.full((head_count, query_rows), -1e30, jnp.float32),
        jnp.zeros((head_count, query_rows), jnp.float32),
        jnp.zeros((query_rows, head_count, HD), jnp.float32),
    )


def body(tokens, mod_shift, mod_scale, mod_gate, w_qkv, w_out, east_rows, west_rows, blend_weight):
    x_rows = tokens[0]
    rows = x_rows.shape[0]
    normed = layer_norm(x_rows.astype(jnp.float32))
    modulated = (normed * (1.0 + mod_scale) + mod_shift).astype(jnp.bfloat16)
    qkv = jnp.einsum(
        "td,idc->itc",
        modulated,
        lax.all_gather(w_qkv, "seq", axis=2, tiled=True),
        preferred_element_type=jnp.float32,
    ).astype(jnp.bfloat16)
    query = qkv[0].reshape(rows, HEADS, HD)
    best, total, summed = fold_keys(
        start_state(HEADS, rows),
        query,
        lax.all_gather(qkv[1], "seq", axis=0, tiled=True),
        lax.all_gather(qkv[2], "seq", axis=0, tiled=True),
    )
    attn = (summed / jnp.transpose(total)[:, :, None]).reshape(rows, HQ).astype(jnp.bfloat16)
    proj = jnp.dot(
        attn, lax.all_gather(w_out, "seq", axis=0, tiled=True), preferred_element_type=jnp.float32
    )
    layer_out = (x_rows.astype(jnp.float32) + mod_gate * proj).astype(jnp.bfloat16)
    east_index = east_rows[0]
    west_index = west_rows[0]
    own_east = jnp.take(layer_out, east_index, axis=0)
    own_west = jnp.take(layer_out, west_index, axis=0)
    prev_east = shifted(own_east, "tile", 1)
    next_west = shifted(own_west, "tile", -1)
    tile_id = lax.axis_index("tile")
    tile_count = lax.axis_size("tile")
    weight_east = lax.dynamic_index_in_dim(blend_weight, tile_id, 0, keepdims=False).astype(
        jnp.float32
    )[:, None]
    weight_west = lax.dynamic_index_in_dim(
        blend_weight, (tile_id + tile_count - 1) % tile_count, 0, keepdims=False
    ).astype(jnp.float32)[:, None]
    new_east = (
        weight_east * own_east.astype(jnp.float32)
        + (8.0 - weight_east) * next_west.astype(jnp.float32)
    ) / 8.0
    new_west = (
        (8.0 - weight_west) * own_west.astype(jnp.float32)
        + weight_west * prev_east.astype(jnp.float32)
    ) / 8.0
    blended = layer_out.at[east_index].set(new_east.astype(jnp.bfloat16))
    blended = blended.at[west_index].set(new_west.astype(jnp.bfloat16))
    return blended[None]


def solution(mesh):
    in_specs = (
        P("tile", "seq", None),
        P("tile", None),
        P("tile", None),
        P("tile", None),
        P(None, None, "seq"),
        P("seq", None),
        P("tile", "seq"),
        P("tile", "seq"),
        P(None, "seq"),
    )
    out_specs = P("tile", "seq", None)
    return jax.shard_map(body, mesh=mesh, in_specs=in_specs, out_specs=out_specs, check_vma=False)
```

profile of v0, /device:TPU:2, one launch (start us, length us, event | category | flops | bytes accessed | tf_op | source)
XLA Modules:
  0.0 347.0 jit_solution(1889906502308558701)
XLA Ops:
  8.7 1.2 convert_reduce_fusion
  10.0 1.4 fusion.22
  11.3 87.7 %all-gather.7.cloned.1.call-done = bf16[3,1152,576]{1,2,0:T(8,128)(2,1)} async-done(((bf16[3,1152,72]{1,2,0:T(8,128)(2,1)}), bf16[3,1152,576]{1,2,0:T(8,128)(2,1)}) %all-gather.7.cloned.1.call-update) | async-done | bytes 3981328 | tf_op jit(solution)/shard_map/all_gather | solution.py:71
  99.0 3.8 %fusion.21 = bf16[3,256,576]{1,2,0:T(8,128)(2,1)S(1)} fusion(bf16[3,1152,576]{1,2,0:T(8,128)(2,1)} %all-gather.7.cloned.1.call-done, bf16[1,256,1152]{2,1,0:T(8,128)(2,1)} %param.13, f32[1152]{0:T(1024)S(1)} %reduce.3, f32[1152]{0:T(1024)S(1)} %add_reduce_fusion, f32[256]{0:T(256)S(1)} %add_rsqrt_fusion, f32[256]{0:T(256)S(1)} %broadcast_multiply_fusion), kind=kOutput, calls=%fused_computation.32 | convolution fusion | flops 1021427712 | bytes 5467136 | tf_op jit(solution)/shard_map/td,idc->itc/dot_general | solution.py:68
  102.9 0.9 fusion.42
  109.5 68.8 %all-gather.11.cloned.1.call-done = bf16[1,2048,576]{1,2,0:T(8,128)(2,1)} async-done(((bf16[1,256,576]{1,2,0:T(8,128)(2,1)}), bf16[1,2048,576]{1,2,0:T(8,128)(2,1)}) %all-gather.11.cloned.1.call-update) | async-done | bytes 2359312 | tf_op jit(solution)/shard_map/all_gather | solution.py:78
  178.3 6.2 %reshape.115 = bf16[4,512,576]{1,0,2:T(4,128)(2,1)} reshape(bf16[1,2048,576]{1,2,0:T(8,128)(2,1)} %all-gather.11.cloned.1.call-done) | data formatting | bytes 4718592 | tf_op jit(solution)/shard_map/reshape | solution.py:45
  184.4 2.1 copy.14
  186.6 69.1 %all-gather.13.cloned.1.call-done = bf16[1,2048,576]{1,2,0:T(8,128)(2,1)} async-done(((bf16[1,256,576]{1,2,0:T(8,128)(2,1)}), bf16[1,2048,576]{1,2,0:T(8,128)(2,1)}) %all-gather.13.cloned.1.call-update) | async-done | bytes 2359312 | tf_op jit(solution)/shard_map/all_gather | solution.py:79
  255.7 6.2 %reshape.116 = bf16[4,512,576]{1,0,2:T(4,128)(2,1)} reshape(bf16[1,2048,576]{1,2,0:T(8,128)(2,1)} %all-gather.13.cloned.1.call-done) | data formatting | bytes 4718592 | tf_op jit(solution)/shard_map/reshape | solution.py:46
  261.8 3.5 %copy.15 = bf16[4,512,576]{1,2,0:T(8,128)(2,1)} copy(bf16[4,512,576]{1,0,2:T(4,128)(2,1)} %reshape.116) | data formatting | bytes 4718592
  265.4 33.5 %while.15 = (s32[]{:T(128)}, f32[8,256]{1,0:T(8,128)S(1)}, f32[8,256]{1,0:T(8,128)}, f32[256,8,72]{0,2,1:T(8,128)S(1)}, bf16[4,512,576]{1,2,0:T(8,128)(2,1)S(1)}...) while((s32[]{:T(128)}, f32[8,256]{1,0:T(8,128)S(1)}, ...), condition=%wide.region_5.6_spmd.clone, body=%wide.region_2.5_spmd.clone.sunk | while | flops 310833152 | bytes 35750116 | solution.py:51
  265.4 1.2 constant_dynamic-slice_fusion.3
  266.6 2.7 bitcast_reduce_fusion.2
  269.3 3.0 fusion.62
  273.7 1.2 constant_dynamic-slice_fusion.3
  275.0 2.7 bitcast_reduce_fusion.2
  277.7 3.0 fusion.62
  282.1 1.2 constant_dynamic-slice_fusion.3
  283.3 2.7 bitcast_reduce_fusion.2
  286.1 3.0 fusion.62
  289.6 0.9 fusion.64
  290.5 1.2 constant_dynamic-slice_fusion.3
  291.7 2.7 bitcast_reduce_fusion.2
  294.5 3.0 fusion.62
  299.7 22.7 %all-gather.9.cloned.1.call-done = bf16[576,1152]{1,0:T(8,128)(2,1)} async-done(((bf16[72,1152]{1,0:T(8,128)(2,1)}), bf16[576,1152]{1,0:T(8,128)(2,1)}) %all-gather.9.cloned.1.call-update) | async-done | bytes 1327120 | tf_op jit(solution)/shard_map/all_gather | solution.py:83
  322.4 2.2 fusion.17
  325.5 4.2 %collective-permute-start = (bf16[32,1152]{1,0:T(8,128)(2,1)S(1)}, bf16[32,1152]{1,0:T(8,128)(2,1)S(1)}, u32[]{:S(2)}, u32[]{:S(2)}) collective-permute-start(bf16[32,1152]{1,0:T(8,128)(2,1)S(1)} %broadcast_select_fusion), channel_id=1, source_target_pairs={{0,504},{8,0},{16,8},{24,16},{32,24},{40,32},{48,40},{56,48},{64,5... | collective-permute-start | bytes 221192 | tf_op jit(solution)/shard_map/ppermute | solution.py:13
  330.6 1.9 collective-permute-start.1
  332.5 1.3 scatter_custom_fusion
  333.9 4.5 %collective-permute-done.1 = bf16[32,1152]{1,0:T(8,128)(2,1)S(1)} collective-permute-done((bf16[32,1152]{1,0:T(8,128)(2,1)S(1)}, bf16[32,1152]{1,0:T(8,128)(2,1)S(1)}, u32[]{:S(2)}, u32[]{:S(2)}) %collective-permute-start.1) | collective-permute-done | bytes 73760 | tf_op jit(solution)/shard_map/ppermute | solution.py:13
  338.3 1.3 scatter_custom_fusion.1
  (95 shorter events, 15.5 us)
Async XLA Ops:
  6.5 92.5 %all-gather.7.cloned.1.call-start = ((), (), s32[]{:S(2)}) async-start(), calls=%async_computation | async-start | bytes 4478976 | tf_op jit(solution)/shard_map/all_gather | solution.py:71
  7.3 171.0 %all-gather.11.cloned.1.call-start = ((), (), s32[]{:S(2)}) async-start(), calls=%async_computation.2 | async-start | bytes 2654208 | tf_op jit(solution)/shard_map/all_gather | solution.py:78
  102.8 2.4 copy-start.9
  102.8 2.4 copy-start.10
  102.8 4.1 %copy-start.6 = (f32[1,1152]{1,0:T(1,128)S(1)}, f32[1,1152]{1,0:T(1,128)}, u32[]{:S(2)}) copy-start(f32[1,1152]{1,0:T(1,128)} %param.16) | copy-start | bytes 13828
  102.9 5.9 %copy-start.5 = (s32[64,32]{0,1:T(8,128)S(1)}, s32[64,32]{0,1:T(8,128)}, u32[]{:S(2)}) copy-start(s32[64,32]{0,1:T(8,128)} %param.21) | copy-start | bytes 24580
  103.8 151.8 %all-gather.13.cloned.1.call-start = ((), (), s32[]{:S(2)}) async-start(), calls=%async_computation.3 | async-start | bytes 2654208 | tf_op jit(solution)/shard_map/all_gather | solution.py:79
  104.6 217.9 %all-gather.9.cloned.1.call-start = ((), (), s32[]{:S(2)}) async-start(), calls=%async_computation.1 | async-start | bytes 1492992 | tf_op jit(solution)/shard_map/all_gather | solution.py:83
  265.4 1.2 copy-start.1
  269.3 3.1 copy-start.3
  269.3 3.5 copy-start
  272.4 1.3 copy-start.4
  273.7 1.2 copy-start.1
  277.7 3.1 copy-start.3
  277.7 3.5 %copy-start = (f32[8,512,256]{2,1,0:T(8,128)S(1)}, f32[8,512,256]{2,1,0:T(8,128)}, u32[]{:S(2)}) copy-start(f32[8,512,256]{2,1,0:T(8,128)} %get-tuple-element.167) | copy-start | bytes 12582916 | tf_op jit(solution)/shard_map/while
  280.8 1.3 copy-start.4
  282.1 1.2 copy-start.1
  286.1 3.1 copy-start.3
  286.1 3.5 copy-start
  289.2 1.3 copy-start.4
  290.5 1.2 copy-start.1
  294.5 3.1 copy-start.3
  294.5 3.5 copy-start
  297.6 1.3 copy-start.4
  298.9 26.5 %copy-start.11 = (pred[32]{0:T(512)(128)(4,1)S(1)}, pred[32]{0:T(512)(128)(4,1)}, u32[]{:S(2)}) copy-start(pred[32]{0:T(512)(128)(4,1)} %compare_and_fusion) | copy-start | bytes 100
  299.7 30.8 %copy-start.12 = (pred[32]{0:T(512)(128)(4,1)S(1)}, pred[32]{0:T(512)(128)(4,1)}, u32[]{:S(2)}) copy-start(pred[32]{0:T(512)(128)(4,1)} %compare_and_fusion.1) | copy-start | bytes 100
  299.7 32.8 %copy-start.7 = (f32[32]{0:T(128)S(1)}, f32[32]{0:T(128)}, u32[]{:S(2)}) copy-start(f32[32]{0:T(128)} %get-tuple-element.84) | copy-start | bytes 388
  299.7 32.8 %copy-start.8 = (f32[32]{0:T(128)S(1)}, f32[32]{0:T(128)}, u32[]{:S(2)}) copy-start(f32[32]{0:T(128)} %get-tuple-element.85) | copy-start | bytes 388
  325.5 7.0 %collective-permute-start = (bf16[32,1152]{1,0:T(8,128)(2,1)S(1)}, bf16[32,1152]{1,0:T(8,128)(2,1)S(1)}, u32[]{:S(2)}, u32[]{:S(2)}) collective-permute-start(bf16[32,1152]{1,0:T(8,128)(2,1)S(1)} %broadcast_select_fusion), channel_id=1, source_target_pairs={{0,504},{8,0},{16,8},{24,16},{32,24},{40,32},{48,40},{56,48},{64,5... | collective-permute-start | bytes 221192 | tf_op jit(solution)/shard_map/ppermute | solution.py:13
  330.6 7.8 %collective-permute-start.1 = (bf16[32,1152]{1,0:T(8,128)(2,1)S(1)}, bf16[32,1152]{1,0:T(8,128)(2,1)S(1)}, u32[]{:S(2)}, u32[]{:S(2)}) collective-permute-start(bf16[32,1152]{1,0:T(8,128)(2,1)S(1)} %broadcast_select_fusion.1), channel_id=1, source_target_pairs={{0,8},{8,16},{16,24},{24,32},{32,40},{40,48},{48,56},{56,64},{64,7... | collective-permute-start | bytes 221192 | tf_op jit(solution)/shard_map/ppermute | solution.py:13
  339.7 0.8 copy-start.2
Sparse Core Ops, SparseCore 0:
  10.6 88.4 all-gather.6
  104.0 74.2 all-gather.10
  181.3 74.3 all-gather.12
  258.7 63.7 all-gather.8
where the time goes:
time: 348 us; the launch traced here: 347 us
  waiting for transfers between devices  255 us (73%)
  local copies, waits for them, and re-layouts  27.6 us (8%)
  other arithmetic  24.1 us (7%)
  matrix products  20.7 us (6%)
  between operations  13.4 us (4%)
  starting transfers between devices  6.22 us (2%)
    all_gather x1, waiting for transfers between devices, body(): lax.all_gather(w_qkv, 'seq', axis=2, tiled=True)  87.7 us
    all_gather x1, waiting for transfers between devices, body(): lax.all_gather(qkv[2], 'seq', axis=0, tiled=True)  69.1 us
    all_gather x1, waiting for transfers between devices, body(): lax.all_gather(qkv[1], 'seq', axis=0, tiled=True)  68.8 us
    all_gather x1, waiting for transfers between devices, body(): lax.all_gather(w_out, 'seq', axis=0, tiled=True)  22.7 us
    reduce_sum x4, other arithmetic, attend_block(): total = total * factor + jnp.sum(expo, axis=-1)  12.1 us
    dot_general x4, matrix products, attend_block(): jnp.einsum('qhd,khd->hqk', query, keys, preferred_element_type=jnp.float32)  10.9 us
  transfers between devices with their start and end apart: 6, of which 5 were waited for; matrix products, arithmetic and copies ran while one was open for 18% of the time, Pallas kernels for 0%

commit v1 on v0

v1 whole, which is shorter than its diff:
```python
import functools
import math

import jax
import jax.numpy as jnp
from jax import lax
from jax.experimental import pallas as pl
from jax.experimental.pallas import tpu as pltpu
from jax.sharding import Mesh
from jax.sharding import PartitionSpec as P

D = 1152
HD = 72
TOK = 256
OV = 32
TILE = ("z", "ylo", "core")
SEQ = ("x", "yhi")
VMEM = pl.BlockSpec(memory_space=pltpu.VMEM)
BF = jnp.bfloat16
F32 = jnp.float32


def call(kernel, outs, args, flops, nbytes, transcendentals=0, vmem=48):
    return pl.pallas_call(
        kernel,
        out_shape=outs,
        in_specs=[VMEM] * len(args),
        out_specs=jax.tree.map(lambda _: VMEM, outs),
        compiler_params=pltpu.CompilerParams(vmem_limit_bytes=vmem * 1024 * 1024),
        cost_estimate=pl.CostEstimate(
            flops=flops, bytes_accessed=nbytes, transcendentals=transcendentals
        ),
    )(*args)


def pack_kernel(w_ref, wo_ref, out_ref):
    core = lax.axis_index("core")

    def put(first, second):
        both = jnp.concatenate([first.astype(F32), second.astype(F32)], axis=0).astype(BF)
        for i in range(4):
            out_ref[i] = both

    @pl.when(core == 0)
    def _():
        put(w_ref[0], w_ref[1])

    @pl.when(core == 1)
    def _():
        put(w_ref[2], wo_ref[...])


def modulate(x_ref, shift, scale):
    x = x_ref[...].astype(F32)
    mean = jnp.sum(x, axis=-1, keepdims=True) * (1.0 / D)
    centered = x - mean
    var = jnp.sum(centered * centered, axis=-1, keepdims=True) * (1.0 / D)
    normed = centered * lax.rsqrt(var + 1e-06)
    return (normed * (1.0 + scale) + shift).astype(BF)


def norm_kernel(x_ref, xo_ref, shift_ref, scale_ref, out_ref):
    shift = shift_ref[...]
    scale = scale_ref[...]
    out_ref[:TOK] = modulate(x_ref, shift, scale)
    out_ref[TOK:] = modulate(xo_ref, shift, scale)


def qkv_kernel(mod_ref, mine_ref, other_ref, out_ref, wo_ref):
    core = lax.axis_index("core")
    mod = mod_ref[...]

    def go(qk_ref, vo_ref):
        for h in range(4):
            qk = lax.dot_general(
                qk_ref[h], mod, (((1,), (1,)), ((), ())), preferred_element_type=F32
            )
            vw = vo_ref[h]
            v = lax.dot_general(
                vw[:80], mod, (((1,), (1,)), ((), ())), preferred_element_type=F32
            )
            out_ref[h] = jnp.concatenate([qk, v[:HD]], axis=0).astype(BF)
            wo_ref[h] = vw.astype(F32)[HD:].astype(BF)

    @pl.when(core == 0)
    def _():
        go(mine_ref, other_ref)

    @pl.when(core == 1)
    def _():
        go(other_ref, mine_ref)


def attention_kernel(qkv_ref, out_ref):
    yhi = lax.axis_index("yhi")
    factor = math.log2(math.e) * HD**-0.5
    keys = []
    values = []
    queries = []
    ones = jnp.ones((8, 2 * TOK), F32)
    for b in range(4):
        block = qkv_ref[b].astype(F32)
        q = block[:HD] * factor
        hi = q.astype(BF).astype(F32)
        lo = q - hi
        k = block[HD : 2 * HD]
        queries.append(jnp.concatenate([hi, lo], axis=0).astype(BF))
        keys.append(jnp.concatenate([k, k], axis=0).T.astype(BF))
        values.append(jnp.concatenate([block[2 * HD :], ones], axis=0).astype(BF))
    k_all = jnp.concatenate(keys, axis=0)
    v_all = jnp.concatenate(values, axis=1)
    for b in range(4):
        for half in range(2):
            q = queries[b][:, half * TOK : (half + 1) * TOK]
            s = jnp.dot(k_all, q, preferred_element_type=F32)
            peak = jnp.max(s, axis=0, keepdims=True)
            p = jnp.exp2(s - peak).astype(BF)
            o = jnp.dot(v_all, p, preferred_element_type=F32)
            res = (o[:HD] / o[HD : HD + 1]).astype(BF)
            owner = yhi if half == 0 else 1 - yhi
            out_ref[owner * 4 + b] = res


def column(row):
    size = row.shape[1]
    eye = lax.broadcasted_iota(jnp.int32, (size, size), 0) == lax.broadcasted_iota(
        jnp.int32, (size, size), 1
    )
    return jnp.sum(jnp.where(eye, row.astype(F32), 0.0), axis=1, keepdims=True)


def select_rows(east_ref, west_ref):
    e = column(east_ref[...])
    w = column(west_ref[...])
    rows = jnp.concatenate([e, w], axis=0).astype(jnp.int32)
    return jnp.where(
        lax.broadcasted_iota(jnp.int32, (2 * OV, TOK), 1) == rows, 1.0, 0.0
    ).astype(BF)


def project(attn, wo):
    return lax.dot_general(attn, wo, (((0,), (0,)), ((), ())), preferred_element_type=F32)


def margin_kernel(attn_ref, wo_ref, wo2_ref, x_ref, gate_ref, east_ref, west_ref, e_ref, w_ref):
    yhi = lax.axis_index("yhi")
    pick = select_rows(east_ref, west_ref)
    nt = (((1,), (1,)), ((), ()))
    mine = lax.dot_general(pick, attn_ref[yhi], nt, preferred_element_type=F32).astype(BF)
    other = lax.dot_general(pick, attn_ref[1 - yhi], nt, preferred_element_type=F32).astype(BF)
    x = jnp.dot(pick, x_ref[...], preferred_element_type=F32)
    proj = jnp.dot(mine, wo_ref[...], preferred_element_type=F32) + jnp.dot(
        other, wo2_ref[...], preferred_element_type=F32
    )
    rows = (x + gate_ref[...] * proj).astype(BF)
    e_ref[...] = rows[:OV]
    w_ref[...] = rows[OV:]


def out_kernel(attn_ref, wo_ref, wo2_ref, x_ref, gate_ref, out_ref):
    yhi = lax.axis_index("yhi")
    proj = project(attn_ref[yhi], wo_ref[...]) + project(attn_ref[1 - yhi], wo2_ref[...])
    out_ref[...] = (x_ref[...].astype(F32) + gate_ref[...] * proj).astype(BF)


def blend_kernel(lay_ref, e_ref, w_ref, prev_ref, next_ref, east_ref, west_ref, bw_ref, out_ref):
    tile = lax.axis_index("z") * 4 + lax.axis_index("ylo") * 2 + lax.axis_index("core")
    prior = jnp.where(tile == 0, 63, tile - 1)
    a_e = column(bw_ref[pl.ds(tile, 1), :])
    a_w = column(bw_ref[pl.ds(prior, 1), :])
    new_e = (a_e * e_ref[...].astype(F32) + (8.0 - a_e) * next_ref[...].astype(F32)) / 8.0
    new_w = ((8.0 - a_w) * w_ref[...].astype(F32) + a_w * prev_ref[...].astype(F32)) / 8.0
    new = jnp.concatenate([new_e, new_w], axis=0).astype(BF)
    index = jnp.concatenate([east_ref[...], west_ref[...]], axis=1)
    hot = jnp.where(
        lax.broadcasted_iota(jnp.int32, (TOK, 2 * OV), 0) == index, 1.0, 0.0
    )
    mask = jnp.sum(hot, axis=1, keepdims=True)
    placed = jnp.dot(hot.astype(BF), new, preferred_element_type=F32)
    out_ref[...] = jnp.where(mask > 0.5, placed, lay_ref[...].astype(F32)).astype(BF)


def body(tokens, mod_shift, mod_scale, mod_gate, w_qkv, w_out, east_rows, west_rows, blend_weight):
    sds = jax.ShapeDtypeStruct
    x = tokens[0]
    swap = [(0, 1), (1, 0)]
    x_other = lax.ppermute(x, "yhi", swap)
    packed = call(
        pack_kernel,
        sds((4, 2 * HD, D), BF),
        (jnp.transpose(w_qkv, (0, 2, 1)), w_out),
        1000,
        2000000,
    )
    mine = lax.all_to_all(packed, "x", 0, 0, tiled=True)
    mine, x_other = lax.optimization_barrier((mine, x_other))
    other = lax.ppermute(mine, "core", swap)
    mod = call(
        norm_kernel,
        sds((2 * TOK, D), BF),
        (x, x_other, mod_shift, mod_scale),
        20 * 512 * D,
        3000000,
    )
    qkv, wo = call(
        qkv_kernel,
        (sds((4, 3 * HD, 2 * TOK), BF), sds((4, HD, D), BF)),
        (mod, mine, other),
        2 * 512 * 896 * D,
        6000000,
    )
    pairs = [(0, 3), (3, 0), (1, 2), (2, 1)]
    wo_other = lax.ppermute(wo, ("ylo", "yhi"), pairs)
    qkv = lax.all_to_all(qkv, "x", 0, 0, tiled=True)
    attn = call(
        attention_kernel,
        sds((8, HD, TOK), BF),
        (qkv,),
        4 * 2048 * 2048 * 128,
        1500000,
        2048 * 2048,
    )
    attn = lax.all_to_all(attn, ("yhi", "x"), 0, 0, tiled=True).reshape(2, 4 * HD, TOK)
    wo = wo.reshape(4 * HD, D)
    wo_other = wo_other.reshape(4 * HD, D)
    own_e, own_w = call(
        margin_kernel,
        (sds((OV, D), BF), sds((OV, D), BF)),
        (attn, wo, wo_other, x, mod_gate, east_rows, west_rows),
        2 * 64 * 576 * D,
        2000000,
    )
    count = 64
    prev_e = lax.ppermute(own_e, TILE, [(i, (i + 1) % count) for i in range(count)])
    next_w = lax.ppermute(own_w, TILE, [(i, (i - 1) % count) for i in range(count)])
    lay = call(
        out_kernel,
        sds((TOK, D), BF),
        (attn, wo, wo_other, x, mod_gate),
        2 * 256 * 576 * D,
        3000000,
    )
    out = call(
        blend_kernel,
        sds((TOK, D), BF),
        (lay, own_e, own_w, prev_e, next_w, east_rows, west_rows, blend_weight),
        2 * 256 * 64 * D,
        1500000,
    )
    return out[None]


def solution(mesh):
    fine = Mesh(mesh.devices.reshape(16, 2, 2, 4, 2), ("z", "ylo", "core", "x", "yhi"))
    in_specs = (
        P(TILE, SEQ, None),
        P(TILE, None),
        P(TILE, None),
        P(TILE, None),
        P(None, None, SEQ),
        P(SEQ, None),
        P(TILE, SEQ),
        P(TILE, SEQ),
        P(None, SEQ),
    )
    out_specs = P(TILE, SEQ, None)
    return jax.shard_map(body, mesh=fine, in_specs=in_specs, out_specs=out_specs, check_vma=False)
```

time: 348 us -> 93.2 us (0.27)
  the two profiles are of different devices: /device:TPU:2 before, /device:TPU:233 now
where the time goes in v1:
time: 93.2 us; the launch traced here: 92.6 us
  waiting for transfers between devices  37.3 us (40%)
  starting transfers between devices  33.7 us (36%)
  Pallas kernels  18.5 us (20%)
  local copies, waits for them, and re-layouts  2.97 us (3%)
    pallas_call x7, Pallas kernels, call(): pl.pallas_call(kernel, out_shape=outs, in_specs=[VMEM] * len(args), out_s...  18.5 us
    ppermute x1, waiting for transfers between devices, body(): x_other = lax.ppermute(x, 'yhi', swap)  13.3 us
    all_to_all x1, waiting for transfers between devices, body(): qkv = lax.all_to_all(qkv, 'x', 0, 0, tiled=True)  9.28 us
    ppermute x1, starting transfers between devices, body(): lax.ppermute(own_e, TILE, [(i, (i + 1) % count) for i in range(count)])  8.15 us
    all_to_all x1, waiting for transfers between devices, body(): lax.all_to_all(attn, ('yhi', 'x'), 0, 0, tiled=True).reshape(2, 4 * HD, TOK)  7.99 us
    ppermute x1, waiting for transfers between devices, body(): lax.ppermute(own_w, TILE, [(i, (i - 1) % count) for i in range(count)])  4.88 us
    all_to_all x1, starting transfers between devices, body(): qkv = lax.all_to_all(qkv, 'x', 0, 0, tiled=True)  4.24 us
    all_to_all x1, starting transfers between devices, body(): mine = lax.all_to_all(packed, 'x', 0, 0, tiled=True)  4.14 us
  transfers between devices with their start and end apart: 8, of which 5 were waited for; matrix products, arithmetic and copies ran while one was open for 0% of the time, Pallas kernels for 13%

profile of v1, /device:TPU:233, one launch (start us, length us, event | category | flops | bytes accessed | tf_op | source)
XLA Modules:
  0.0 92.6 jit_solution(7704631054597496952)
XLA Ops:
  0.0 1.0 %copy-done.2 = bf16[3,1152,72]{1,2,0:T(8,128)(2,1)S(1)} copy-done((bf16[3,1152,72]{1,2,0:T(8,128)(2,1)S(1)}, bf16[3,1152,72]{1,2,0:T(8,128)(2,1)}, u32[]{:S(2)}) %copy-start.2) | copy-done | bytes 497688
  1.0 0.9 copy-done.3
  1.9 1.2 %shard_map.91 = bf16[4,144,1152]{2,1,0:T(8,128)(2,1)} custom-call(bf16[3,72,1152]{2,1,0:T(8,128)(2,1)S(1)} %bitcast.16, bf16[72,1152]{1,0:T(8,128)(2,1)S(1)} %copy-done.3), custom_call_target="tpu_custom_call" | custom-call | flops 1000 | bytes 2000000 | tf_op jit(solution)/shard_map/pallas_call | solution.py:24
  3.1 4.1 %all-to-all-start = ((bf16[4,144,1152]{2,1,0:T(8,128)(2,1)}), bf16[4,144,1152]{2,1,0:T(8,128)(2,1)S(1)}, u32[]{:S(2)}, u32[]{:S(2)}) async-start(bf16[4,144,1152]{2,1,0:T(8,128)(2,1)} %shard_map.91), calls=%async_computation | async-start | bytes 2654208 | tf_op jit(solution)/shard_map/all_to_all | solution.py:195
  7.3 0.0 copy-done
  7.3 3.9 %collective-permute-start = (bf16[256,1152]{1,0:T(8,128)(2,1)S(1)}, bf16[256,1152]{1,0:T(8,128)(2,1)S(1)}, u32[]{:S(2)}, u32[]{:S(2)}) collective-permute-start(bf16[256,1152]{1,0:T(8,128)(2,1)S(1)} %bitcast.6), channel_id=1, source_target_pairs={{0,1},{1,0},{2,3},{3,2},{4,5},{5,4},{6,7},{7,6},{8,9},{9,8},{10,11... | collective-permute-start | bytes 1769480 | tf_op jit(solution)/shard_map/ppermute | solution.py:187
  11.2 13.3 %collective-permute-done.xo_ref = bf16[256,1152]{1,0:T(8,128)(2,1)S(1)} collective-permute-done((bf16[256,1152]{1,0:T(8,128)(2,1)S(1)}, bf16[256,1152]{1,0:T(8,128)(2,1)S(1)}, u32[]{:S(2)}, u32[]{:S(2)}) %collective-permute-start) | collective-permute-done | bytes 589856 | tf_op jit(solution)/shard_map/ppermute | solution.py:187
  24.5 0.0 all-to-all-done.mine_ref
  24.5 3.8 %collective-permute-start.1 = (bf16[4,144,1152]{2,1,0:T(8,128)(2,1)S(1)}, bf16[4,144,1152]{2,1,0:T(8,128)(2,1)S(1)}, u32[]{:S(2)}, u32[]{:S(2)}) collective-permute-start(bf16[4,144,1152]{2,1,0:T(8,128)(2,1)S(1)} %all-to-all-done.mine_ref), channel_id=1, source_target_pairs={{0,8},{8,0},{1,9},{9,1},{2,10},{10,2},{3,11},{11,3},{4,12},{12,4},... | collective-permute-start | bytes 3981320 | tf_op jit(solution)/shard_map/ppermute | solution.py:197
  28.3 0.0 copy-done.5
  28.3 0.0 copy-done.6
  28.3 0.9 shard_map.92.mod_ref
  29.2 1.8 %collective-permute-done.1.other_ref = bf16[4,144,1152]{2,1,0:T(8,128)(2,1)S(1)} collective-permute-done((bf16[4,144,1152]{2,1,0:T(8,128)(2,1)S(1)}, bf16[4,144,1152]{2,1,0:T(8,128)(2,1)S(1)}, u32[]{:S(2)}, u32[]{:S(2)}) %collective-permute-start.1) | collective-permute-done | bytes 1327136 | tf_op jit(solution)/shard_map/ppermute | solution.py:197
  31.0 3.2 %shard_map.93 = (bf16[4,216,512]{2,1,0:T(8,128)(2,1)S(1)}, bf16[4,72,1152]{2,1,0:T(8,128)(2,1)S(1)}) custom-call(bf16[512,1152]{1,0:T(8,128)(2,1)S(1)} %shard_map.92.mod_ref, bf16[4,144,1152]{2,1,0:T(8,128)(2,1)S(1)} %all-to-all-done.mine_ref, bf16[4,144,1152]{2,1,0:T(8,128)(2,1)S(1)} %collective-permute-done.1.other_ref), custom_call_target="tpu_custom_call" | custom-call | flops 1056964608 | bytes 6000000 | tf_op jit(solution)/shard_map/pallas_call | solution.py:24
  34.1 0.0 copy-start.1
  34.1 0.9 copy-done.1
  35.1 4.2 %all-to-all-start.1 = ((bf16[4,216,512]{2,1,0:T(8,128)(2,1)}), bf16[4,216,512]{2,1,0:T(8,128)(2,1)S(1)}, u32[]{:S(2)}, u32[]{:S(2)}) async-start(bf16[4,216,512]{2,1,0:T(8,128)(2,1)} %copy-done.1), calls=%async_computation.1 | async-start | bytes 1769472 | tf_op jit(solution)/shard_map/all_to_all | solution.py:214
  39.3 3.5 %collective-permute-start.2 = (bf16[4,72,1152]{2,1,0:T(8,128)(2,1)S(1)}, bf16[4,72,1152]{2,1,0:T(8,128)(2,1)S(1)}, u32[]{:S(2)}, u32[]{:S(2)}) collective-permute-start(bf16[4,72,1152]{2,1,0:T(8,128)(2,1)S(1)} %get-tuple-element.14), channel_id=1, source_target_pairs={{0,17},{17,0},{1,16},{16,1},{2,19},{19,2},{3,18},{18,3},{4,21},{21... | collective-permute-start | bytes 1990664 | tf_op jit(solution)/shard_map/ppermute | solution.py:213
  42.8 9.3 %all-to-all-done.1.qkv_ref = bf16[4,216,512]{2,1,0:T(8,128)(2,1)S(1)} async-done(((bf16[4,216,512]{2,1,0:T(8,128)(2,1)}), bf16[4,216,512]{2,1,0:T(8,128)(2,1)S(1)}, u32[]{:S(2)}, u32[]{:S(2)}) %all-to-all-start.1) | async-done | bytes 884768 | tf_op jit(solution)/shard_map/all_to_all | solution.py:214
  52.1 10.3 %shard_map.94 = bf16[8,72,256]{2,1,0:T(8,128)(2,1)} custom-call(bf16[4,216,512]{2,1,0:T(8,128)(2,1)S(1)} %all-to-all-done.1.qkv_ref), custom_call_target="tpu_custom_call" | custom-call | flops 2147483648 | bytes 1500000 | tf_op jit(solution)/shard_map/pallas_call | solution.py:24
  62.4 4.0 %all-to-all-start.2 = ((bf16[8,72,256]{2,1,0:T(8,128)(2,1)}), bf16[8,72,256]{2,1,0:T(8,128)(2,1)S(1)}, u32[]{:S(2)}, u32[]{:S(2)}) async-start(bf16[8,72,256]{2,1,0:T(8,128)(2,1)} %shard_map.94), calls=%async_computation.2 | async-start | bytes 589824 | tf_op jit(solution)/shard_map/all_to_all | solution.py:223
  66.5 0.0 collective-permute-done.2
  66.5 8.0 %all-to-all-done.2 = bf16[8,72,256]{2,1,0:T(8,128)(2,1)S(1)} async-done(((bf16[8,72,256]{2,1,0:T(8,128)(2,1)}), bf16[8,72,256]{2,1,0:T(8,128)(2,1)S(1)}, u32[]{:S(2)}, u32[]{:S(2)}) %all-to-all-start.2) | async-done | bytes 294944 | tf_op jit(solution)/shard_map/all_to_all | solution.py:223
  74.5 0.9 shard_map.96
  75.4 8.2 %collective-permute-start.3 = (bf16[32,1152]{1,0:T(8,128)(2,1)S(1)}, bf16[32,1152]{1,0:T(8,128)(2,1)S(1)}, u32[]{:S(2)}, u32[]{:S(2)}) collective-permute-start(bf16[32,1152]{1,0:T(8,128)(2,1)S(1)} %get-tuple-element.15.e_ref), channel_id=1, source_target_pairs={{0,8},{8,16},{16,24},{24,32},{32,40},{40,48},{48,56},{56,64},{64,7... | collective-permute-start | bytes 221192 | tf_op jit(solution)/shard_map/ppermute | solution.py:234
  83.5 1.9 %collective-permute-start.4 = (bf16[32,1152]{1,0:T(8,128)(2,1)S(1)}, bf16[32,1152]{1,0:T(8,128)(2,1)S(1)}, u32[]{:S(2)}, u32[]{:S(2)}) collective-permute-start(bf16[32,1152]{1,0:T(8,128)(2,1)S(1)} %get-tuple-element.16.w_ref), channel_id=1, source_target_pairs={{0,504},{8,0},{16,8},{24,16},{32,24},{40,32},{48,40},{56,48},{64,5... | collective-permute-start | bytes 221192 | tf_op jit(solution)/shard_map/ppermute | solution.py:235
  85.5 0.0 copy-done.9
  85.5 0.1 copy.10.bw_ref
  85.6 0.9 shard_map.95.lay_ref
  86.4 0.0 collective-permute-done.3.prev_ref
  86.4 4.9 %collective-permute-done.4.next_ref = bf16[32,1152]{1,0:T(8,128)(2,1)S(1)} collective-permute-done((bf16[32,1152]{1,0:T(8,128)(2,1)S(1)}, bf16[32,1152]{1,0:T(8,128)(2,1)S(1)}, u32[]{:S(2)}, u32[]{:S(2)}) %collective-permute-start.4) | collective-permute-done | bytes 73760 | tf_op jit(solution)/shard_map/ppermute | solution.py:235
  91.3 1.2 %shard_map.97 = bf16[256,1152]{1,0:T(8,128)(2,1)} custom-call(bf16[256,1152]{1,0:T(8,128)(2,1)S(1)} %shard_map.95.lay_ref, bf16[32,1152]{1,0:T(8,128)(2,1)S(1)} %get-tuple-element.15.e_ref, bf16[32,1152]{1,0:T(8,128)(2,1)S(1)} %get-tuple-element.16.w_ref, bf16[32,1152]{1,0:T(8,128)(2,1)S(1)} %collective-permute-done.3.prev_ref, ...), custom_call_target="tpu_custom_call" | custom-call | flops 37748736 | bytes 1500000 | tf_op jit(solution)/shard_map/pallas_call | solution.py:24
  (12 shorter events, 0.0 us)
Async XLA Ops:
  0.0 1.0 %copy-start.2 = (bf16[3,1152,72]{1,2,0:T(8,128)(2,1)S(1)}, bf16[3,1152,72]{1,2,0:T(8,128)(2,1)}, u32[]{:S(2)}) copy-start(bf16[3,1152,72]{1,2,0:T(8,128)(2,1)} %param.13) | copy-start | bytes 1492996
  1.0 0.9 copy-start.3
  3.1 4.2 %copy-start = (bf16[1,256,1152]{2,1,0:T(8,128)(2,1)S(1)}, bf16[1,256,1152]{2,1,0:T(8,128)(2,1)}, u32[]{:S(2)}) copy-start(bf16[1,256,1152]{2,1,0:T(8,128)(2,1)} %param.9) | copy-start | bytes 1769476
  3.1 25.2 %copy-start.5 = (f32[1,1152]{1,0:T(1,128)S(1)}, f32[1,1152]{1,0:T(1,128)}, u32[]{:S(2)}) copy-start(f32[1,1152]{1,0:T(1,128)} %shift_ref.1) | copy-start | bytes 13828
  3.1 25.2 %copy-start.6 = (f32[1,1152]{1,0:T(1,128)S(1)}, f32[1,1152]{1,0:T(1,128)}, u32[]{:S(2)}) copy-start(f32[1,1152]{1,0:T(1,128)} %scale_ref.1) | copy-start | bytes 13828
  3.1 21.4 %all-to-all-start = ((bf16[4,144,1152]{2,1,0:T(8,128)(2,1)}), bf16[4,144,1152]{2,1,0:T(8,128)(2,1)S(1)}, u32[]{:S(2)}, u32[]{:S(2)}) async-start(bf16[4,144,1152]{2,1,0:T(8,128)(2,1)} %shard_map.91), calls=%async_computation | async-start | bytes 2654208 | tf_op jit(solution)/shard_map/all_to_all | solution.py:195
  7.3 17.3 %collective-permute-start = (bf16[256,1152]{1,0:T(8,128)(2,1)S(1)}, bf16[256,1152]{1,0:T(8,128)(2,1)S(1)}, u32[]{:S(2)}, u32[]{:S(2)}) collective-permute-start(bf16[256,1152]{1,0:T(8,128)(2,1)S(1)} %bitcast.6), channel_id=1, source_target_pairs={{0,1},{1,0},{2,3},{3,2},{4,5},{5,4},{6,7},{7,6},{8,9},{9,8},{10,11... | collective-permute-start | bytes 1769480 | tf_op jit(solution)/shard_map/ppermute | solution.py:187
  24.5 6.4 %collective-permute-start.1 = (bf16[4,144,1152]{2,1,0:T(8,128)(2,1)S(1)}, bf16[4,144,1152]{2,1,0:T(8,128)(2,1)S(1)}, u32[]{:S(2)}, u32[]{:S(2)}) collective-permute-start(bf16[4,144,1152]{2,1,0:T(8,128)(2,1)S(1)} %all-to-all-done.mine_ref), channel_id=1, source_target_pairs={{0,8},{8,0},{1,9},{9,1},{2,10},{10,2},{3,11},{11,3},{4,12},{12,4},... | collective-permute-start | bytes 3981320 | tf_op jit(solution)/shard_map/ppermute | solution.py:197
  34.1 0.9 %copy-start.1 = (bf16[4,216,512]{2,1,0:T(8,128)(2,1)}, bf16[4,216,512]{2,1,0:T(8,128)(2,1)S(1)}, u32[]{:S(2)}) copy-start(bf16[4,216,512]{2,1,0:T(8,128)(2,1)S(1)} %get-tuple-element.13) | copy-start | bytes 2654212
  35.1 17.1 %all-to-all-start.1 = ((bf16[4,216,512]{2,1,0:T(8,128)(2,1)}), bf16[4,216,512]{2,1,0:T(8,128)(2,1)S(1)}, u32[]{:S(2)}, u32[]{:S(2)}) async-start(bf16[4,216,512]{2,1,0:T(8,128)(2,1)} %copy-done.1), calls=%async_computation.1 | async-start | bytes 1769472 | tf_op jit(solution)/shard_map/all_to_all | solution.py:214
  39.3 35.2 %copy-start.4 = (f32[1,1152]{1,0:T(1,128)S(1)}, f32[1,1152]{1,0:T(1,128)}, u32[]{:S(2)}) copy-start(f32[1,1152]{1,0:T(1,128)} %gate_ref.3) | copy-start | bytes 13828
  39.3 35.2 %copy-start.7 = (s32[1,32]{1,0:T(1,128)S(1)}, s32[1,32]{1,0:T(1,128)}, u32[]{:S(2)}) copy-start(s32[1,32]{1,0:T(1,128)} %east_ref.3) | copy-start | bytes 388
  39.3 35.2 %copy-start.8 = (s32[1,32]{1,0:T(1,128)S(1)}, s32[1,32]{1,0:T(1,128)}, u32[]{:S(2)}) copy-start(s32[1,32]{1,0:T(1,128)} %west_ref.3) | copy-start | bytes 388
  39.3 27.2 %collective-permute-start.2 = (bf16[4,72,1152]{2,1,0:T(8,128)(2,1)S(1)}, bf16[4,72,1152]{2,1,0:T(8,128)(2,1)S(1)}, u32[]{:S(2)}, u32[]{:S(2)}) collective-permute-start(bf16[4,72,1152]{2,1,0:T(8,128)(2,1)S(1)} %get-tuple-element.14), channel_id=1, source_target_pairs={{0,17},{17,0},{1,16},{16,1},{2,19},{19,2},{3,18},{18,3},{4,21},{21... | collective-permute-start | bytes 1990664 | tf_op jit(solution)/shard_map/ppermute | solution.py:213
  62.4 23.0 %copy-start.9 = (s32[64,32]{0,1:T(8,128)S(1)}, s32[64,32]{0,1:T(8,128)}, u32[]{:S(2)}) copy-start(s32[64,32]{0,1:T(8,128)} %param.17) | copy-start | bytes 24580
  62.4 12.0 %all-to-all-start.2 = ((bf16[8,72,256]{2,1,0:T(8,128)(2,1)}), bf16[8,72,256]{2,1,0:T(8,128)(2,1)S(1)}, u32[]{:S(2)}, u32[]{:S(2)}) async-start(bf16[8,72,256]{2,1,0:T(8,128)(2,1)} %shard_map.94), calls=%async_computation.2 | async-start | bytes 589824 | tf_op jit(solution)/shard_map/all_to_all | solution.py:223
  75.4 11.1 %collective-permute-start.3 = (bf16[32,1152]{1,0:T(8,128)(2,1)S(1)}, bf16[32,1152]{1,0:T(8,128)(2,1)S(1)}, u32[]{:S(2)}, u32[]{:S(2)}) collective-permute-start(bf16[32,1152]{1,0:T(8,128)(2,1)S(1)} %get-tuple-element.15.e_ref), channel_id=1, source_target_pairs={{0,8},{8,16},{16,24},{24,32},{32,40},{40,48},{48,56},{56,64},{64,7... | collective-permute-start | bytes 221192 | tf_op jit(solution)/shard_map/ppermute | solution.py:234
  83.5 7.8 %collective-permute-start.4 = (bf16[32,1152]{1,0:T(8,128)(2,1)S(1)}, bf16[32,1152]{1,0:T(8,128)(2,1)S(1)}, u32[]{:S(2)}, u32[]{:S(2)}) collective-permute-start(bf16[32,1152]{1,0:T(8,128)(2,1)S(1)} %get-tuple-element.16.w_ref), channel_id=1, source_target_pairs={{0,504},{8,0},{16,8},{24,16},{32,24},{40,32},{48,40},{56,48},{64,5... | collective-permute-start | bytes 221192 | tf_op jit(solution)/shard_map/ppermute | solution.py:235

commit v2 on v1

v2 whole, which is shorter than its diff:
```python
import functools
import math

import jax
import jax.numpy as jnp
from jax import lax
from jax.experimental import pallas as pl
from jax.experimental.pallas import tpu as pltpu
from jax.sharding import Mesh
from jax.sharding import PartitionSpec as P

D = 1152
HD = 72
TOK = 256
OV = 32
TILE = ("z", "ylo", "core")
SEQ = ("x", "yhi")
VMEM = pl.BlockSpec(memory_space=pltpu.VMEM)
HBM = pl.BlockSpec(memory_space=pltpu.HBM)
BF = jnp.bfloat16
F32 = jnp.float32


def call(kernel, outs, args, flops, nbytes, trans=0, ins=None, out_specs=None, scratch=()):
    return pl.pallas_call(
        kernel,
        out_shape=outs,
        in_specs=ins or [VMEM] * len(args),
        out_specs=out_specs or jax.tree.map(lambda _: VMEM, outs),
        scratch_shapes=scratch,
        compiler_params=pltpu.CompilerParams(vmem_limit_bytes=48 * 1024 * 1024),
        cost_estimate=pl.CostEstimate(
            flops=flops, bytes_accessed=nbytes, transcendentals=trans
        ),
    )(*args)


def pack_kernel(w_ref, wo_ref, out_ref, buf, sems):
    core = lax.axis_index("core")

    def put(first, second):
        loads = [
            pltpu.make_async_copy(first, buf.at[0], sems.at[4, 0]),
            pltpu.make_async_copy(second, buf.at[1], sems.at[4, 1]),
        ]
        for copy in loads:
            copy.start()
        copies = []
        for j in range(2):
            loads[j].wait()
            for i in range(4):
                copies.append(pltpu.make_async_copy(buf.at[j], out_ref.at[i, j], sems.at[i, j]))
                copies[-1].start()
        for copy in copies:
            copy.wait()

    @pl.when(core == 0)
    def _():
        put(w_ref.at[0], w_ref.at[1])

    @pl.when(core == 1)
    def _():
        put(w_ref.at[2], wo_ref)


def modulate(x_ref, shift, scale):
    x = x_ref[...].astype(F32)
    mean = jnp.sum(x, axis=-1, keepdims=True) * (1.0 / D)
    centered = x - mean
    var = jnp.sum(centered * centered, axis=-1, keepdims=True) * (1.0 / D)
    normed = centered * lax.rsqrt(var + 1e-06)
    return normed * (1.0 + scale) + shift


def norm_kernel(x_ref, xo_ref, shift_ref, scale_ref, out_ref):
    shift = shift_ref[...]
    scale = scale_ref[...]
    out_ref[:, :TOK] = modulate(x_ref, shift, scale).T.astype(BF)
    out_ref[:, TOK:] = modulate(xo_ref, shift, scale).T.astype(BF)


def qkv_kernel(mod_ref, mine_ref, other_ref, mine4_ref, other4_ref, out_ref, wo_ref, buf, sems, wsems):
    core = lax.axis_index("core")

    def go(qk_ref, vo_ref, vo4_ref):
        moves = [
            pltpu.make_async_copy(vo4_ref.at[h, 1], wo_ref.at[h], wsems.at[h]) for h in range(4)
        ]
        for move in moves:
            move.start()
        mod = mod_ref[...]
        qk = jnp.dot(qk_ref[...], mod, preferred_element_type=F32)
        vo = jnp.dot(vo_ref[...], mod, preferred_element_type=F32)
        for h in range(4):
            rows = jnp.concatenate(
                [qk[2 * HD * h : 2 * HD * (h + 1)], vo[2 * HD * h : 2 * HD * h + HD]], axis=0
            )
            buf[h] = rows.astype(BF)
            copy = pltpu.make_async_copy(buf.at[h], out_ref.at[h], sems.at[h])
            copy.start()
            moves.append(copy)
        for move in moves:
            move.wait()

    @pl.when(core == 0)
    def _():
        go(mine_ref, other_ref, other4_ref)

    @pl.when(core == 1)
    def _():
        go(other_ref, mine_ref, mine4_ref)


def attention_kernel(qkv_ref, out_ref, buf, sems):
    yhi = lax.axis_index("yhi")
    factor = math.log2(math.e) * HD**-0.5
    keys = []
    values = []
    queries = []
    ones = jnp.ones((8, 2 * TOK), F32)
    for b in range(4):
        block = qkv_ref[b].astype(F32)
        q = block[:HD] * factor
        hi = q.astype(BF).astype(F32)
        lo = q - hi
        k = block[HD : 2 * HD]
        both = jnp.concatenate([hi, lo], axis=0).astype(BF)
        queries.append((both[:, :TOK], b, 0))
        queries.append((both[:, TOK:], b, 1))
        kt = k.T.astype(BF)
        keys.append(jnp.concatenate([kt, kt], axis=1))
        values.append(jnp.concatenate([block[2 * HD :], ones], axis=0).astype(BF))

    def score(i):
        return [jnp.dot(k, queries[i][0], preferred_element_type=F32) for k in keys]

    copies = []
    ahead = score(0)
    for i in range(8):
        s = ahead
        if i < 7:
            ahead = score(i + 1)
        peak = functools.reduce(jnp.maximum, [jnp.max(c, axis=0, keepdims=True) for c in s])
        o = sum(
            jnp.dot(v, jnp.exp2(c - peak).astype(BF), preferred_element_type=F32)
            for c, v in zip(s, values)
        )
        _, b, half = queries[i]
        slot = (yhi if half == 0 else 1 - yhi) * 4 + b
        buf[i] = (o[:HD] / o[HD : HD + 1]).astype(BF)
        copies.append(pltpu.make_async_copy(buf.at[i], out_ref.at[slot], sems.at[i]))
        copies[-1].start()
    for copy in copies:
        copy.wait()


def column(row):
    size = row.shape[1]
    eye = lax.broadcasted_iota(jnp.int32, (size, size), 0) == lax.broadcasted_iota(
        jnp.int32, (size, size), 1
    )
    return jnp.sum(jnp.where(eye, row.astype(F32), 0.0), axis=1, keepdims=True)


def ordered(east_ref, west_ref):
    first = lax.axis_index("core") == 0
    east = east_ref[...]
    west = west_ref[...]
    return jnp.where(first, east, west), jnp.where(first, west, east)


def select_rows(east_ref, west_ref):
    a, b = ordered(east_ref, west_ref)
    rows = jnp.concatenate([column(a), column(b)], axis=0).astype(jnp.int32)
    return jnp.where(
        lax.broadcasted_iota(jnp.int32, (2 * OV, TOK), 1) == rows, 1.0, 0.0
    ).astype(BF)


def project(attn, wo):
    return lax.dot_general(attn, wo, (((0,), (0,)), ((), ())), preferred_element_type=F32)


def margin_kernel(attn_ref, wo_ref, wo2_ref, x_ref, gate_ref, east_ref, west_ref, a_ref, b_ref):
    yhi = lax.axis_index("yhi")
    pick = select_rows(east_ref, west_ref)
    nt = (((1,), (1,)), ((), ()))
    mine = lax.dot_general(pick, attn_ref[yhi], nt, preferred_element_type=F32).astype(BF)
    other = lax.dot_general(pick, attn_ref[1 - yhi], nt, preferred_element_type=F32).astype(BF)
    x = jnp.dot(pick, x_ref[...], preferred_element_type=F32)
    proj = jnp.dot(mine, wo_ref[...], preferred_element_type=F32) + jnp.dot(
        other, wo2_ref[...], preferred_element_type=F32
    )
    rows = (x + gate_ref[...] * proj).astype(BF)
    a_ref[...] = rows[:OV]
    b_ref[...] = rows[OV:]


def out_kernel(attn_ref, wo_ref, wo2_ref, x_ref, gate_ref, out_ref):
    yhi = lax.axis_index("yhi")
    proj = project(attn_ref[yhi], wo_ref[...]) + project(attn_ref[1 - yhi], wo2_ref[...])
    out_ref[...] = (x_ref[...].astype(F32) + gate_ref[...] * proj).astype(BF)


def blend_kernel(lay_ref, a_ref, b_ref, ra_ref, rb_ref, east_ref, west_ref, bw_ref, out_ref):
    core = lax.axis_index("core")
    tile = lax.axis_index("z") * 4 + lax.axis_index("ylo") * 2 + core
    prior = jnp.where(tile == 0, 63, tile - 1)
    east = column(bw_ref[pl.ds(tile, 1), :])
    west = 8.0 - column(bw_ref[pl.ds(prior, 1), :])
    own_a = jnp.where(core == 0, east, west)
    own_b = jnp.where(core == 0, west, east)
    new_a = (own_a * a_ref[...].astype(F32) + (8.0 - own_a) * ra_ref[...].astype(F32)) / 8.0
    new_b = (own_b * b_ref[...].astype(F32) + (8.0 - own_b) * rb_ref[...].astype(F32)) / 8.0
    new = jnp.concatenate([new_a, new_b], axis=0).astype(BF)
    index = jnp.concatenate(ordered(east_ref, west_ref), axis=1)
    hot = jnp.where(
        lax.broadcasted_iota(jnp.int32, (TOK, 2 * OV), 0) == index, 1.0, 0.0
    )
    mask = jnp.sum(hot, axis=1, keepdims=True)
    placed = jnp.dot(hot.astype(BF), new, preferred_element_type=F32)
    out_ref[...] = jnp.where(mask > 0.5, placed, lay_ref[...].astype(F32)).astype(BF)


def body(tokens, mod_shift, mod_scale, mod_gate, w_qkv, w_out, east_rows, west_rows, blend_weight):
    sds = jax.ShapeDtypeStruct
    dma = pltpu.SemaphoreType.DMA
    x = tokens[0]
    swap = [(0, 1), (1, 0)]
    x_other = lax.ppermute(x, "yhi", swap)
    packed = call(
        pack_kernel,
        pltpu.HBM((4, 2, HD, D), BF),
        tuple(
            pltpu.with_memory_space_constraint(w, pltpu.HBM)
            for w in (jnp.transpose(w_qkv, (0, 2, 1)), w_out)
        ),
        1000,
        2000000,
        ins=[HBM, HBM],
        out_specs=HBM,
        scratch=[pltpu.VMEM((2, HD, D), BF), dma((5, 2))],
    )
    mine = lax.all_to_all(packed, "x", 0, 0, tiled=True)
    mine, x_other = lax.optimization_barrier((mine, x_other))
    other = lax.ppermute(mine, "core", swap)
    mod = call(
        norm_kernel,
        sds((D, 2 * TOK), BF),
        (x, x_other, mod_shift, mod_scale),
        20 * 512 * D,
        3000000,
    )
    qkv, wo = call(
        qkv_kernel,
        (pltpu.HBM((4, 3 * HD, 2 * TOK), BF), sds((4, HD, D), BF)),
        (mod, mine.reshape(8 * HD, D), other.reshape(8 * HD, D), mine, other),
        2 * 512 * 1152 * D,
        6000000,
        out_specs=(HBM, VMEM),
        scratch=[pltpu.VMEM((4, 3 * HD, 2 * TOK), BF), dma((4,)), dma((4,))],
    )
    pairs = [(0, 3), (3, 0), (1, 2), (2, 1)]
    wo_other = lax.ppermute(wo, ("ylo", "yhi"), pairs)
    qkv = lax.all_to_all(qkv, "x", 0, 0, tiled=True)
    attn = call(
        attention_kernel,
        pltpu.HBM((8, HD, TOK), BF),
        (qkv,),
        4 * 2048 * 2048 * 128,
        1500000,
        2048 * 2048,
        out_specs=HBM,
        scratch=[pltpu.VMEM((8, HD, TOK), BF), dma((8,))],
    )
    attn = lax.all_to_all(attn, ("yhi", "x"), 0, 0, tiled=True).reshape(2, 4 * HD, TOK)
    wo = wo.reshape(4 * HD, D)
    wo_other = wo_other.reshape(4 * HD, D)
    a, b = call(
        margin_kernel,
        (sds((OV, D), BF), sds((OV, D), BF)),
        (attn, wo, wo_other, x, mod_gate, east_rows, west_rows),
        2 * 64 * 576 * D,
        2000000,
    )
    other_b = lax.ppermute(b, TILE, [(i, (i + 2 * (i % 2) - 1) % 64) for i in range(64)])
    other_a = lax.ppermute(a, TILE, [(i, i + 1 - 2 * (i % 2)) for i in range(64)])
    lay = call(
        out_kernel,
        sds((TOK, D), BF),
        (attn, wo, wo_other, x, mod_gate),
        2 * 256 * 576 * D,
        3000000,
    )
    out = call(
        blend_kernel,
        sds((TOK, D), BF),
        (lay, a, b, other_a, other_b, east_rows, west_rows, blend_weight),
        2 * 256 * 64 * D,
        1500000,
    )
    return out[None]


def solution(mesh):
    fine = Mesh(mesh.devices.reshape(16, 2, 2, 4, 2), ("z", "ylo", "core", "x", "yhi"))
    in_specs = (
        P(TILE, SEQ, None),
        P(TILE, None),
        P(TILE, None),
        P(TILE, None),
        P(None, None, SEQ),
        P(SEQ, None),
        P(TILE, SEQ),
        P(TILE, SEQ),
        P(None, SEQ),
    )
    out_specs = P(TILE, SEQ, None)
    return jax.shard_map(body, mesh=fine, in_specs=in_specs, out_specs=out_specs, check_vma=False)
```

time: 93.2 us -> 89 us (0.955)
  the two profiles are of different devices: /device:TPU:233 before, /device:TPU:2 now
where the time goes in v2:
time: 89 us; the launch traced here: 88.4 us
  starting transfers between devices  43.3 us (49%)
  waiting for transfers between devices  29.3 us (33%)
  Pallas kernels  15.5 us (17%)
    pallas_call x7, Pallas kernels, call(): pl.pallas_call(kernel, out_shape=outs, in_specs=ins or [VMEM] * len(args)...  15.5 us
    ppermute x1, starting transfers between devices, body(): lax.ppermute(b, TILE, [(i, (i + 2 * (i % 2) - 1) % 64) for i in range(64)])  11.6 us
    ppermute x1, waiting for transfers between devices, body(): x_other = lax.ppermute(x, 'yhi', swap)  11.4 us
    all_to_all x1, starting transfers between devices, body(): mine = lax.all_to_all(packed, 'x', 0, 0, tiled=True)  9.56 us
    all_to_all x1, waiting for transfers between devices, body(): lax.all_to_all(attn, ('yhi', 'x'), 0, 0, tiled=True).reshape(2, 4 * HD, TOK)  7.8 us
    all_to_all x1, waiting for transfers between devices, body(): qkv = lax.all_to_all(qkv, 'x', 0, 0, tiled=True)  7.12 us
    all_to_all x1, starting transfers between devices, body(): lax.all_to_all(attn, ('yhi', 'x'), 0, 0, tiled=True).reshape(2, 4 * HD, TOK)  6.54 us
    ppermute x1, starting transfers between devices, body(): wo_other = lax.ppermute(wo, ('ylo', 'yhi'), pairs)  5.04 us
  transfers between devices with their start and end apart: 8, of which 5 were waited for; matrix products, arithmetic and copies ran while one was open for 0% of the time, Pallas kernels for 9%

profile of v2, /device:TPU:2, one launch (start us, length us, event | category | flops | bytes accessed | tf_op | source)
XLA Modules:
  0.0 88.4 jit_solution(9739108688615046875)
XLA Ops:
  0.0 2.1 %shard_map.91 = bf16[4,2,72,1152]{3,2,1,0:T(8,128)(2,1)} custom-call(bf16[3,72,1152]{2,1,0:T(8,128)(2,1)} %bitcast.20, bf16[72,1152]{1,0:T(8,128)(2,1)} %wo_ref.1), custom_call_target="tpu_custom_call" | custom-call | flops 1000 | bytes 2000000 | tf_op jit(solution)/shard_map/pallas_call | solution.py:25
  2.1 0.0 copy-start
  2.1 0.0 copy-start.2
  2.1 0.0 copy-start.3
  2.1 9.6 %all-to-all-start = ((bf16[4,2,72,1152]{3,2,1,0:T(8,128)(2,1)}), bf16[4,2,72,1152]{3,2,1,0:T(8,128)(2,1)S(1)}, u32[]{:S(2)}, u32[]{:S(2)}) async-start(bf16[4,2,72,1152]{3,2,1,0:T(8,128)(2,1)} %shard_map.91), calls=%async_computation | async-start | bytes 2654208 | tf_op jit(solution)/shard_map/all_to_all | solution.py:244
  11.7 0.0 copy-done
  11.7 1.9 %collective-permute-start = (bf16[256,1152]{1,0:T(8,128)(2,1)S(1)}, bf16[256,1152]{1,0:T(8,128)(2,1)S(1)}, u32[]{:S(2)}, u32[]{:S(2)}) collective-permute-start(bf16[256,1152]{1,0:T(8,128)(2,1)S(1)} %bitcast.9), channel_id=1, source_target_pairs={{0,1},{1,0},{2,3},{3,2},{4,5},{5,4},{6,7},{7,6},{8,9},{9,8},{10,11... | collective-permute-start | bytes 1769480 | tf_op jit(solution)/shard_map/ppermute | solution.py:230
  13.6 11.4 %collective-permute-done.xo_ref = bf16[256,1152]{1,0:T(8,128)(2,1)S(1)} collective-permute-done((bf16[256,1152]{1,0:T(8,128)(2,1)S(1)}, bf16[256,1152]{1,0:T(8,128)(2,1)S(1)}, u32[]{:S(2)}, u32[]{:S(2)}) %collective-permute-start) | collective-permute-done | bytes 589856 | tf_op jit(solution)/shard_map/ppermute | solution.py:230
  25.0 0.0 all-to-all-done.mine4_ref
  25.0 1.9 %collective-permute-start.1 = (bf16[4,2,72,1152]{3,2,1,0:T(8,128)(2,1)S(1)}, bf16[4,2,72,1152]{3,2,1,0:T(8,128)(2,1)S(1)}, u32[]{:S(2)}, u32[]{:S(2)}) collective-permute-start(bf16[4,2,72,1152]{3,2,1,0:T(8,128)(2,1)S(1)} %all-to-all-done.mine4_ref), channel_id=1, source_target_pairs={{0,8},{8,0},{1,9},{9,1},{2,10},{10,2},{3,11},{11,3},{4,12},{12,4},... | collective-permute-start | bytes 3981320 | tf_op jit(solution)/shard_map/ppermute | solution.py:246
  26.9 0.0 copy-done.2
  26.9 0.0 copy-done.3
  26.9 1.0 %shard_map.92.mod_ref = bf16[1152,512]{1,0:T(8,128)(2,1)S(1)} custom-call(bf16[256,1152]{1,0:T(8,128)(2,1)S(1)} %bitcast.10, bf16[256,1152]{1,0:T(8,128)(2,1)S(1)} %collective-permute-done.xo_ref, f32[1,1152]{1,0:T(1,128)S(1)} %copy-done.2, f32[1,1152]{1,0:T(1,128)S(1)} %copy-done.3), custom_call_target="tpu_custom_call" | custom-call | flops 11796480 | bytes 3000000 | tf_op jit(solution)/shard_map/pallas_call | solution.py:25
  28.0 2.0 %collective-permute-done.1.other4_ref = bf16[4,2,72,1152]{3,2,1,0:T(8,128)(2,1)S(1)} collective-permute-done((bf16[4,2,72,1152]{3,2,1,0:T(8,128)(2,1)S(1)}, bf16[4,2,72,1152]{3,2,1,0:T(8,128)(2,1)S(1)}, u32[]{:S(2)}, u32[]{:S(2)}) %collective-permute-start.1) | collective-permute-done | bytes 1327136 | tf_op jit(solution)/shard_map/ppermute | solution.py:246
  29.9 3.4 %shard_map.93 = (bf16[4,216,512]{2,1,0:T(8,128)(2,1)}, bf16[4,72,1152]{2,1,0:T(8,128)(2,1)S(1)}) custom-call(bf16[1152,512]{1,0:T(8,128)(2,1)S(1)} %shard_map.92.mod_ref, bf16[576,1152]{1,0:T(8,128)(2,1)S(1)} %bitcast.8, bf16[576,1152]{1,0:T(8,128)(2,1)S(1)} %bitcast.13, bf16[4,2,72,1152]{3,2,1,0:T(8,128)(2,1)S(1)} %all-to-all-done.mine4_ref, ...), custom_call_target="tpu_custom_call" | custom-call | flops 1358954496 | bytes 6000000 | tf_op jit(solution)/shard_map/pallas_call | solution.py:25
  33.3 4.8 %all-to-all-start.1 = ((bf16[4,216,512]{2,1,0:T(8,128)(2,1)}), bf16[4,216,512]{2,1,0:T(8,128)(2,1)S(1)}, u32[]{:S(2)}, u32[]{:S(2)}) async-start(bf16[4,216,512]{2,1,0:T(8,128)(2,1)} %get-tuple-element.13), calls=%async_computation.1 | async-start | bytes 1769472 | tf_op jit(solution)/shard_map/all_to_all | solution.py:265
  38.1 5.0 %collective-permute-start.2 = (bf16[4,72,1152]{2,1,0:T(8,128)(2,1)S(1)}, bf16[4,72,1152]{2,1,0:T(8,128)(2,1)S(1)}, u32[]{:S(2)}, u32[]{:S(2)}) collective-permute-start(bf16[4,72,1152]{2,1,0:T(8,128)(2,1)S(1)} %get-tuple-element.14), channel_id=1, source_target_pairs={{0,17},{17,0},{1,16},{16,1},{2,19},{19,2},{3,18},{18,3},{4,21},{21... | collective-permute-start | bytes 1990664 | tf_op jit(solution)/shard_map/ppermute | solution.py:264
  43.2 7.1 %all-to-all-done.1.qkv_ref = bf16[4,216,512]{2,1,0:T(8,128)(2,1)S(1)} async-done(((bf16[4,216,512]{2,1,0:T(8,128)(2,1)}), bf16[4,216,512]{2,1,0:T(8,128)(2,1)S(1)}, u32[]{:S(2)}, u32[]{:S(2)}) %all-to-all-start.1) | async-done | bytes 884768 | tf_op jit(solution)/shard_map/all_to_all | solution.py:265
  50.3 6.0 %shard_map.94 = bf16[8,72,256]{2,1,0:T(8,128)(2,1)} custom-call(bf16[4,216,512]{2,1,0:T(8,128)(2,1)S(1)} %all-to-all-done.1.qkv_ref), custom_call_target="tpu_custom_call" | custom-call | flops 2147483648 | bytes 1500000 | tf_op jit(solution)/shard_map/pallas_call | solution.py:25
  56.3 0.0 copy-start.6
  56.3 6.5 %all-to-all-start.2 = ((bf16[8,72,256]{2,1,0:T(8,128)(2,1)}), bf16[8,72,256]{2,1,0:T(8,128)(2,1)S(1)}, u32[]{:S(2)}, u32[]{:S(2)}) async-start(bf16[8,72,256]{2,1,0:T(8,128)(2,1)} %shard_map.94), calls=%async_computation.2 | async-start | bytes 589824 | tf_op jit(solution)/shard_map/all_to_all | solution.py:276
  62.9 0.0 collective-permute-done.2
  62.9 7.8 %all-to-all-done.2 = bf16[8,72,256]{2,1,0:T(8,128)(2,1)S(1)} async-done(((bf16[8,72,256]{2,1,0:T(8,128)(2,1)}), bf16[8,72,256]{2,1,0:T(8,128)(2,1)S(1)}, u32[]{:S(2)}, u32[]{:S(2)}) %all-to-all-start.2) | async-done | bytes 294944 | tf_op jit(solution)/shard_map/all_to_all | solution.py:276
  70.7 0.9 %shard_map.96 = (bf16[32,1152]{1,0:T(8,128)(2,1)S(1)}, bf16[32,1152]{1,0:T(8,128)(2,1)S(1)}) custom-call(bf16[2,288,256]{2,1,0:T(8,128)(2,1)S(1)} %bitcast.14, bf16[288,1152]{1,0:T(8,128)(2,1)S(1)} %bitcast.16, bf16[288,1152]{1,0:T(8,128)(2,1)S(1)} %bitcast.18, bf16[256,1152]{1,0:T(8,128)(2,1)S(1)} %bitcast.11, f32[1,1152]{1,0:T(1,128)S(1)} %copy-done.1, ...), custom_call_target="tpu_custom_call" | custom-call | flops 84934656 | bytes 2000000 | tf_op jit(solution)/shard_map/pallas_call | solution.py:25
  71.6 1.9 %collective-permute-start.3 = (bf16[32,1152]{1,0:T(8,128)(2,1)S(1)}, bf16[32,1152]{1,0:T(8,128)(2,1)S(1)}, u32[]{:S(2)}, u32[]{:S(2)}) collective-permute-start(bf16[32,1152]{1,0:T(8,128)(2,1)S(1)} %get-tuple-element.15.a_ref), channel_id=1, source_target_pairs={{0,8},{8,0},{16,24},{24,16},{32,40},{40,32},{48,56},{56,48},{64,72... | collective-permute-start | bytes 221192 | tf_op jit(solution)/shard_map/ppermute | solution.py:287
  73.5 11.6 %collective-permute-start.4 = (bf16[32,1152]{1,0:T(8,128)(2,1)S(1)}, bf16[32,1152]{1,0:T(8,128)(2,1)S(1)}, u32[]{:S(2)}, u32[]{:S(2)}) collective-permute-start(bf16[32,1152]{1,0:T(8,128)(2,1)S(1)} %get-tuple-element.16.b_ref), channel_id=1, source_target_pairs={{0,504},{8,16},{16,8},{24,32},{32,24},{40,48},{48,40},{56,64},{64,... | collective-permute-start | bytes 221192 | tf_op jit(solution)/shard_map/ppermute | solution.py:286
  85.1 0.0 copy-done.6
  85.2 0.1 copy.10.bw_ref
  85.2 0.9 shard_map.95.lay_ref
  86.1 0.0 collective-permute-done.3.ra_ref
  86.1 1.1 %collective-permute-done.4.rb_ref = bf16[32,1152]{1,0:T(8,128)(2,1)S(1)} collective-permute-done((bf16[32,1152]{1,0:T(8,128)(2,1)S(1)}, bf16[32,1152]{1,0:T(8,128)(2,1)S(1)}, u32[]{:S(2)}, u32[]{:S(2)}) %collective-permute-start.4) | collective-permute-done | bytes 73760 | tf_op jit(solution)/shard_map/ppermute | solution.py:286
  87.2 1.2 %shard_map.97 = bf16[256,1152]{1,0:T(8,128)(2,1)} custom-call(bf16[256,1152]{1,0:T(8,128)(2,1)S(1)} %shard_map.95.lay_ref, bf16[32,1152]{1,0:T(8,128)(2,1)S(1)} %get-tuple-element.15.a_ref, bf16[32,1152]{1,0:T(8,128)(2,1)S(1)} %get-tuple-element.16.b_ref, bf16[32,1152]{1,0:T(8,128)(2,1)S(1)} %collective-permute-done.3.ra_ref, ...), custom_call_target="tpu_custom_call" | custom-call | flops 37748736 | bytes 1500000 | tf_op jit(solution)/shard_map/pallas_call | solution.py:25
  (6 shorter events, 0.0 us)
Async XLA Ops:
  2.1 9.6 %copy-start = (bf16[1,256,1152]{2,1,0:T(8,128)(2,1)S(1)}, bf16[1,256,1152]{2,1,0:T(8,128)(2,1)}, u32[]{:S(2)}) copy-start(bf16[1,256,1152]{2,1,0:T(8,128)(2,1)} %param.9) | copy-start | bytes 1769476
  2.1 24.8 %copy-start.2 = (f32[1,1152]{1,0:T(1,128)S(1)}, f32[1,1152]{1,0:T(1,128)}, u32[]{:S(2)}) copy-start(f32[1,1152]{1,0:T(1,128)} %shift_ref.1) | copy-start | bytes 13828
  2.1 24.8 %copy-start.3 = (f32[1,1152]{1,0:T(1,128)S(1)}, f32[1,1152]{1,0:T(1,128)}, u32[]{:S(2)}) copy-start(f32[1,1152]{1,0:T(1,128)} %scale_ref.1) | copy-start | bytes 13828
  2.1 22.9 %all-to-all-start = ((bf16[4,2,72,1152]{3,2,1,0:T(8,128)(2,1)}), bf16[4,2,72,1152]{3,2,1,0:T(8,128)(2,1)S(1)}, u32[]{:S(2)}, u32[]{:S(2)}) async-start(bf16[4,2,72,1152]{3,2,1,0:T(8,128)(2,1)} %shard_map.91), calls=%async_computation | async-start | bytes 2654208 | tf_op jit(solution)/shard_map/all_to_all | solution.py:244
  11.7 13.3 %collective-permute-start = (bf16[256,1152]{1,0:T(8,128)(2,1)S(1)}, bf16[256,1152]{1,0:T(8,128)(2,1)S(1)}, u32[]{:S(2)}, u32[]{:S(2)}) collective-permute-start(bf16[256,1152]{1,0:T(8,128)(2,1)S(1)} %bitcast.9), channel_id=1, source_target_pairs={{0,1},{1,0},{2,3},{3,2},{4,5},{5,4},{6,7},{7,6},{8,9},{9,8},{10,11... | collective-permute-start | bytes 1769480 | tf_op jit(solution)/shard_map/ppermute | solution.py:230
  25.0 4.9 %collective-permute-start.1 = (bf16[4,2,72,1152]{3,2,1,0:T(8,128)(2,1)S(1)}, bf16[4,2,72,1152]{3,2,1,0:T(8,128)(2,1)S(1)}, u32[]{:S(2)}, u32[]{:S(2)}) collective-permute-start(bf16[4,2,72,1152]{3,2,1,0:T(8,128)(2,1)S(1)} %all-to-all-done.mine4_ref), channel_id=1, source_target_pairs={{0,8},{8,0},{1,9},{9,1},{2,10},{10,2},{3,11},{11,3},{4,12},{12,4},... | collective-permute-start | bytes 3981320 | tf_op jit(solution)/shard_map/ppermute | solution.py:246
  33.3 17.0 %all-to-all-start.1 = ((bf16[4,216,512]{2,1,0:T(8,128)(2,1)}), bf16[4,216,512]{2,1,0:T(8,128)(2,1)S(1)}, u32[]{:S(2)}, u32[]{:S(2)}) async-start(bf16[4,216,512]{2,1,0:T(8,128)(2,1)} %get-tuple-element.13), calls=%async_computation.1 | async-start | bytes 1769472 | tf_op jit(solution)/shard_map/all_to_all | solution.py:265
  38.1 32.6 %copy-start.1 = (f32[1,1152]{1,0:T(1,128)S(1)}, f32[1,1152]{1,0:T(1,128)}, u32[]{:S(2)}) copy-start(f32[1,1152]{1,0:T(1,128)} %gate_ref.3) | copy-start | bytes 13828
  38.1 32.6 %copy-start.4 = (s32[1,32]{1,0:T(1,128)S(1)}, s32[1,32]{1,0:T(1,128)}, u32[]{:S(2)}) copy-start(s32[1,32]{1,0:T(1,128)} %east_ref.3) | copy-start | bytes 388
  38.1 32.6 %copy-start.5 = (s32[1,32]{1,0:T(1,128)S(1)}, s32[1,32]{1,0:T(1,128)}, u32[]{:S(2)}) copy-start(s32[1,32]{1,0:T(1,128)} %west_ref.3) | copy-start | bytes 388
  38.1 24.8 %collective-permute-start.2 = (bf16[4,72,1152]{2,1,0:T(8,128)(2,1)S(1)}, bf16[4,72,1152]{2,1,0:T(8,128)(2,1)S(1)}, u32[]{:S(2)}, u32[]{:S(2)}) collective-permute-start(bf16[4,72,1152]{2,1,0:T(8,128)(2,1)S(1)} %get-tuple-element.14), channel_id=1, source_target_pairs={{0,17},{17,0},{1,16},{16,1},{2,19},{19,2},{3,18},{18,3},{4,21},{21... | collective-permute-start | bytes 1990664 | tf_op jit(solution)/shard_map/ppermute | solution.py:264
  56.3 28.8 %copy-start.6 = (s32[64,32]{0,1:T(8,128)S(1)}, s32[64,32]{0,1:T(8,128)}, u32[]{:S(2)}) copy-start(s32[64,32]{0,1:T(8,128)} %param.17) | copy-start | bytes 24580
  56.3 14.3 %all-to-all-start.2 = ((bf16[8,72,256]{2,1,0:T(8,128)(2,1)}), bf16[8,72,256]{2,1,0:T(8,128)(2,1)S(1)}, u32[]{:S(2)}, u32[]{:S(2)}) async-start(bf16[8,72,256]{2,1,0:T(8,128)(2,1)} %shard_map.94), calls=%async_computation.2 | async-start | bytes 589824 | tf_op jit(solution)/shard_map/all_to_all | solution.py:276
  71.6 14.5 %collective-permute-start.3 = (bf16[32,1152]{1,0:T(8,128)(2,1)S(1)}, bf16[32,1152]{1,0:T(8,128)(2,1)S(1)}, u32[]{:S(2)}, u32[]{:S(2)}) collective-permute-start(bf16[32,1152]{1,0:T(8,128)(2,1)S(1)} %get-tuple-element.15.a_ref), channel_id=1, source_target_pairs={{0,8},{8,0},{16,24},{24,16},{32,40},{40,32},{48,56},{56,48},{64,72... | collective-permute-start | bytes 221192 | tf_op jit(solution)/shard_map/ppermute | solution.py:287
  73.5 13.7 %collective-permute-start.4 = (bf16[32,1152]{1,0:T(8,128)(2,1)S(1)}, bf16[32,1152]{1,0:T(8,128)(2,1)S(1)}, u32[]{:S(2)}, u32[]{:S(2)}) collective-permute-start(bf16[32,1152]{1,0:T(8,128)(2,1)S(1)} %get-tuple-element.16.b_ref), channel_id=1, source_target_pairs={{0,504},{8,16},{16,8},{24,32},{32,24},{40,48},{48,40},{56,64},{64,... | collective-permute-start | bytes 221192 | tf_op jit(solution)/shard_map/ppermute | solution.py:286

commit v3 on v2

v3 whole, which is shorter than its diff:
```python
import functools
import math

import jax
import jax.numpy as jnp
from jax import lax
from jax.experimental import pallas as pl
from jax.experimental.pallas import tpu as pltpu
from jax.sharding import Mesh
from jax.sharding import PartitionSpec as P

D = 1152
HD = 72
TOK = 256
OV = 32
TILE = ("z", "ylo", "core")
SEQ = ("x", "yhi")
VMEM = pl.BlockSpec(memory_space=pltpu.VMEM)
HBM = pl.BlockSpec(memory_space=pltpu.HBM)
BF = jnp.bfloat16
F32 = jnp.float32


def call(kernel, outs, args, flops, nbytes, trans=0, ins=None, out_specs=None, scratch=()):
    return pl.pallas_call(
        kernel,
        out_shape=outs,
        in_specs=ins or [VMEM] * len(args),
        out_specs=out_specs or jax.tree.map(lambda _: VMEM, outs),
        scratch_shapes=scratch,
        compiler_params=pltpu.CompilerParams(vmem_limit_bytes=48 * 1024 * 1024),
        cost_estimate=pl.CostEstimate(
            flops=flops, bytes_accessed=nbytes, transcendentals=trans
        ),
    )(*args)


def pack_kernel(w_ref, wo_ref, out_ref, buf, sems):
    core = lax.axis_index("core")

    def put(first, second):
        loads = [
            pltpu.make_async_copy(first, buf.at[0], sems.at[4, 0]),
            pltpu.make_async_copy(second, buf.at[1], sems.at[4, 1]),
        ]
        for copy in loads:
            copy.start()
        copies = []
        for j in range(2):
            loads[j].wait()
            for i in range(4):
                copies.append(pltpu.make_async_copy(buf.at[j], out_ref.at[i, j], sems.at[i, j]))
                copies[-1].start()
        for copy in copies:
            copy.wait()

    @pl.when(core == 0)
    def _():
        put(w_ref.at[0], w_ref.at[1])

    @pl.when(core == 1)
    def _():
        put(w_ref.at[2], wo_ref)


def modulate(x_ref, shift, scale):
    x = x_ref[...].astype(F32)
    mean = jnp.sum(x, axis=-1, keepdims=True) * (1.0 / D)
    centered = x - mean
    var = jnp.sum(centered * centered, axis=-1, keepdims=True) * (1.0 / D)
    normed = centered * lax.rsqrt(var + 1e-06)
    return (normed * (1.0 + scale) + shift).astype(BF)


def column(row):
    size = row.shape[1]
    eye = lax.broadcasted_iota(jnp.int32, (size, size), 0) == lax.broadcasted_iota(
        jnp.int32, (size, size), 1
    )
    return jnp.sum(jnp.where(eye, row.astype(F32), 0.0), axis=1, keepdims=True)


def margin_rows(east, west):
    rows = jnp.concatenate([column(east), column(west)], axis=0).astype(jnp.int32)
    token = lax.broadcasted_iota(jnp.int32, (2 * OV, TOK), 1)
    return jnp.where(token == rows, 1.0, 0.0)


def token_order(east, west):
    margin = margin_rows(east, west)
    rest = 1.0 - jnp.sum(margin, axis=0, keepdims=True)
    before = lax.broadcasted_iota(jnp.int32, (TOK, TOK), 0) < lax.broadcasted_iota(
        jnp.int32, (TOK, TOK), 1
    )
    rank = jnp.dot(
        jnp.broadcast_to(rest, (16, TOK)).astype(BF),
        jnp.where(before, 1.0, 0.0).astype(BF),
        preferred_element_type=F32,
    )[:1].astype(jnp.int32)
    place = lax.broadcasted_iota(jnp.int32, (TOK - 2 * OV, TOK), 0)
    others = jnp.where(place == rank, rest, 0.0)
    return jnp.concatenate([margin, others], axis=0).astype(BF)


def norm_kernel(x_ref, xo_ref, shift_ref, scale_ref, east_ref, west_ref, oidx_ref, out_ref, perm_ref):
    shift = shift_ref[...]
    scale = scale_ref[...]
    mine = token_order(east_ref[...], west_ref[...])
    other = token_order(oidx_ref[:, :OV], oidx_ref[:, OV:])
    perm_ref[...] = mine
    a = jnp.dot(mine, modulate(x_ref, shift, scale), preferred_element_type=F32)
    b = jnp.dot(other, modulate(xo_ref, shift, scale), preferred_element_type=F32)
    m = 2 * OV
    out_ref[:, : 2 * m] = jnp.concatenate([a[:m], b[:m]], axis=0).T.astype(BF)
    out_ref[:, 2 * m :] = jnp.concatenate([a[m:], b[m:]], axis=0).T.astype(BF)


def qkv_kernel(mod_ref, mine_ref, other_ref, mine4_ref, other4_ref, out_ref, wo_ref, buf, sems, wsems):
    core = lax.axis_index("core")

    def go(qk_ref, vo_ref, vo4_ref):
        moves = [
            pltpu.make_async_copy(vo4_ref.at[h, 1], wo_ref.at[h], wsems.at[h]) for h in range(4)
        ]
        for move in moves:
            move.start()
        mod = mod_ref[...]
        qk = jnp.dot(qk_ref[...], mod, preferred_element_type=F32)
        vo = jnp.dot(vo_ref[...], mod, preferred_element_type=F32)
        for h in range(4):
            rows = jnp.concatenate(
                [qk[2 * HD * h : 2 * HD * (h + 1)], vo[2 * HD * h : 2 * HD * h + HD]], axis=0
            )
            buf[h] = rows.astype(BF)
            copy = pltpu.make_async_copy(buf.at[h], out_ref.at[h], sems.at[h])
            copy.start()
            moves.append(copy)
        for move in moves:
            move.wait()

    @pl.when(core == 0)
    def _():
        go(mine_ref, other_ref, other4_ref)

    @pl.when(core == 1)
    def _():
        go(other_ref, mine_ref, mine4_ref)


def attend(queries, keys, values, count, finish):
    def score(i):
        return [jnp.dot(k, queries(i), preferred_element_type=F32) for k in keys]

    ahead = score(0)
    for i in range(count):
        s = ahead
        if i + 1 < count:
            ahead = score(i + 1)
        peak = functools.reduce(jnp.maximum, [jnp.max(c, axis=0, keepdims=True) for c in s])
        o = sum(
            jnp.dot(v, jnp.exp2(c - peak).astype(BF), preferred_element_type=F32)
            for c, v in zip(s, values)
        )
        finish(i, (o[:HD] / o[HD : HD + 1]).astype(BF))


def margin_attention_kernel(qkv_ref, out_ref, k_ref, v_ref, q_ref, buf, sems):
    factor = math.log2(math.e) * HD**-0.5
    keys = []
    values = []
    first = []
    ones = jnp.ones((8, 2 * TOK), F32)
    for b in range(4):
        block = qkv_ref[b].astype(F32)
        q = block[:HD] * factor
        hi = q.astype(BF).astype(F32)
        lo = q - hi
        both = jnp.concatenate([hi, lo], axis=0).astype(BF)
        first.append(both[:, :128])
        q_ref[:, 384 * b : 384 * (b + 1)] = both[:, 128:]
        kt = block[HD : 2 * HD].T.astype(BF)
        keys.append(jnp.concatenate([kt, kt], axis=1))
        k_ref[b] = keys[b]
        values.append(jnp.concatenate([block[2 * HD :], ones], axis=0).astype(BF))
        v_ref[b] = values[b]
    groups = [jnp.concatenate(first[:2], axis=1), jnp.concatenate(first[2:], axis=1)]
    copies = []

    def finish(i, o):
        for j in range(2):
            b = 2 * i + j
            buf[b] = o[:, 128 * j : 128 * (j + 1)]
            for half in range(2):
                copies.append(
                    pltpu.make_async_copy(buf.at[b], out_ref.at[4 * half + b], sems.at[4 * half + b])
                )
                copies[-1].start()

    attend(lambda i: groups[i], keys, values, 2, finish)
    for copy in copies:
        copy.wait()


def attention_kernel(k_ref, v_ref, q_ref, out_ref, buf, sems):
    yhi = lax.axis_index("yhi")
    keys = [k_ref[b] for b in range(4)]
    values = [v_ref[b] for b in range(4)]
    ready = {1: (0,), 2: (1,), 4: (2,), 5: (3,)}
    copies = []

    def finish(i, o):
        buf[:, TOK * i : TOK * (i + 1)] = o
        for b in ready.get(i, ()):
            for half in range(2):
                slot = (yhi if half == 0 else 1 - yhi) * 4 + b
                copies.append(
                    pltpu.make_async_copy(
                        buf.at[:, pl.ds(384 * b + 128 * half, TOK)],
                        out_ref.at[slot],
                        sems.at[4 * half + b],
                    )
                )
                copies[-1].start()

    attend(lambda i: q_ref[:, TOK * i : TOK * (i + 1)], keys, values, 6, finish)
    for copy in copies:
        copy.wait()


def project(attn, wo):
    return lax.dot_general(attn, wo, (((0,), (0,)), ((), ())), preferred_element_type=F32)


def margin_kernel(attn_ref, wo_ref, wo2_ref, x_ref, gate_ref, east_ref, west_ref, a_ref, b_ref):
    yhi = lax.axis_index("yhi")
    first = lax.axis_index("core") == 0
    pick = margin_rows(east_ref[...], west_ref[...]).astype(BF)
    x = jnp.dot(pick, x_ref[...], preferred_element_type=F32)
    m = 2 * OV
    proj = project(attn_ref[yhi], wo_ref[...])[:m] + project(attn_ref[1 - yhi], wo2_ref[...])[m:]
    rows = x + gate_ref[...] * proj
    a_ref[...] = jnp.where(first, rows[:OV], rows[OV:]).astype(BF)
    b_ref[...] = jnp.where(first, rows[OV:], rows[:OV]).astype(BF)


def out_kernel(attn_ref, wo_ref, wo2_ref, x_ref, gate_ref, perm_ref, out_ref):
    yhi = lax.axis_index("yhi")
    m = 2 * OV
    proj = (
        project(attn_ref[yhi], wo_ref[...])[: TOK - m]
        + project(attn_ref[1 - yhi], wo2_ref[...])[m:]
    )
    x = jnp.dot(perm_ref[m:], x_ref[...], preferred_element_type=F32)
    out_ref[...] = (x + gate_ref[...] * proj).astype(BF)


def blend_kernel(rest_ref, a_ref, b_ref, ra_ref, rb_ref, perm_ref, bw_ref, out_ref):
    core = lax.axis_index("core")
    tile = lax.axis_index("z") * 4 + lax.axis_index("ylo") * 2 + core
    prior = jnp.where(tile == 0, 63, tile - 1)
    east = column(bw_ref[pl.ds(tile, 1), :])
    west = 8.0 - column(bw_ref[pl.ds(prior, 1), :])
    own_a = jnp.where(core == 0, east, west)
    own_b = jnp.where(core == 0, west, east)
    new_a = (own_a * a_ref[...].astype(F32) + (8.0 - own_a) * ra_ref[...].astype(F32)) / 8.0
    new_b = (own_b * b_ref[...].astype(F32) + (8.0 - own_b) * rb_ref[...].astype(F32)) / 8.0
    new_e = jnp.where(core == 0, new_a, new_b)
    new_w = jnp.where(core == 0, new_b, new_a)
    rows = jnp.concatenate([jnp.concatenate([new_e, new_w], axis=0).astype(BF), rest_ref[...]], axis=0)
    out_ref[...] = project(perm_ref[...], rows).astype(BF)


def body(tokens, mod_shift, mod_scale, mod_gate, w_qkv, w_out, east_rows, west_rows, blend_weight):
    sds = jax.ShapeDtypeStruct
    dma = pltpu.SemaphoreType.DMA
    x = tokens[0]
    swap = [(0, 1), (1, 0)]
    x_other = lax.ppermute(x, "yhi", swap)
    packed = call(
        pack_kernel,
        pltpu.HBM((4, 2, HD, D), BF),
        tuple(
            pltpu.with_memory_space_constraint(w, pltpu.HBM)
            for w in (jnp.transpose(w_qkv, (0, 2, 1)), w_out)
        ),
        1000,
        2000000,
        ins=[HBM, HBM],
        out_specs=HBM,
        scratch=[pltpu.VMEM((2, HD, D), BF), dma((5, 2))],
    )
    mine = lax.all_to_all(packed, "x", 0, 0, tiled=True)
    other_rows = lax.ppermute(jnp.concatenate([east_rows, west_rows], axis=1), "yhi", swap)
    mine, x_other, other_rows = lax.optimization_barrier((mine, x_other, other_rows))
    other = lax.ppermute(mine, "core", swap)
    mod, perm = call(
        norm_kernel,
        (sds((D, 2 * TOK), BF), sds((TOK, TOK), BF)),
        (x, x_other, mod_shift, mod_scale, east_rows, west_rows, other_rows),
        2 * 512 * 256 * D,
        3000000,
    )
    qkv, wo = call(
        qkv_kernel,
        (pltpu.HBM((4, 3 * HD, 2 * TOK), BF), sds((4, HD, D), BF)),
        (mod, mine.reshape(8 * HD, D), other.reshape(8 * HD, D), mine, other),
        2 * 512 * 1152 * D,
        6000000,
        out_specs=(HBM, VMEM),
        scratch=[pltpu.VMEM((4, 3 * HD, 2 * TOK), BF), dma((4,)), dma((4,))],
    )
    pairs = [(0, 3), (3, 0), (1, 2), (2, 1)]
    wo_other = lax.ppermute(wo, ("ylo", "yhi"), pairs)
    qkv = lax.all_to_all(qkv, "x", 0, 0, tiled=True)
    margins, keys, values, queries = call(
        margin_attention_kernel,
        (
            pltpu.HBM((8, HD, 128), BF),
            sds((4, 2 * TOK, 2 * HD), BF),
            sds((4, HD + 8, 2 * TOK), BF),
            sds((2 * HD, 1536), BF),
        ),
        (qkv,),
        4 * 512 * 2048 * 128,
        3000000,
        512 * 2048,
        out_specs=(HBM, VMEM, VMEM, VMEM),
        scratch=[pltpu.VMEM((4, HD, 128), BF), dma((8,))],
    )
    margins = lax.all_to_all(margins, ("yhi", "x"), 0, 0, tiled=True)
    attn = call(
        attention_kernel,
        pltpu.HBM((8, HD, TOK), BF),
        (keys, values, queries),
        4 * 1536 * 2048 * 128,
        2500000,
        1536 * 2048,
        out_specs=HBM,
        scratch=[pltpu.VMEM((HD, 1536), BF), dma((8,))],
    )
    margins, _ = lax.optimization_barrier((margins, attn))
    margins = margins.reshape(2, 4 * HD, 128)
    attn = lax.all_to_all(attn, ("yhi", "x"), 0, 0, tiled=True).reshape(2, 4 * HD, TOK)
    wo = wo.reshape(4 * HD, D)
    wo_other = wo_other.reshape(4 * HD, D)
    a, b = call(
        margin_kernel,
        (sds((OV, D), BF), sds((OV, D), BF)),
        (margins, wo, wo_other, x, mod_gate, east_rows, west_rows),
        2 * 128 * 576 * D,
        2000000,
    )
    other_b = lax.ppermute(b, TILE, [(i, (i + 2 * (i % 2) - 1) % 64) for i in range(64)])
    other_a = lax.ppermute(a, TILE, [(i, i + 1 - 2 * (i % 2)) for i in range(64)])
    rest = call(
        out_kernel,
        sds((TOK - 2 * OV, D), BF),
        (attn, wo, wo_other, x, mod_gate, perm),
        2 * 256 * 832 * D,
        3000000,
    )
    out = call(
        blend_kernel,
        sds((TOK, D), BF),
        (rest, a, b, other_a, other_b, perm, blend_weight),
        2 * 256 * 256 * D,
        1500000,
    )
    return out[None]


def solution(mesh):
    fine = Mesh(mesh.devices.reshape(16, 2, 2, 4, 2), ("z", "ylo", "core", "x", "yhi"))
    in_specs = (
        P(TILE, SEQ, None),
        P(TILE, None),
        P(TILE, None),
        P(TILE, None),
        P(None, None, SEQ),
        P(SEQ, None),
        P(TILE, SEQ),
        P(TILE, SEQ),
        P(None, SEQ),
    )
    out_specs = P(TILE, SEQ, None)
    return jax.shard_map(body, mesh=fine, in_specs=in_specs, out_specs=out_specs, check_vma=False)
```

time: 89 us -> 96 us (1.079)
  the two profiles are of different devices: /device:TPU:2 before, /device:TPU:16 now
where the time goes in v3:
time: 96 us; the launch traced here: 95.3 us
  starting transfers between devices  48.9 us (51%)
  waiting for transfers between devices  23.1 us (24%)
  Pallas kernels  17.2 us (18%)
  local copies, waits for them, and re-layouts  5.79 us (6%)
    pallas_call x8, Pallas kernels, call(): pl.pallas_call(kernel, out_shape=outs, in_specs=ins or [VMEM] * len(args)...  17.2 us
    ppermute x1, starting transfers between devices, body(): lax.ppermute(b, TILE, [(i, (i + 2 * (i % 2) - 1) % 64) for i in range(64)])  12.2 us
    all_to_all x1, waiting for transfers between devices, body(): qkv = lax.all_to_all(qkv, 'x', 0, 0, tiled=True)  11.3 us
    ppermute x1, waiting for transfers between devices, body(): lax.ppermute(jnp.concatenate([east_rows, west_rows], axis=1), 'yhi', swap)  9.34 us
    all_to_all x1, starting transfers between devices, body(): lax.all_to_all(attn, ('yhi', 'x'), 0, 0, tiled=True).reshape(2, 4 * HD, TOK)  7.35 us
    ppermute x1, starting transfers between devices, body(): x_other = lax.ppermute(x, 'yhi', swap)  6.88 us
    unnamed x31, local copies, waits for them, and re-layouts  5.79 us
    all_to_all x1, starting transfers between devices, body(): margins = lax.all_to_all(margins, ('yhi', 'x'), 0, 0, tiled=True)  5.41 us
  transfers between devices with their start and end apart: 10, of which 4 were waited for; matrix products, arithmetic and copies ran while one was open for 0% of the time, Pallas kernels for 11%

profile of v3, /device:TPU:16, one launch (start us, length us, event | category | flops | bytes accessed | tf_op | source)
XLA Modules:
  0.0 95.3 jit_solution(5662072213489801648)
XLA Ops:
  0.0 2.1 %shard_map.91 = bf16[4,2,72,1152]{3,2,1,0:T(8,128)(2,1)} custom-call(bf16[3,72,1152]{2,1,0:T(8,128)(2,1)} %bitcast.21, bf16[72,1152]{1,0:T(8,128)(2,1)} %wo_ref.1), custom_call_target="tpu_custom_call" | custom-call | flops 1000 | bytes 2000000 | tf_op jit(solution)/shard_map/pallas_call | solution.py:25
  2.1 0.0 copy-start
  2.1 0.0 copy-start.6
  2.2 4.4 %all-to-all-start = ((bf16[4,2,72,1152]{3,2,1,0:T(8,128)(2,1)}), bf16[4,2,72,1152]{3,2,1,0:T(8,128)(2,1)S(1)}, u32[]{:S(2)}, u32[]{:S(2)}) async-start(bf16[4,2,72,1152]{3,2,1,0:T(8,128)(2,1)} %shard_map.91), calls=%async_computation | async-start | bytes 2654208 | tf_op jit(solution)/shard_map/all_to_all | solution.py:292
  6.6 6.9 %collective-permute-start = (bf16[256,1152]{1,0:T(8,128)(2,1)S(1)}, bf16[256,1152]{1,0:T(8,128)(2,1)S(1)}, u32[]{:S(2)}, u32[]{:S(2)}) collective-permute-start(bf16[256,1152]{1,0:T(8,128)(2,1)S(1)} %bitcast.11), channel_id=1, source_target_pairs={{0,1},{1,0},{2,3},{3,2},{4,5},{5,4},{6,7},{7,6},{8,9},{9,8},{10,11... | collective-permute-start | bytes 1769480 | tf_op jit(solution)/shard_map/ppermute | solution.py:278
  13.5 0.1 pad_add_fusion
  13.6 1.9 %collective-permute-start.1 = (s32[1,64]{1,0:T(1,128)S(1)}, s32[1,64]{1,0:T(1,128)S(1)}, u32[]{:S(2)}, u32[]{:S(2)}) collective-permute-start(s32[1,64]{1,0:T(1,128)S(1)} %pad_add_fusion), channel_id=1, source_target_pairs={{0,1},{1,0},{2,3},{3,2},{4,5},{5,4},{6,7},{7,6},{8,9},{9,8},{10,11... | collective-permute-start | bytes 776 | tf_op jit(solution)/shard_map/ppermute | solution.py:293
  15.5 9.3 %collective-permute-done.1.oidx_ref = s32[1,64]{1,0:T(1,128)S(1)} collective-permute-done((s32[1,64]{1,0:T(1,128)S(1)}, s32[1,64]{1,0:T(1,128)S(1)}, u32[]{:S(2)}, u32[]{:S(2)}) %collective-permute-start.1) | collective-permute-done | bytes 288 | tf_op jit(solution)/shard_map/ppermute | solution.py:293
  24.8 1.9 %collective-permute-start.2 = (bf16[4,2,72,1152]{3,2,1,0:T(8,128)(2,1)S(1)}, bf16[4,2,72,1152]{3,2,1,0:T(8,128)(2,1)S(1)}, u32[]{:S(2)}, u32[]{:S(2)}) collective-permute-start(bf16[4,2,72,1152]{3,2,1,0:T(8,128)(2,1)S(1)} %all-to-all-done.mine4_ref), channel_id=1, source_target_pairs={{0,8},{8,0},{1,9},{9,1},{2,10},{10,2},{3,11},{11,3},{4,12},{12,4},... | collective-permute-start | bytes 3981320 | tf_op jit(solution)/shard_map/ppermute | solution.py:295
  26.8 1.4 %shard_map.92 = (bf16[1152,512]{1,0:T(8,128)(2,1)S(1)}, bf16[256,256]{1,0:T(8,128)(2,1)S(1)}) custom-call(bf16[256,1152]{1,0:T(8,128)(2,1)S(1)} %bitcast.12, bf16[256,1152]{1,0:T(8,128)(2,1)S(1)} %collective-permute-done.xo_ref, f32[1,1152]{1,0:T(1,128)S(1)} %copy-done.4, f32[1,1152]{1,0:T(1,128)S(1)} %copy-done.5, s32[1,32]{1,0:T(1,128)S(1)} %copy-done.6, ...), custom_call_target="tpu_custom_call" | custom-call | flops 301989888 | bytes 3000000 | tf_op jit(solution)/shard_map/pallas_call | solution.py:25
  28.2 1.5 %collective-permute-done.2.other4_ref = bf16[4,2,72,1152]{3,2,1,0:T(8,128)(2,1)S(1)} collective-permute-done((bf16[4,2,72,1152]{3,2,1,0:T(8,128)(2,1)S(1)}, bf16[4,2,72,1152]{3,2,1,0:T(8,128)(2,1)S(1)}, u32[]{:S(2)}, u32[]{:S(2)}) %collective-permute-start.2) | collective-permute-done | bytes 1327136 | tf_op jit(solution)/shard_map/ppermute | solution.py:295
  29.8 3.4 %shard_map.93 = (bf16[4,216,512]{2,1,0:T(8,128)(2,1)}, bf16[4,72,1152]{2,1,0:T(8,128)(2,1)S(1)}) custom-call(bf16[1152,512]{1,0:T(8,128)(2,1)S(1)} %get-tuple-element.21.mod_ref, bf16[576,1152]{1,0:T(8,128)(2,1)S(1)} %bitcast.9, bf16[576,1152]{1,0:T(8,128)(2,1)S(1)} %bitcast.10, bf16[4,2,72,1152]{3,2,1,0:T(8,128)(2,1)S(1)} %all-to-all-done.mine4_ref, ...), custom_call_target="tpu_custom_call" | custom-call | flops 1358954496 | bytes 6000000 | tf_op jit(solution)/shard_map/pallas_call | solution.py:25
  33.2 4.5 %all-to-all-start.1 = ((bf16[4,216,512]{2,1,0:T(8,128)(2,1)}), bf16[4,216,512]{2,1,0:T(8,128)(2,1)S(1)}, u32[]{:S(2)}, u32[]{:S(2)}) async-start(bf16[4,216,512]{2,1,0:T(8,128)(2,1)} %get-tuple-element.23), calls=%async_computation.1 | async-start | bytes 1769472 | tf_op jit(solution)/shard_map/all_to_all | solution.py:314
  37.7 2.3 %collective-permute-start.3 = (bf16[4,72,1152]{2,1,0:T(8,128)(2,1)S(1)}, bf16[4,72,1152]{2,1,0:T(8,128)(2,1)S(1)}, u32[]{:S(2)}, u32[]{:S(2)}) collective-permute-start(bf16[4,72,1152]{2,1,0:T(8,128)(2,1)S(1)} %get-tuple-element.27), channel_id=1, source_target_pairs={{0,17},{17,0},{1,16},{16,1},{2,19},{19,2},{3,18},{18,3},{4,21},{21... | collective-permute-start | bytes 1990664 | tf_op jit(solution)/shard_map/ppermute | solution.py:313
  40.1 11.3 %all-to-all-done.1.qkv_ref = bf16[4,216,512]{2,1,0:T(8,128)(2,1)S(1)} async-done(((bf16[4,216,512]{2,1,0:T(8,128)(2,1)}), bf16[4,216,512]{2,1,0:T(8,128)(2,1)S(1)}, u32[]{:S(2)}, u32[]{:S(2)}) %all-to-all-start.1) | async-done | bytes 884768 | tf_op jit(solution)/shard_map/all_to_all | solution.py:314
  51.4 2.7 %shard_map.94 = (bf16[8,72,128]{2,1,0:T(8,128)(2,1)}, bf16[4,512,144]{2,1,0:T(8,128)(2,1)S(1)}, bf16[4,80,512]{2,1,0:T(8,128)(2,1)S(1)}, bf16[144,1536]{1,0:T(8,128)(2,1)S(1)}) custom-call(bf16[4,216,512]{2,1,0:T(8,128)(2,1)S(1)} %all-to-all-done.1.qkv_ref), custom_call_target="tpu_custom_call" | custom-call | flops 536870912 | bytes 3000000 | tf_op jit(solution)/shard_map/pallas_call | solution.py:25
  54.1 1.0 %copy-done.8 = bf16[4,512,144]{2,1,0:T(8,128)(2,1)} copy-done((bf16[4,512,144]{2,1,0:T(8,128)(2,1)}, bf16[4,512,144]{2,1,0:T(8,128)(2,1)S(1)}, u32[]{:S(2)}) %copy-start.8) | copy-done | bytes 589848
  55.1 0.8 copy-done.10
  55.8 0.7 copy-done.12
  56.5 5.4 %all-to-all-start.3 = ((bf16[8,72,128]{2,1,0:T(8,128)(2,1)}), bf16[8,72,128]{2,1,0:T(8,128)(2,1)S(1)}, u32[]{:S(2)}, u32[]{:S(2)}) async-start(bf16[8,72,128]{2,1,0:T(8,128)(2,1)} %get-tuple-element.29), calls=%async_computation.3 | async-start | bytes 294912 | tf_op jit(solution)/shard_map/all_to_all | solution.py:330
  62.0 1.2 %copy-done.9 = bf16[4,512,144]{2,1,0:T(8,128)(2,1)S(1)} copy-done((bf16[4,512,144]{2,1,0:T(8,128)(2,1)S(1)}, bf16[4,512,144]{2,1,0:T(8,128)(2,1)}, u32[]{:S(2)}) %copy-start.9) | copy-done | bytes 589848
  63.2 1.0 %copy-done.11 = bf16[144,1536]{1,0:T(8,128)(2,1)S(1)} copy-done((bf16[144,1536]{1,0:T(8,128)(2,1)S(1)}, bf16[144,1536]{1,0:T(8,128)(2,1)}, u32[]{:S(2)}) %copy-start.11) | copy-done | bytes 442392
  64.2 1.0 %copy-done.13 = bf16[4,80,512]{2,1,0:T(8,128)(2,1)S(1)} copy-done((bf16[4,80,512]{2,1,0:T(8,128)(2,1)S(1)}, bf16[4,80,512]{2,1,0:T(8,128)(2,1)}, u32[]{:S(2)}) %copy-start.13) | copy-done | bytes 327704
  65.2 4.6 %shard_map.95 = bf16[8,72,256]{2,1,0:T(8,128)(2,1)} custom-call(bf16[4,512,144]{2,1,0:T(8,128)(2,1)S(1)} %copy-done.9, bf16[4,80,512]{2,1,0:T(8,128)(2,1)S(1)} %copy-done.13, bf16[144,1536]{1,0:T(8,128)(2,1)S(1)} %copy-done.11), custom_call_target="tpu_custom_call" | custom-call | flops 1610612736 | bytes 2500000 | tf_op jit(solution)/shard_map/pallas_call | solution.py:25
  69.8 7.4 %all-to-all-start.2 = ((bf16[8,72,256]{2,1,0:T(8,128)(2,1)}), bf16[8,72,256]{2,1,0:T(8,128)(2,1)S(1)}, u32[]{:S(2)}, u32[]{:S(2)}) async-start(bf16[8,72,256]{2,1,0:T(8,128)(2,1)} %shard_map.95), calls=%async_computation.2 | async-start | bytes 589824 | tf_op jit(solution)/shard_map/all_to_all | solution.py:343
  77.2 0.7 shard_map.97
  77.9 1.9 %collective-permute-start.4 = (bf16[32,1152]{1,0:T(8,128)(2,1)S(1)}, bf16[32,1152]{1,0:T(8,128)(2,1)S(1)}, u32[]{:S(2)}, u32[]{:S(2)}) collective-permute-start(bf16[32,1152]{1,0:T(8,128)(2,1)S(1)} %get-tuple-element.31.a_ref), channel_id=1, source_target_pairs={{0,8},{8,0},{16,24},{24,16},{32,40},{40,32},{48,56},{56,48},{64,72... | collective-permute-start | bytes 221192 | tf_op jit(solution)/shard_map/ppermute | solution.py:354
  79.8 12.2 %collective-permute-start.5 = (bf16[32,1152]{1,0:T(8,128)(2,1)S(1)}, bf16[32,1152]{1,0:T(8,128)(2,1)S(1)}, u32[]{:S(2)}, u32[]{:S(2)}) collective-permute-start(bf16[32,1152]{1,0:T(8,128)(2,1)S(1)} %get-tuple-element.32.b_ref), channel_id=1, source_target_pairs={{0,504},{8,16},{16,8},{24,32},{32,24},{40,48},{48,40},{56,64},{64,... | collective-permute-start | bytes 221192 | tf_op jit(solution)/shard_map/ppermute | solution.py:353
  92.0 0.1 copy.10.bw_ref
  92.1 1.0 %shard_map.96.rest_ref = bf16[192,1152]{1,0:T(8,128)(2,1)S(1)} custom-call(bf16[2,288,256]{2,1,0:T(8,128)(2,1)S(1)} %bitcast.19, bf16[288,1152]{1,0:T(8,128)(2,1)S(1)} %bitcast.16, bf16[288,1152]{1,0:T(8,128)(2,1)S(1)} %bitcast.18, bf16[256,1152]{1,0:T(8,128)(2,1)S(1)} %bitcast.14, f32[1,1152]{1,0:T(1,128)S(1)} %copy-done.3, bf16[256,256]{1,0:T(8,128)(2,1)S(1)} %copy-done.2), custom_call_target="tpu_custom_call" | custom-call | flops 490733568 | bytes 3000000 | tf_op jit(solution)/shard_map/pallas_call | solution.py:25
  93.1 0.9 collective-permute-done.5.rb_ref
  94.0 1.3 %shard_map.98 = bf16[256,1152]{1,0:T(8,128)(2,1)} custom-call(bf16[192,1152]{1,0:T(8,128)(2,1)S(1)} %shard_map.96.rest_ref, bf16[32,1152]{1,0:T(8,128)(2,1)S(1)} %get-tuple-element.31.a_ref, bf16[32,1152]{1,0:T(8,128)(2,1)S(1)} %get-tuple-element.32.b_ref, bf16[32,1152]{1,0:T(8,128)(2,1)S(1)} %collective-permute-done.4.ra_ref, ...), custom_call_target="tpu_custom_call" | custom-call | flops 150994944 | bytes 1500000 | tf_op jit(solution)/shard_map/pallas_call | solution.py:25
  (28 shorter events, 0.1 us)
Async XLA Ops:
  2.1 4.5 %copy-start = (bf16[1,256,1152]{2,1,0:T(8,128)(2,1)S(1)}, bf16[1,256,1152]{2,1,0:T(8,128)(2,1)}, u32[]{:S(2)}) copy-start(bf16[1,256,1152]{2,1,0:T(8,128)(2,1)} %param.9) | copy-start | bytes 1769476
  2.1 11.4 %copy-start.6 = (s32[1,32]{1,0:T(1,128)S(1)}, s32[1,32]{1,0:T(1,128)}, u32[]{:S(2)}) copy-start(s32[1,32]{1,0:T(1,128)} %east_ref.3) | copy-start | bytes 388
  2.1 11.4 %copy-start.7 = (s32[1,32]{1,0:T(1,128)S(1)}, s32[1,32]{1,0:T(1,128)}, u32[]{:S(2)}) copy-start(s32[1,32]{1,0:T(1,128)} %west_ref.3) | copy-start | bytes 388
  2.1 24.6 %copy-start.4 = (f32[1,1152]{1,0:T(1,128)S(1)}, f32[1,1152]{1,0:T(1,128)}, u32[]{:S(2)}) copy-start(f32[1,1152]{1,0:T(1,128)} %shift_ref.1) | copy-start | bytes 13828
  2.1 24.6 %copy-start.5 = (f32[1,1152]{1,0:T(1,128)S(1)}, f32[1,1152]{1,0:T(1,128)}, u32[]{:S(2)}) copy-start(f32[1,1152]{1,0:T(1,128)} %scale_ref.1) | copy-start | bytes 13828
  2.2 22.7 %all-to-all-start = ((bf16[4,2,72,1152]{3,2,1,0:T(8,128)(2,1)}), bf16[4,2,72,1152]{3,2,1,0:T(8,128)(2,1)S(1)}, u32[]{:S(2)}, u32[]{:S(2)}) async-start(bf16[4,2,72,1152]{3,2,1,0:T(8,128)(2,1)} %shard_map.91), calls=%async_computation | async-start | bytes 2654208 | tf_op jit(solution)/shard_map/all_to_all | solution.py:292
  6.6 18.2 %collective-permute-start = (bf16[256,1152]{1,0:T(8,128)(2,1)S(1)}, bf16[256,1152]{1,0:T(8,128)(2,1)S(1)}, u32[]{:S(2)}, u32[]{:S(2)}) collective-permute-start(bf16[256,1152]{1,0:T(8,128)(2,1)S(1)} %bitcast.11), channel_id=1, source_target_pairs={{0,1},{1,0},{2,3},{3,2},{4,5},{5,4},{6,7},{7,6},{8,9},{9,8},{10,11... | collective-permute-start | bytes 1769480 | tf_op jit(solution)/shard_map/ppermute | solution.py:278
  13.6 11.3 %collective-permute-start.1 = (s32[1,64]{1,0:T(1,128)S(1)}, s32[1,64]{1,0:T(1,128)S(1)}, u32[]{:S(2)}, u32[]{:S(2)}) collective-permute-start(s32[1,64]{1,0:T(1,128)S(1)} %pad_add_fusion), channel_id=1, source_target_pairs={{0,1},{1,0},{2,3},{3,2},{4,5},{5,4},{6,7},{7,6},{8,9},{9,8},{10,11... | collective-permute-start | bytes 776 | tf_op jit(solution)/shard_map/ppermute | solution.py:293
  24.8 4.9 %collective-permute-start.2 = (bf16[4,2,72,1152]{3,2,1,0:T(8,128)(2,1)S(1)}, bf16[4,2,72,1152]{3,2,1,0:T(8,128)(2,1)S(1)}, u32[]{:S(2)}, u32[]{:S(2)}) collective-permute-start(bf16[4,2,72,1152]{3,2,1,0:T(8,128)(2,1)S(1)} %all-to-all-done.mine4_ref), channel_id=1, source_target_pairs={{0,8},{8,0},{1,9},{9,1},{2,10},{10,2},{3,11},{11,3},{4,12},{12,4},... | collective-permute-start | bytes 3981320 | tf_op jit(solution)/shard_map/ppermute | solution.py:295
  28.2 4.9 %copy-start.1 = (bf16[256,256]{1,0:T(8,128)(2,1)}, bf16[256,256]{1,0:T(8,128)(2,1)S(1)}, u32[]{:S(2)}) copy-start(bf16[256,256]{1,0:T(8,128)(2,1)S(1)} %get-tuple-element.28.perm_ref) | copy-start | bytes 393220
  33.2 18.2 %all-to-all-start.1 = ((bf16[4,216,512]{2,1,0:T(8,128)(2,1)}), bf16[4,216,512]{2,1,0:T(8,128)(2,1)S(1)}, u32[]{:S(2)}, u32[]{:S(2)}) async-start(bf16[4,216,512]{2,1,0:T(8,128)(2,1)} %get-tuple-element.23), calls=%async_computation.1 | async-start | bytes 1769472 | tf_op jit(solution)/shard_map/all_to_all | solution.py:314
  37.7 39.5 %collective-permute-start.3 = (bf16[4,72,1152]{2,1,0:T(8,128)(2,1)S(1)}, bf16[4,72,1152]{2,1,0:T(8,128)(2,1)S(1)}, u32[]{:S(2)}, u32[]{:S(2)}) collective-permute-start(bf16[4,72,1152]{2,1,0:T(8,128)(2,1)S(1)} %get-tuple-element.27), channel_id=1, source_target_pairs={{0,17},{17,0},{1,16},{16,1},{2,19},{19,2},{3,18},{18,3},{4,21},{21... | collective-permute-start | bytes 1990664 | tf_op jit(solution)/shard_map/ppermute | solution.py:313
  54.1 1.0 %copy-start.8 = (bf16[4,512,144]{2,1,0:T(8,128)(2,1)}, bf16[4,512,144]{2,1,0:T(8,128)(2,1)S(1)}, u32[]{:S(2)}) copy-start(bf16[4,512,144]{2,1,0:T(8,128)(2,1)S(1)} %get-tuple-element.24.k_ref) | copy-start | bytes 1769476
  55.1 0.8 copy-start.10
  55.8 0.7 copy-start.12
  56.5 13.3 %all-to-all-start.3 = ((bf16[8,72,128]{2,1,0:T(8,128)(2,1)}), bf16[8,72,128]{2,1,0:T(8,128)(2,1)S(1)}, u32[]{:S(2)}, u32[]{:S(2)}) async-start(bf16[8,72,128]{2,1,0:T(8,128)(2,1)} %get-tuple-element.29), calls=%async_computation.3 | async-start | bytes 294912 | tf_op jit(solution)/shard_map/all_to_all | solution.py:330
  62.0 1.2 %copy-start.9 = (bf16[4,512,144]{2,1,0:T(8,128)(2,1)S(1)}, bf16[4,512,144]{2,1,0:T(8,128)(2,1)}, u32[]{:S(2)}) copy-start(bf16[4,512,144]{2,1,0:T(8,128)(2,1)} %copy-done.8) | copy-start | bytes 1769476
  63.2 1.0 %copy-start.11 = (bf16[144,1536]{1,0:T(8,128)(2,1)S(1)}, bf16[144,1536]{1,0:T(8,128)(2,1)}, u32[]{:S(2)}) copy-start(bf16[144,1536]{1,0:T(8,128)(2,1)} %copy-done.10) | copy-start | bytes 1327108
  64.2 1.0 %copy-start.13 = (bf16[4,80,512]{2,1,0:T(8,128)(2,1)S(1)}, bf16[4,80,512]{2,1,0:T(8,128)(2,1)}, u32[]{:S(2)}) copy-start(bf16[4,80,512]{2,1,0:T(8,128)(2,1)} %copy-done.12) | copy-start | bytes 983044
  65.2 12.0 %copy-start.3 = (f32[1,1152]{1,0:T(1,128)S(1)}, f32[1,1152]{1,0:T(1,128)}, u32[]{:S(2)}) copy-start(f32[1,1152]{1,0:T(1,128)} %gate_ref.3) | copy-start | bytes 13828
  69.8 22.2 %copy-start.14 = (s32[64,32]{0,1:T(8,128)S(1)}, s32[64,32]{0,1:T(8,128)}, u32[]{:S(2)}) copy-start(s32[64,32]{0,1:T(8,128)} %param.17) | copy-start | bytes 24580
  69.8 22.3 %copy-start.2 = (bf16[256,256]{1,0:T(8,128)(2,1)S(1)}, bf16[256,256]{1,0:T(8,128)(2,1)}, u32[]{:S(2)}) copy-start(bf16[256,256]{1,0:T(8,128)(2,1)} %copy-done.1) | copy-start | bytes 393220
  69.8 22.3 %all-to-all-start.2 = ((bf16[8,72,256]{2,1,0:T(8,128)(2,1)}), bf16[8,72,256]{2,1,0:T(8,128)(2,1)S(1)}, u32[]{:S(2)}, u32[]{:S(2)}) async-start(bf16[8,72,256]{2,1,0:T(8,128)(2,1)} %shard_map.95), calls=%async_computation.2 | async-start | bytes 589824 | tf_op jit(solution)/shard_map/all_to_all | solution.py:343
  77.9 15.3 %collective-permute-start.4 = (bf16[32,1152]{1,0:T(8,128)(2,1)S(1)}, bf16[32,1152]{1,0:T(8,128)(2,1)S(1)}, u32[]{:S(2)}, u32[]{:S(2)}) collective-permute-start(bf16[32,1152]{1,0:T(8,128)(2,1)S(1)} %get-tuple-element.31.a_ref), channel_id=1, source_target_pairs={{0,8},{8,0},{16,24},{24,16},{32,40},{40,32},{48,56},{56,48},{64,72... | collective-permute-start | bytes 221192 | tf_op jit(solution)/shard_map/ppermute | solution.py:354
  79.8 14.3 %collective-permute-start.5 = (bf16[32,1152]{1,0:T(8,128)(2,1)S(1)}, bf16[32,1152]{1,0:T(8,128)(2,1)S(1)}, u32[]{:S(2)}, u32[]{:S(2)}) collective-permute-start(bf16[32,1152]{1,0:T(8,128)(2,1)S(1)} %get-tuple-element.32.b_ref), channel_id=1, source_target_pairs={{0,504},{8,16},{16,8},{24,32},{32,24},{40,48},{48,40},{56,64},{64,... | collective-permute-start | bytes 221192 | tf_op jit(solution)/shard_map/ppermute | solution.py:353

commit v4 on v2

--- a/solution.py
+++ b/solution.py
@@ -35,22 +35,16 @@
     )(*args)
 
 
-def pack_kernel(w_ref, wo_ref, out_ref, buf, sems):
+def pack_kernel(w_ref, wo_ref, out_ref, sems):
     core = lax.axis_index("core")
 
     def put(first, second):
-        loads = [
-            pltpu.make_async_copy(first, buf.at[0], sems.at[4, 0]),
-            pltpu.make_async_copy(second, buf.at[1], sems.at[4, 1]),
+        copies = [
+            pltpu.make_async_copy(first, out_ref.at[0], sems.at[0]),
+            pltpu.make_async_copy(second, out_ref.at[1], sems.at[1]),
         ]
-        for copy in loads:
+        for copy in copies:
             copy.start()
-        copies = []
-        for j in range(2):
-            loads[j].wait()
-            for i in range(4):
-                copies.append(pltpu.make_async_copy(buf.at[j], out_ref.at[i, j], sems.at[i, j]))
-                copies[-1].start()
         for copy in copies:
             copy.wait()
 
@@ -79,47 +73,61 @@
     out_ref[:, TOK:] = modulate(xo_ref, shift, scale).T.astype(BF)
 
 
-def qkv_kernel(mod_ref, mine_ref, other_ref, mine4_ref, other4_ref, out_ref, wo_ref, buf, sems, wsems):
+def half_kernel(mod_ref, w0_ref, w1_ref, w2_ref, w3_ref, out_ref):
+    mod = mod_ref[...]
+    for d, w_ref in enumerate((w0_ref, w1_ref, w2_ref, w3_ref)):
+        out_ref[d] = jnp.dot(w_ref[...], mod, preferred_element_type=F32).astype(BF)
+
+
+def qkv_kernel(mod_ref, half_ref, *refs):
+    others, mine3, other3 = refs[:4], refs[4:8], refs[8:12]
+    outs, wo_ref, sems = refs[12:16], refs[16], refs[17]
     core = lax.axis_index("core")
-
-    def go(qk_ref, vo_ref, vo4_ref):
+    x = lax.axis_index("x")
+
+    def moved(pieces):
         moves = [
-            pltpu.make_async_copy(vo4_ref.at[h, 1], wo_ref.at[h], wsems.at[h]) for h in range(4)
+            pltpu.make_async_copy(
+                pieces[d].at[1], wo_ref.at[lax.rem(x + d, 4)], sems.at[d]
+            )
+            for d in range(4)
         ]
         for move in moves:
             move.start()
+        return moves
+
+    @pl.when(core == 0)
+    def _():
+        moves = moved(other3)
         mod = mod_ref[...]
-        qk = jnp.dot(qk_ref[...], mod, preferred_element_type=F32)
-        vo = jnp.dot(vo_ref[...], mod, preferred_element_type=F32)
-        for h in range(4):
-            rows = jnp.concatenate(
-                [qk[2 * HD * h : 2 * HD * (h + 1)], vo[2 * HD * h : 2 * HD * h + HD]], axis=0
-            )
-            buf[h] = rows.astype(BF)
-            copy = pltpu.make_async_copy(buf.at[h], out_ref.at[h], sems.at[h])
-            copy.start()
-            moves.append(copy)
+        for d in range(4):
+            v = jnp.dot(others[d][:80], mod, preferred_element_type=F32)[:HD]
+            outs[d][...] = jnp.concatenate([half_ref[d].astype(F32), v], axis=0).astype(BF)
         for move in moves:
             move.wait()
 
-    @pl.when(core == 0)
-    def _():
-        go(mine_ref, other_ref, other4_ref)
-
     @pl.when(core == 1)
     def _():
-        go(other_ref, mine_ref, mine4_ref)
-
-
-def attention_kernel(qkv_ref, out_ref, buf, sems):
+        moves = moved(mine3)
+        mod = mod_ref[...]
+        for d in range(4):
+            qk = jnp.dot(others[d][...], mod, preferred_element_type=F32)
+            v = half_ref[d].astype(F32)[:HD]
+            outs[d][...] = jnp.concatenate([qk, v], axis=0).astype(BF)
+        for move in moves:
+            move.wait()
+
+
+def attention_kernel(q0_ref, q1_ref, q2_ref, q3_ref, out_ref, buf, sems):
     yhi = lax.axis_index("yhi")
+    x = lax.axis_index("x")
     factor = math.log2(math.e) * HD**-0.5
     keys = []
     values = []
     queries = []
     ones = jnp.ones((8, 2 * TOK), F32)
     for b in range(4):
-        block = qkv_ref[b].astype(F32)
+        block = (q0_ref, q1_ref, q2_ref, q3_ref)[b][...].astype(F32)
         q = block[:HD] * factor
         hi = q.astype(BF).astype(F32)
         lo = q - hi
@@ -146,7 +154,7 @@
             for c, v in zip(s, values)
         )
         _, b, half = queries[i]
-        slot = (yhi if half == 0 else 1 - yhi) * 4 + b
+        slot = (yhi if half == 0 else 1 - yhi) * 4 + lax.rem(x + 4 - b, 4)
         buf[i] = (o[:HD] / o[HD : HD + 1]).astype(BF)
         copies.append(pltpu.make_async_copy(buf.at[i], out_ref.at[slot], sems.at[i]))
         copies[-1].start()
@@ -181,7 +189,7 @@
     return lax.dot_general(attn, wo, (((0,), (0,)), ((), ())), preferred_element_type=F32)
 
 
-def margin_kernel(attn_ref, wo_ref, wo2_ref, x_ref, gate_ref, east_ref, west_ref, a_ref, b_ref):
+def margin_kernel(attn_ref, wo_ref, wo2_ref, x_ref, gate_ref, east_ref, west_ref, b_ref, a_ref):
     yhi = lax.axis_index("yhi")
     pick = select_rows(east_ref, west_ref)
     nt = (((1,), (1,)), ((), ()))
@@ -202,7 +210,7 @@
     out_ref[...] = (x_ref[...].astype(F32) + gate_ref[...] * proj).astype(BF)
 
 
-def blend_kernel(lay_ref, a_ref, b_ref, ra_ref, rb_ref, east_ref, west_ref, bw_ref, out_ref):
+def blend_kernel(lay_ref, b_ref, a_ref, rb_ref, ra_ref, east_ref, west_ref, bw_ref, out_ref):
     core = lax.axis_index("core")
     tile = lax.axis_index("z") * 4 + lax.axis_index("ylo") * 2 + core
     prior = jnp.where(tile == 0, 63, tile - 1)
@@ -228,22 +236,27 @@
     x = tokens[0]
     swap = [(0, 1), (1, 0)]
     x_other = lax.ppermute(x, "yhi", swap)
-    packed = call(
+    piece = call(
         pack_kernel,
-        pltpu.HBM((4, 2, HD, D), BF),
+        sds((2, HD, D), BF),
         tuple(
             pltpu.with_memory_space_constraint(w, pltpu.HBM)
             for w in (jnp.transpose(w_qkv, (0, 2, 1)), w_out)
         ),
         1000,
-        2000000,
+        600000,
         ins=[HBM, HBM],
-        out_specs=HBM,
-        scratch=[pltpu.VMEM((2, HD, D), BF), dma((5, 2))],
-    )
-    mine = lax.all_to_all(packed, "x", 0, 0, tiled=True)
-    mine, x_other = lax.optimization_barrier((mine, x_other))
-    other = lax.ppermute(mine, "core", swap)
+        scratch=[dma((2,))],
+    )
+
+    def send(value, by):
+        return lax.ppermute(value, "x", [(i, (i + by) % 4) for i in range(4)])
+
+    mine = [piece, send(piece, -1), send(piece, -2), send(piece, -3)]
+    other = [lax.ppermute(mine[d], "core", swap) for d in (0, 1, 3)]
+    last, x_other, other = lax.optimization_barrier((mine[2], x_other, other))
+    mine[2] = last
+    other.insert(2, lax.ppermute(last, "core", swap))
     mod = call(
         norm_kernel,
         sds((D, 2 * TOK), BF),
@@ -251,22 +264,28 @@
         20 * 512 * D,
         3000000,
     )
-    qkv, wo = call(
+    half = call(
+        half_kernel,
+        sds((4, 2 * HD, 2 * TOK), BF),
+        (mod, *[w.reshape(2 * HD, D) for w in mine]),
+        2 * 512 * 576 * D,
+        3000000,
+    )
+    *qkv, wo = call(
         qkv_kernel,
-        (pltpu.HBM((4, 3 * HD, 2 * TOK), BF), sds((4, HD, D), BF)),
-        (mod, mine.reshape(8 * HD, D), other.reshape(8 * HD, D), mine, other),
-        2 * 512 * 1152 * D,
+        (sds((3 * HD, 2 * TOK), BF),) * 4 + (sds((4, HD, D), BF),),
+        (mod, half, *[w.reshape(2 * HD, D) for w in other], *mine, *other),
+        2 * 512 * 576 * D,
         6000000,
-        out_specs=(HBM, VMEM),
-        scratch=[pltpu.VMEM((4, 3 * HD, 2 * TOK), BF), dma((4,)), dma((4,))],
+        scratch=[dma((4,))],
     )
     pairs = [(0, 3), (3, 0), (1, 2), (2, 1)]
     wo_other = lax.ppermute(wo, ("ylo", "yhi"), pairs)
-    qkv = lax.all_to_all(qkv, "x", 0, 0, tiled=True)
+    qkv = [qkv[0]] + [send(qkv[d], d) for d in (1, 2, 3)]
     attn = call(
         attention_kernel,
         pltpu.HBM((8, HD, TOK), BF),
-        (qkv,),
+        tuple(qkv),
         4 * 2048 * 2048 * 128,
         1500000,
         2048 * 2048,
@@ -276,7 +295,7 @@
     attn = lax.all_to_all(attn, ("yhi", "x"), 0, 0, tiled=True).reshape(2, 4 * HD, TOK)
     wo = wo.reshape(4 * HD, D)
     wo_other = wo_other.reshape(4 * HD, D)
-    a, b = call(
+    b, a = call(
         margin_kernel,
         (sds((OV, D), BF), sds((OV, D), BF)),
         (attn, wo, wo_other, x, mod_gate, east_rows, west_rows),
@@ -295,7 +314,7 @@
     out = call(
         blend_kernel,
         sds((TOK, D), BF),
-        (lay, a, b, other_a, other_b, east_rows, west_rows, blend_weight),
+        (lay, b, a, other_b, other_a, east_rows, west_rows, blend_weight),
         2 * 256 * 64 * D,
         1500000,
     )

time: 89 us -> 91.5 us (1.028)
  the two profiles are of different devices: /device:TPU:2 before, /device:TPU:1 now
where the time goes in v4:
time: 91.5 us; the launch traced here: 90.9 us
  starting transfers between devices  55.1 us (60%)
  Pallas kernels  14.3 us (16%)
  blocking collectives  12.9 us (14%)
  waiting for transfers between devices  6.79 us (7%)
  local copies, waits for them, and re-layouts  1.47 us (2%)
    ppermute x6, starting transfers between devices, send(): return lax.ppermute(value, 'x', [(i, (i + by) % 4) for i in range(4)])  18 us
    pallas_call x8, Pallas kernels, call(): pl.pallas_call(kernel, out_shape=outs, in_specs=ins or [VMEM] * len(args)...  14.3 us
    all_to_all x1, blocking collectives, body(): lax.all_to_all(attn, ('yhi', 'x'), 0, 0, tiled=True).reshape(2, 4 * HD, TOK)  12.9 us
    ppermute x3, starting transfers between devices, body(): other = [lax.ppermute(mine[d], 'core', swap) for d in (0, 1, 3)]  12.4 us
    ppermute x1, starting transfers between devices, body(): lax.ppermute(a, TILE, [(i, i + 1 - 2 * (i % 2)) for i in range(64)])  8.99 us
    ppermute x6, waiting for transfers between devices, send(): return lax.ppermute(value, 'x', [(i, (i + by) % 4) for i in range(4)])  5.58 us
    ppermute x1, starting transfers between devices, body(): x_other = lax.ppermute(x, 'yhi', swap)  4.82 us
    ppermute x1, starting transfers between devices, body(): lax.ppermute(b, TILE, [(i, (i + 2 * (i % 2) - 1) % 64) for i in range(64)])  4.55 us
  transfers between devices with their start and end apart: 14, of which 2 were waited for; matrix products, arithmetic and copies ran while one was open for 0% of the time, Pallas kernels for 10%

profile of v4, /device:TPU:1, one launch (start us, length us, event | category | flops | bytes accessed | tf_op | source)
XLA Modules:
  0.0 90.9 jit_solution(2254089107347260161)
XLA Ops:
  0.0 1.1 %shard_map.91.refs_4_ = bf16[2,72,1152]{2,1,0:T(8,128)(2,1)S(1)} custom-call(bf16[3,72,1152]{2,1,0:T(8,128)(2,1)} %bitcast.32, bf16[72,1152]{1,0:T(8,128)(2,1)} %wo_ref.1), custom_call_target="tpu_custom_call" | custom-call | flops 1000 | bytes 600000 | tf_op jit(solution)/shard_map/pallas_call | solution.py:25
  1.1 5.2 %collective-permute-start.3 = (bf16[2,72,1152]{2,1,0:T(8,128)(2,1)S(1)}, bf16[2,72,1152]{2,1,0:T(8,128)(2,1)S(1)}, u32[]{:S(2)}, u32[]{:S(2)}) collective-permute-start(bf16[2,72,1152]{2,1,0:T(8,128)(2,1)S(1)} %shard_map.91.refs_4_), channel_id=1, source_target_pairs={{0,6},{2,0},{4,2},{6,4},{1,7},{3,1},{5,3},{7,5},{8,14},{10,8},{12,... | collective-permute-start | bytes 995336 | tf_op jit(solution)/shard_map/ppermute | solution.py:253
  6.3 1.9 %collective-permute-start.5 = (bf16[2,72,1152]{2,1,0:T(8,128)(2,1)S(1)}, bf16[2,72,1152]{2,1,0:T(8,128)(2,1)S(1)}, u32[]{:S(2)}, u32[]{:S(2)}) collective-permute-start(bf16[2,72,1152]{2,1,0:T(8,128)(2,1)S(1)} %shard_map.91.refs_4_), channel_id=1, source_target_pairs={{0,2},{2,4},{4,6},{6,0},{1,3},{3,5},{5,7},{7,1},{8,10},{10,12},{12... | collective-permute-start | bytes 995336 | tf_op jit(solution)/shard_map/ppermute | solution.py:253
  8.2 4.8 %collective-permute-start.1 = (bf16[256,1152]{1,0:T(8,128)(2,1)}, bf16[256,1152]{1,0:T(8,128)(2,1)S(1)}, u32[]{:S(2)}, u32[]{:S(2)}) collective-permute-start(bf16[256,1152]{1,0:T(8,128)(2,1)} %bitcast.14), channel_id=1, source_target_pairs={{0,1},{1,0},{2,3},{3,2},{4,5},{5,4},{6,7},{7,6},{8,9},{9,8},{10,11... | collective-permute-start | bytes 1769480 | tf_op jit(solution)/shard_map/ppermute | solution.py:238
  13.1 3.6 %collective-permute-start = (bf16[2,72,1152]{2,1,0:T(8,128)(2,1)S(1)}, bf16[2,72,1152]{2,1,0:T(8,128)(2,1)S(1)}, u32[]{:S(2)}, u32[]{:S(2)}) collective-permute-start(bf16[2,72,1152]{2,1,0:T(8,128)(2,1)S(1)} %shard_map.91.refs_4_), channel_id=1, source_target_pairs={{0,4},{2,6},{4,0},{6,2},{1,5},{3,7},{5,1},{7,3},{8,12},{10,14},{12... | collective-permute-start | bytes 995336 | tf_op jit(solution)/shard_map/ppermute | solution.py:253
  16.7 3.7 %collective-permute-start.2 = (bf16[2,72,1152]{2,1,0:T(8,128)(2,1)S(1)}, bf16[2,72,1152]{2,1,0:T(8,128)(2,1)S(1)}, u32[]{:S(2)}, u32[]{:S(2)}) collective-permute-start(bf16[2,72,1152]{2,1,0:T(8,128)(2,1)S(1)} %shard_map.91.refs_4_), channel_id=1, source_target_pairs={{0,8},{8,0},{1,9},{9,1},{2,10},{10,2},{3,11},{11,3},{4,12},{12,4},... | collective-permute-start | bytes 995336 | tf_op jit(solution)/shard_map/ppermute | solution.py:256
  20.4 1.9 %collective-permute-start.4 = (bf16[2,72,1152]{2,1,0:T(8,128)(2,1)S(1)}, bf16[2,72,1152]{2,1,0:T(8,128)(2,1)S(1)}, u32[]{:S(2)}, u32[]{:S(2)}) collective-permute-start(bf16[2,72,1152]{2,1,0:T(8,128)(2,1)S(1)} %collective-permute-done.3.refs_5_), channel_id=1, source_target_pairs={{0,8},{8,0},{1,9},{9,1},{2,10},{10,2},{3,11},{11,3},{4,12},{12,4},... | collective-permute-start | bytes 995336 | tf_op jit(solution)/shard_map/ppermute | solution.py:256
  22.4 0.0 collective-permute-done.5.refs_7_
  22.4 6.8 %collective-permute-start.6 = (bf16[2,72,1152]{2,1,0:T(8,128)(2,1)S(1)}, bf16[2,72,1152]{2,1,0:T(8,128)(2,1)S(1)}, u32[]{:S(2)}, u32[]{:S(2)}) collective-permute-start(bf16[2,72,1152]{2,1,0:T(8,128)(2,1)S(1)} %collective-permute-done.5.refs_7_), channel_id=1, source_target_pairs={{0,8},{8,0},{1,9},{9,1},{2,10},{10,2},{3,11},{11,3},{4,12},{12,4},... | collective-permute-start | bytes 995336 | tf_op jit(solution)/shard_map/ppermute | solution.py:256
  29.1 0.0 collective-permute-done.refs_6_
  29.2 0.0 collective-permute-done.1.xo_ref
  29.2 1.2 %collective-permute-done.6.refs_11_ = bf16[2,72,1152]{2,1,0:T(8,128)(2,1)S(1)} collective-permute-done((bf16[2,72,1152]{2,1,0:T(8,128)(2,1)S(1)}, bf16[2,72,1152]{2,1,0:T(8,128)(2,1)S(1)}, u32[]{:S(2)}, u32[]{:S(2)}) %collective-permute-start.6) | collective-permute-done | bytes 331808 | tf_op jit(solution)/shard_map/ppermute | solution.py:256
  30.4 2.3 %collective-permute-start.7 = (bf16[2,72,1152]{2,1,0:T(8,128)(2,1)S(1)}, bf16[2,72,1152]{2,1,0:T(8,128)(2,1)S(1)}, u32[]{:S(2)}, u32[]{:S(2)}) collective-permute-start(bf16[2,72,1152]{2,1,0:T(8,128)(2,1)S(1)} %collective-permute-done.refs_6_), channel_id=1, source_target_pairs={{0,8},{8,0},{1,9},{9,1},{2,10},{10,2},{3,11},{11,3},{4,12},{12,4},... | collective-permute-start | bytes 995336 | tf_op jit(solution)/shard_map/ppermute | solution.py:259
  32.7 0.0 copy-start.2
  32.7 0.7 copy-done.2
  33.4 0.7 copy-done.3
  34.0 1.0 %shard_map.92.mod_ref = bf16[1152,512]{1,0:T(8,128)(2,1)S(1)} custom-call(bf16[256,1152]{1,0:T(8,128)(2,1)S(1)} %bitcast.15, bf16[256,1152]{1,0:T(8,128)(2,1)S(1)} %collective-permute-done.1.xo_ref, f32[1,1152]{1,0:T(1,128)S(1)} %copy-done.2, f32[1,1152]{1,0:T(1,128)S(1)} %copy-done.3), custom_call_target="tpu_custom_call" | custom-call | flops 11796480 | bytes 3000000 | tf_op jit(solution)/shard_map/pallas_call | solution.py:25
  35.1 1.0 %shard_map.93.half_ref = bf16[4,144,512]{2,1,0:T(8,128)(2,1)S(1)} custom-call(bf16[1152,512]{1,0:T(8,128)(2,1)S(1)} %shard_map.92.mod_ref, bf16[144,1152]{1,0:T(8,128)(2,1)S(1)} %bitcast.18, bf16[144,1152]{1,0:T(8,128)(2,1)S(1)} %bitcast.25, bf16[144,1152]{1,0:T(8,128)(2,1)S(1)} %bitcast.27, bf16[144,1152]{1,0:T(8,128)(2,1)S(1)} %bitcast.26), custom_call_target="tpu_custom_call" | custom-call | flops 679477248 | bytes 3000000 | tf_op jit(solution)/shard_map/pallas_call | solution.py:25
  36.0 2.1 %shard_map.94 = (bf16[216,512]{1,0:T(8,128)(2,1)S(1)}, bf16[216,512]{1,0:T(8,128)(2,1)S(1)}, bf16[216,512]{1,0:T(8,128)(2,1)S(1)}, bf16[216,512]{1,0:T(8,128)(2,1)S(1)}, bf16[4,72,1152]{2,1,0:T(8,128)(2,1)S(1)}) custom-call(bf16[1152,512]{1,0:T(8,128)(2,1)S(1)} %shard_map.92.mod_ref, bf16[4,144,512]{2,1,0:T(8,128)(2,1)S(1)} %shard_map.93.half_ref, ...), custom_call_target="tpu_custom_call" | custom-call | flops 679477248 | bytes 6000000 | tf_op jit(solution)/shard_map/pallas_call | solution.py:25
  38.2 1.9 %collective-permute-start.10 = (bf16[216,512]{1,0:T(8,128)(2,1)S(1)}, bf16[216,512]{1,0:T(8,128)(2,1)S(1)}, u32[]{:S(2)}, u32[]{:S(2)}) collective-permute-start(bf16[216,512]{1,0:T(8,128)(2,1)S(1)} %get-tuple-element.25), channel_id=1, source_target_pairs={{0,6},{2,0},{4,2},{6,4},{1,7},{3,1},{5,3},{7,5},{8,14},{10,8},{12,... | collective-permute-start | bytes 663560 | tf_op jit(solution)/shard_map/ppermute | solution.py:253
  40.1 3.4 %collective-permute-start.8 = (bf16[216,512]{1,0:T(8,128)(2,1)S(1)}, bf16[216,512]{1,0:T(8,128)(2,1)S(1)}, u32[]{:S(2)}, u32[]{:S(2)}) collective-permute-start(bf16[216,512]{1,0:T(8,128)(2,1)S(1)} %get-tuple-element.23), channel_id=1, source_target_pairs={{0,2},{2,4},{4,6},{6,0},{1,3},{3,5},{5,7},{7,1},{8,10},{10,12},{12... | collective-permute-start | bytes 663560 | tf_op jit(solution)/shard_map/ppermute | solution.py:253
  43.5 1.9 %collective-permute-start.9 = (bf16[216,512]{1,0:T(8,128)(2,1)S(1)}, bf16[216,512]{1,0:T(8,128)(2,1)S(1)}, u32[]{:S(2)}, u32[]{:S(2)}) collective-permute-start(bf16[216,512]{1,0:T(8,128)(2,1)S(1)} %get-tuple-element.24), channel_id=1, source_target_pairs={{0,4},{2,6},{4,0},{6,2},{1,5},{3,7},{5,1},{7,3},{8,12},{10,14},{12... | collective-permute-start | bytes 663560 | tf_op jit(solution)/shard_map/ppermute | solution.py:253
  45.4 4.2 %collective-permute-start.11 = (bf16[4,72,1152]{2,1,0:T(8,128)(2,1)S(1)}, bf16[4,72,1152]{2,1,0:T(8,128)(2,1)S(1)}, u32[]{:S(2)}, u32[]{:S(2)}) collective-permute-start(bf16[4,72,1152]{2,1,0:T(8,128)(2,1)S(1)} %get-tuple-element.26), channel_id=1, source_target_pairs={{0,17},{17,0},{1,16},{16,1},{2,19},{19,2},{3,18},{18,3},{4,21},{21... | collective-permute-start | bytes 1990664 | tf_op jit(solution)/shard_map/ppermute | solution.py:283
  49.6 5.6 %collective-permute-done.8.q1_ref = bf16[216,512]{1,0:T(8,128)(2,1)S(1)} collective-permute-done((bf16[216,512]{1,0:T(8,128)(2,1)S(1)}, bf16[216,512]{1,0:T(8,128)(2,1)S(1)}, u32[]{:S(2)}, u32[]{:S(2)}) %collective-permute-start.8) | collective-permute-done | bytes 221216 | tf_op jit(solution)/shard_map/ppermute | solution.py:253
  55.2 6.0 %shard_map.95 = bf16[8,72,256]{2,1,0:T(8,128)(2,1)} custom-call(bf16[216,512]{1,0:T(8,128)(2,1)S(1)} %get-tuple-element.22.q0_ref, bf16[216,512]{1,0:T(8,128)(2,1)S(1)} %collective-permute-done.8.q1_ref, bf16[216,512]{1,0:T(8,128)(2,1)S(1)} %collective-permute-done.9.q2_ref, bf16[216,512]{1,0:T(8,128)(2,1)S(1)} %collective-permute-done.10.q3_ref), custom_call_target="tpu_custom_call" | custom-call | flops 2147483648 | bytes 1500000 | tf_op jit(solution)/shard_map/pallas_call | solution.py:25
  61.2 12.9 %all_to_all.5 = bf16[8,72,256]{2,1,0:T(8,128)(2,1)S(1)} all-to-all(bf16[8,72,256]{2,1,0:T(8,128)(2,1)} %shard_map.95), channel_id=1, replica_groups=mesh['z'=16,'ylo'=2,'core'=2,'x'=4,'yhi'=2] {'yhi','x'}, dimensions={0} | all-to-all | bytes 589824 | tf_op jit(solution)/shard_map/all_to_all | solution.py:295
  74.2 0.9 shard_map.97
  75.1 4.6 %collective-permute-start.12 = (bf16[32,1152]{1,0:T(8,128)(2,1)S(1)}, bf16[32,1152]{1,0:T(8,128)(2,1)S(1)}, u32[]{:S(2)}, u32[]{:S(2)}) collective-permute-start(bf16[32,1152]{1,0:T(8,128)(2,1)S(1)} %get-tuple-element.27.b_ref), channel_id=1, source_target_pairs={{0,504},{8,16},{16,8},{24,32},{32,24},{40,48},{48,40},{56,64},{64,... | collective-permute-start | bytes 221192 | tf_op jit(solution)/shard_map/ppermute | solution.py:305
  79.6 9.0 %collective-permute-start.13 = (bf16[32,1152]{1,0:T(8,128)(2,1)S(1)}, bf16[32,1152]{1,0:T(8,128)(2,1)S(1)}, u32[]{:S(2)}, u32[]{:S(2)}) collective-permute-start(bf16[32,1152]{1,0:T(8,128)(2,1)S(1)} %get-tuple-element.28.a_ref), channel_id=1, source_target_pairs={{0,8},{8,0},{16,24},{24,16},{32,40},{40,32},{48,56},{56,48},{64,72... | collective-permute-start | bytes 221192 | tf_op jit(solution)/shard_map/ppermute | solution.py:306
  88.6 0.1 copy.10.bw_ref
  88.7 0.9 shard_map.96.lay_ref
  89.6 1.2 %shard_map.98 = bf16[256,1152]{1,0:T(8,128)(2,1)} custom-call(bf16[256,1152]{1,0:T(8,128)(2,1)S(1)} %shard_map.96.lay_ref, bf16[32,1152]{1,0:T(8,128)(2,1)S(1)} %get-tuple-element.27.b_ref, bf16[32,1152]{1,0:T(8,128)(2,1)S(1)} %get-tuple-element.28.a_ref, bf16[32,1152]{1,0:T(8,128)(2,1)S(1)} %collective-permute-done.12.rb_ref, ...), custom_call_target="tpu_custom_call" | custom-call | flops 37748736 | bytes 1500000 | tf_op jit(solution)/shard_map/pallas_call | solution.py:25
  (20 shorter events, 0.0 us)
Async XLA Ops:
  0.0 32.6 %copy-start = (bf16[1,256,1152]{2,1,0:T(8,128)(2,1)S(1)}, bf16[1,256,1152]{2,1,0:T(8,128)(2,1)}, u32[]{:S(2)}) copy-start(bf16[1,256,1152]{2,1,0:T(8,128)(2,1)} %param.9) | copy-start | bytes 1769476
  1.1 19.3 %collective-permute-start.3 = (bf16[2,72,1152]{2,1,0:T(8,128)(2,1)S(1)}, bf16[2,72,1152]{2,1,0:T(8,128)(2,1)S(1)}, u32[]{:S(2)}, u32[]{:S(2)}) collective-permute-start(bf16[2,72,1152]{2,1,0:T(8,128)(2,1)S(1)} %shard_map.91.refs_4_), channel_id=1, source_target_pairs={{0,6},{2,0},{4,2},{6,4},{1,7},{3,1},{5,3},{7,5},{8,14},{10,8},{12,... | collective-permute-start | bytes 995336 | tf_op jit(solution)/shard_map/ppermute | solution.py:253
  6.3 16.0 %collective-permute-start.5 = (bf16[2,72,1152]{2,1,0:T(8,128)(2,1)S(1)}, bf16[2,72,1152]{2,1,0:T(8,128)(2,1)S(1)}, u32[]{:S(2)}, u32[]{:S(2)}) collective-permute-start(bf16[2,72,1152]{2,1,0:T(8,128)(2,1)S(1)} %shard_map.91.refs_4_), channel_id=1, source_target_pairs={{0,2},{2,4},{4,6},{6,0},{1,3},{3,5},{5,7},{7,1},{8,10},{10,12},{12... | collective-permute-start | bytes 995336 | tf_op jit(solution)/shard_map/ppermute | solution.py:253
  8.2 20.9 %collective-permute-start.1 = (bf16[256,1152]{1,0:T(8,128)(2,1)}, bf16[256,1152]{1,0:T(8,128)(2,1)S(1)}, u32[]{:S(2)}, u32[]{:S(2)}) collective-permute-start(bf16[256,1152]{1,0:T(8,128)(2,1)} %bitcast.14), channel_id=1, source_target_pairs={{0,1},{1,0},{2,3},{3,2},{4,5},{5,4},{6,7},{7,6},{8,9},{9,8},{10,11... | collective-permute-start | bytes 1769480 | tf_op jit(solution)/shard_map/ppermute | solution.py:238
  13.1 16.1 %collective-permute-start = (bf16[2,72,1152]{2,1,0:T(8,128)(2,1)S(1)}, bf16[2,72,1152]{2,1,0:T(8,128)(2,1)S(1)}, u32[]{:S(2)}, u32[]{:S(2)}) collective-permute-start(bf16[2,72,1152]{2,1,0:T(8,128)(2,1)S(1)} %shard_map.91.refs_4_), channel_id=1, source_target_pairs={{0,4},{2,6},{4,0},{6,2},{1,5},{3,7},{5,1},{7,3},{8,12},{10,14},{12... | collective-permute-start | bytes 995336 | tf_op jit(solution)/shard_map/ppermute | solution.py:253
  16.7 12.4 %collective-permute-start.2 = (bf16[2,72,1152]{2,1,0:T(8,128)(2,1)S(1)}, bf16[2,72,1152]{2,1,0:T(8,128)(2,1)S(1)}, u32[]{:S(2)}, u32[]{:S(2)}) collective-permute-start(bf16[2,72,1152]{2,1,0:T(8,128)(2,1)S(1)} %shard_map.91.refs_4_), channel_id=1, source_target_pairs={{0,8},{8,0},{1,9},{9,1},{2,10},{10,2},{3,11},{11,3},{4,12},{12,4},... | collective-permute-start | bytes 995336 | tf_op jit(solution)/shard_map/ppermute | solution.py:256
  20.4 8.7 %collective-permute-start.4 = (bf16[2,72,1152]{2,1,0:T(8,128)(2,1)S(1)}, bf16[2,72,1152]{2,1,0:T(8,128)(2,1)S(1)}, u32[]{:S(2)}, u32[]{:S(2)}) collective-permute-start(bf16[2,72,1152]{2,1,0:T(8,128)(2,1)S(1)} %collective-permute-done.3.refs_5_), channel_id=1, source_target_pairs={{0,8},{8,0},{1,9},{9,1},{2,10},{10,2},{3,11},{11,3},{4,12},{12,4},... | collective-permute-start | bytes 995336 | tf_op jit(solution)/shard_map/ppermute | solution.py:256
  22.4 8.0 %collective-permute-start.6 = (bf16[2,72,1152]{2,1,0:T(8,128)(2,1)S(1)}, bf16[2,72,1152]{2,1,0:T(8,128)(2,1)S(1)}, u32[]{:S(2)}, u32[]{:S(2)}) collective-permute-start(bf16[2,72,1152]{2,1,0:T(8,128)(2,1)S(1)} %collective-permute-done.5.refs_7_), channel_id=1, source_target_pairs={{0,8},{8,0},{1,9},{9,1},{2,10},{10,2},{3,11},{11,3},{4,12},{12,4},... | collective-permute-start | bytes 995336 | tf_op jit(solution)/shard_map/ppermute | solution.py:256
  30.4 5.7 %collective-permute-start.7 = (bf16[2,72,1152]{2,1,0:T(8,128)(2,1)S(1)}, bf16[2,72,1152]{2,1,0:T(8,128)(2,1)S(1)}, u32[]{:S(2)}, u32[]{:S(2)}) collective-permute-start(bf16[2,72,1152]{2,1,0:T(8,128)(2,1)S(1)} %collective-permute-done.refs_6_), channel_id=1, source_target_pairs={{0,8},{8,0},{1,9},{9,1},{2,10},{10,2},{3,11},{11,3},{4,12},{12,4},... | collective-permute-start | bytes 995336 | tf_op jit(solution)/shard_map/ppermute | solution.py:259
  32.7 0.7 copy-start.2
  33.3 0.7 copy-start.3
  38.2 11.4 %collective-permute-start.10 = (bf16[216,512]{1,0:T(8,128)(2,1)S(1)}, bf16[216,512]{1,0:T(8,128)(2,1)S(1)}, u32[]{:S(2)}, u32[]{:S(2)}) collective-permute-start(bf16[216,512]{1,0:T(8,128)(2,1)S(1)} %get-tuple-element.25), channel_id=1, source_target_pairs={{0,6},{2,0},{4,2},{6,4},{1,7},{3,1},{5,3},{7,5},{8,14},{10,8},{12,... | collective-permute-start | bytes 663560 | tf_op jit(solution)/shard_map/ppermute | solution.py:253
  40.1 15.0 %collective-permute-start.8 = (bf16[216,512]{1,0:T(8,128)(2,1)S(1)}, bf16[216,512]{1,0:T(8,128)(2,1)S(1)}, u32[]{:S(2)}, u32[]{:S(2)}) collective-permute-start(bf16[216,512]{1,0:T(8,128)(2,1)S(1)} %get-tuple-element.23), channel_id=1, source_target_pairs={{0,2},{2,4},{4,6},{6,0},{1,3},{3,5},{5,7},{7,1},{8,10},{10,12},{12... | collective-permute-start | bytes 663560 | tf_op jit(solution)/shard_map/ppermute | solution.py:253
  43.5 11.7 %collective-permute-start.9 = (bf16[216,512]{1,0:T(8,128)(2,1)S(1)}, bf16[216,512]{1,0:T(8,128)(2,1)S(1)}, u32[]{:S(2)}, u32[]{:S(2)}) collective-permute-start(bf16[216,512]{1,0:T(8,128)(2,1)S(1)} %get-tuple-element.24), channel_id=1, source_target_pairs={{0,4},{2,6},{4,0},{6,2},{1,5},{3,7},{5,1},{7,3},{8,12},{10,14},{12... | collective-permute-start | bytes 663560 | tf_op jit(solution)/shard_map/ppermute | solution.py:253
  45.4 28.7 %collective-permute-start.11 = (bf16[4,72,1152]{2,1,0:T(8,128)(2,1)S(1)}, bf16[4,72,1152]{2,1,0:T(8,128)(2,1)S(1)}, u32[]{:S(2)}, u32[]{:S(2)}) collective-permute-start(bf16[4,72,1152]{2,1,0:T(8,128)(2,1)S(1)} %get-tuple-element.26), channel_id=1, source_target_pairs={{0,17},{17,0},{1,16},{16,1},{2,19},{19,2},{3,18},{18,3},{4,21},{21... | collective-permute-start | bytes 1990664 | tf_op jit(solution)/shard_map/ppermute | solution.py:283
  55.2 19.0 %copy-start.1 = (f32[1,1152]{1,0:T(1,128)S(1)}, f32[1,1152]{1,0:T(1,128)}, u32[]{:S(2)}) copy-start(f32[1,1152]{1,0:T(1,128)} %gate_ref.3) | copy-start | bytes 13828
  55.2 19.0 %copy-start.4 = (s32[1,32]{1,0:T(1,128)S(1)}, s32[1,32]{1,0:T(1,128)}, u32[]{:S(2)}) copy-start(s32[1,32]{1,0:T(1,128)} %east_ref.3) | copy-start | bytes 388
  55.2 19.0 %copy-start.5 = (s32[1,32]{1,0:T(1,128)S(1)}, s32[1,32]{1,0:T(1,128)}, u32[]{:S(2)}) copy-start(s32[1,32]{1,0:T(1,128)} %west_ref.3) | copy-start | bytes 388
  74.1 14.5 %copy-start.6 = (s32[64,32]{0,1:T(8,128)S(1)}, s32[64,32]{0,1:T(8,128)}, u32[]{:S(2)}) copy-start(s32[64,32]{0,1:T(8,128)} %param.17) | copy-start | bytes 24580
  75.1 14.5 %collective-permute-start.12 = (bf16[32,1152]{1,0:T(8,128)(2,1)S(1)}, bf16[32,1152]{1,0:T(8,128)(2,1)S(1)}, u32[]{:S(2)}, u32[]{:S(2)}) collective-permute-start(bf16[32,1152]{1,0:T(8,128)(2,1)S(1)} %get-tuple-element.27.b_ref), channel_id=1, source_target_pairs={{0,504},{8,16},{16,8},{24,32},{32,24},{40,48},{48,40},{56,64},{64,... | collective-permute-start | bytes 221192 | tf_op jit(solution)/shard_map/ppermute | solution.py:305
  79.6 10.0 %collective-permute-start.13 = (bf16[32,1152]{1,0:T(8,128)(2,1)S(1)}, bf16[32,1152]{1,0:T(8,128)(2,1)S(1)}, u32[]{:S(2)}, u32[]{:S(2)}) collective-permute-start(bf16[32,1152]{1,0:T(8,128)(2,1)S(1)} %get-tuple-element.28.a_ref), channel_id=1, source_target_pairs={{0,8},{8,0},{16,24},{24,16},{32,40},{40,32},{48,56},{56,48},{64,72... | collective-permute-start | bytes 221192 | tf_op jit(solution)/shard_map/ppermute | solution.py:306

commit v5 on v2

--- a/solution.py
+++ b/solution.py
@@ -79,23 +79,25 @@
     out_ref[:, TOK:] = modulate(xo_ref, shift, scale).T.astype(BF)
 
 
-def qkv_kernel(mod_ref, mine_ref, other_ref, mine4_ref, other4_ref, out_ref, wo_ref, buf, sems, wsems):
+def half_kernel(mod_ref, w_ref, out_ref):
+    out_ref[...] = jnp.dot(w_ref[...], mod_ref[...], preferred_element_type=F32).astype(BF)
+
+
+def qkv_kernel(mod_ref, half_ref, other_ref, mine4_ref, other4_ref, out_ref, wo_ref, buf, sems, wsems):
     core = lax.axis_index("core")
 
-    def go(qk_ref, vo_ref, vo4_ref):
+    def go(vo4_ref, own_first):
         moves = [
             pltpu.make_async_copy(vo4_ref.at[h, 1], wo_ref.at[h], wsems.at[h]) for h in range(4)
         ]
         for move in moves:
             move.start()
-        mod = mod_ref[...]
-        qk = jnp.dot(qk_ref[...], mod, preferred_element_type=F32)
-        vo = jnp.dot(vo_ref[...], mod, preferred_element_type=F32)
+        other = jnp.dot(other_ref[...], mod_ref[...], preferred_element_type=F32)
         for h in range(4):
-            rows = jnp.concatenate(
-                [qk[2 * HD * h : 2 * HD * (h + 1)], vo[2 * HD * h : 2 * HD * h + HD]], axis=0
-            )
-            buf[h] = rows.astype(BF)
+            own = half_ref[2 * HD * h : 2 * HD * (h + 1)].astype(F32)
+            swapped = other[2 * HD * h : 2 * HD * (h + 1)]
+            qk, vo = (own, swapped) if own_first else (swapped, own)
+            buf[h] = jnp.concatenate([qk, vo[:HD]], axis=0).astype(BF)
             copy = pltpu.make_async_copy(buf.at[h], out_ref.at[h], sems.at[h])
             copy.start()
             moves.append(copy)
@@ -104,11 +106,11 @@
 
     @pl.when(core == 0)
     def _():
-        go(mine_ref, other_ref, other4_ref)
+        go(other4_ref, True)
 
     @pl.when(core == 1)
     def _():
-        go(other_ref, mine_ref, mine4_ref)
+        go(mine4_ref, False)
 
 
 def attention_kernel(qkv_ref, out_ref, buf, sems):
@@ -162,16 +164,10 @@
     return jnp.sum(jnp.where(eye, row.astype(F32), 0.0), axis=1, keepdims=True)
 
 
-def ordered(east_ref, west_ref):
-    first = lax.axis_index("core") == 0
-    east = east_ref[...]
-    west = west_ref[...]
-    return jnp.where(first, east, west), jnp.where(first, west, east)
-
-
 def select_rows(east_ref, west_ref):
-    a, b = ordered(east_ref, west_ref)
-    rows = jnp.concatenate([column(a), column(b)], axis=0).astype(jnp.int32)
+    e = column(east_ref[...])
+    w = column(west_ref[...])
+    rows = jnp.concatenate([e, w], axis=0).astype(jnp.int32)
     return jnp.where(
         lax.broadcasted_iota(jnp.int32, (2 * OV, TOK), 1) == rows, 1.0, 0.0
     ).astype(BF)
@@ -181,7 +177,7 @@
     return lax.dot_general(attn, wo, (((0,), (0,)), ((), ())), preferred_element_type=F32)
 
 
-def margin_kernel(attn_ref, wo_ref, wo2_ref, x_ref, gate_ref, east_ref, west_ref, a_ref, b_ref):
+def margin_kernel(attn_ref, wo_ref, wo2_ref, x_ref, gate_ref, east_ref, west_ref, w_ref, e_ref):
     yhi = lax.axis_index("yhi")
     pick = select_rows(east_ref, west_ref)
     nt = (((1,), (1,)), ((), ()))
@@ -192,8 +188,8 @@
         other, wo2_ref[...], preferred_element_type=F32
     )
     rows = (x + gate_ref[...] * proj).astype(BF)
-    a_ref[...] = rows[:OV]
-    b_ref[...] = rows[OV:]
+    w_ref[...] = rows[OV:]
+    e_ref[...] = rows[:OV]
 
 
 def out_kernel(attn_ref, wo_ref, wo2_ref, x_ref, gate_ref, out_ref):
@@ -202,18 +198,15 @@
     out_ref[...] = (x_ref[...].astype(F32) + gate_ref[...] * proj).astype(BF)
 
 
-def blend_kernel(lay_ref, a_ref, b_ref, ra_ref, rb_ref, east_ref, west_ref, bw_ref, out_ref):
-    core = lax.axis_index("core")
-    tile = lax.axis_index("z") * 4 + lax.axis_index("ylo") * 2 + core
+def blend_kernel(lay_ref, w_ref, e_ref, next_ref, prev_ref, east_ref, west_ref, bw_ref, out_ref):
+    tile = lax.axis_index("z") * 4 + lax.axis_index("ylo") * 2 + lax.axis_index("core")
     prior = jnp.where(tile == 0, 63, tile - 1)
-    east = column(bw_ref[pl.ds(tile, 1), :])
-    west = 8.0 - column(bw_ref[pl.ds(prior, 1), :])
-    own_a = jnp.where(core == 0, east, west)
-    own_b = jnp.where(core == 0, west, east)
-    new_a = (own_a * a_ref[...].astype(F32) + (8.0 - own_a) * ra_ref[...].astype(F32)) / 8.0
-    new_b = (own_b * b_ref[...].astype(F32) + (8.0 - own_b) * rb_ref[...].astype(F32)) / 8.0
-    new = jnp.concatenate([new_a, new_b], axis=0).astype(BF)
-    index = jnp.concatenate(ordered(east_ref, west_ref), axis=1)
+    a_e = column(bw_ref[pl.ds(tile, 1), :])
+    a_w = column(bw_ref[pl.ds(prior, 1), :])
+    new_e = (a_e * e_ref[...].astype(F32) + (8.0 - a_e) * next_ref[...].astype(F32)) / 8.0
+    new_w = ((8.0 - a_w) * w_ref[...].astype(F32) + a_w * prev_ref[...].astype(F32)) / 8.0
+    new = jnp.concatenate([new_e, new_w], axis=0).astype(BF)
+    index = jnp.concatenate([east_ref[...], west_ref[...]], axis=1)
     hot = jnp.where(
         lax.broadcasted_iota(jnp.int32, (TOK, 2 * OV), 0) == index, 1.0, 0.0
     )
@@ -251,12 +244,19 @@
         20 * 512 * D,
         3000000,
     )
+    half = call(
+        half_kernel,
+        sds((8 * HD, 2 * TOK), BF),
+        (mod, mine.reshape(8 * HD, D)),
+        2 * 512 * 576 * D,
+        2500000,
+    )
     qkv, wo = call(
         qkv_kernel,
         (pltpu.HBM((4, 3 * HD, 2 * TOK), BF), sds((4, HD, D), BF)),
-        (mod, mine.reshape(8 * HD, D), other.reshape(8 * HD, D), mine, other),
-        2 * 512 * 1152 * D,
-        6000000,
+        (mod, half, other.reshape(8 * HD, D), mine, other),
+        2 * 512 * 576 * D,
+        5000000,
         out_specs=(HBM, VMEM),
         scratch=[pltpu.VMEM((4, 3 * HD, 2 * TOK), BF), dma((4,)), dma((4,))],
     )
@@ -276,15 +276,15 @@
     attn = lax.all_to_all(attn, ("yhi", "x"), 0, 0, tiled=True).reshape(2, 4 * HD, TOK)
     wo = wo.reshape(4 * HD, D)
     wo_other = wo_other.reshape(4 * HD, D)
-    a, b = call(
+    own_w, own_e = call(
         margin_kernel,
         (sds((OV, D), BF), sds((OV, D), BF)),
         (attn, wo, wo_other, x, mod_gate, east_rows, west_rows),
         2 * 64 * 576 * D,
         2000000,
     )
-    other_b = lax.ppermute(b, TILE, [(i, (i + 2 * (i % 2) - 1) % 64) for i in range(64)])
-    other_a = lax.ppermute(a, TILE, [(i, i + 1 - 2 * (i % 2)) for i in range(64)])
+    next_w = lax.ppermute(own_w, TILE, [(i, (i - 1) % 64) for i in range(64)])
+    prev_e = lax.ppermute(own_e, TILE, [(i, (i + 1) % 64) for i in range(64)])
     lay = call(
         out_kernel,
         sds((TOK, D), BF),
@@ -295,7 +295,7 @@
     out = call(
         blend_kernel,
         sds((TOK, D), BF),
-        (lay, a, b, other_a, other_b, east_rows, west_rows, blend_weight),
+        (lay, own_w, own_e, next_w, prev_e, east_rows, west_rows, blend_weight),
         2 * 256 * 64 * D,
         1500000,
     )

time: 89 us -> 89.1 us (level)
  waiting for transfers between devices: 29.3 us -> 32.2 us
  starting transfers between devices: 43.3 us -> 40.4 us
    ppermute x2, waiting for transfers between devices: 1.06 us -> 4.89 us  [the longest x1 4.89 us: body(): prev_e = lax.ppermute(own_e, TILE, [(i, (i + 1) % 64) for i in range(64)])]
    ppermute x2, starting transfers between devices: 13.5 us -> 10.7 us  [the longest x1 8.73 us: body(): next_w = lax.ppermute(own_w, TILE, [(i, (i - 1) % 64) for i in range(64)])]
    ppermute x1, waiting for transfers between devices: 1.97 us -> 1.04 us  [body(): other = lax.ppermute(mine, 'core', swap)]
    pallas_call x7 -> x8, Pallas kernels: 15.5 us -> 15.6 us  [call(): pl.pallas_call(kernel, out_shape=outs, in_specs=ins or [VMEM] * len(args)...]
  transfers between devices with their start and end apart: 8 -> 8, of which waited for: 5 -> 5; matrix products, arithmetic and copies ran while one was open for 0% -> 0% of each run, Pallas kernels for 9% -> 10%
where the time goes in v5:
time: 89.1 us; the launch traced here: 88.6 us
  starting transfers between devices  40.4 us (45%)
  waiting for transfers between devices  32.2 us (36%)
  Pallas kernels  15.6 us (18%)
    pallas_call x8, Pallas kernels, call(): pl.pallas_call(kernel, out_shape=outs, in_specs=ins or [VMEM] * len(args)...  15.6 us
    ppermute x1, waiting for transfers between devices, body(): x_other = lax.ppermute(x, 'yhi', swap)  11.4 us
    all_to_all x1, starting transfers between devices, body(): mine = lax.all_to_all(packed, 'x', 0, 0, tiled=True)  9.56 us
    ppermute x1, starting transfers between devices, body(): next_w = lax.ppermute(own_w, TILE, [(i, (i - 1) % 64) for i in range(64)])  8.73 us
    all_to_all x1, waiting for transfers between devices, body(): lax.all_to_all(attn, ('yhi', 'x'), 0, 0, tiled=True).reshape(2, 4 * HD, TOK)  7.8 us
    all_to_all x1, waiting for transfers between devices, body(): qkv = lax.all_to_all(qkv, 'x', 0, 0, tiled=True)  7.13 us
    all_to_all x1, starting transfers between devices, body(): lax.all_to_all(attn, ('yhi', 'x'), 0, 0, tiled=True).reshape(2, 4 * HD, TOK)  6.54 us
    ppermute x1, starting transfers between devices, body(): wo_other = lax.ppermute(wo, ('ylo', 'yhi'), pairs)  5.04 us
  transfers between devices with their start and end apart: 8, of which 5 were waited for; matrix products, arithmetic and copies ran while one was open for 0% of the time, Pallas kernels for 10%

profile of v5, /device:TPU:2, one launch (start us, length us, event | category | flops | bytes accessed | tf_op | source)
XLA Modules:
  0.0 88.6 jit_solution(14648125100881092042)
XLA Ops:
  0.0 2.1 %shard_map.91 = bf16[4,2,72,1152]{3,2,1,0:T(8,128)(2,1)} custom-call(bf16[3,72,1152]{2,1,0:T(8,128)(2,1)} %bitcast.20, bf16[72,1152]{1,0:T(8,128)(2,1)} %wo_ref.1), custom_call_target="tpu_custom_call" | custom-call | flops 1000 | bytes 2000000 | tf_op jit(solution)/shard_map/pallas_call | solution.py:25
  2.1 0.0 copy-start
  2.1 0.0 copy-start.2
  2.1 0.0 copy-start.3
  2.1 9.6 %all-to-all-start = ((bf16[4,2,72,1152]{3,2,1,0:T(8,128)(2,1)}), bf16[4,2,72,1152]{3,2,1,0:T(8,128)(2,1)S(1)}, u32[]{:S(2)}, u32[]{:S(2)}) async-start(bf16[4,2,72,1152]{3,2,1,0:T(8,128)(2,1)} %shard_map.91), calls=%async_computation | async-start | bytes 2654208 | tf_op jit(solution)/shard_map/all_to_all | solution.py:237
  11.7 0.0 copy-done
  11.7 1.9 %collective-permute-start = (bf16[256,1152]{1,0:T(8,128)(2,1)S(1)}, bf16[256,1152]{1,0:T(8,128)(2,1)S(1)}, u32[]{:S(2)}, u32[]{:S(2)}) collective-permute-start(bf16[256,1152]{1,0:T(8,128)(2,1)S(1)} %bitcast.9), channel_id=1, source_target_pairs={{0,1},{1,0},{2,3},{3,2},{4,5},{5,4},{6,7},{7,6},{8,9},{9,8},{10,11... | collective-permute-start | bytes 1769480 | tf_op jit(solution)/shard_map/ppermute | solution.py:223
  13.6 11.4 %collective-permute-done.xo_ref = bf16[256,1152]{1,0:T(8,128)(2,1)S(1)} collective-permute-done((bf16[256,1152]{1,0:T(8,128)(2,1)S(1)}, bf16[256,1152]{1,0:T(8,128)(2,1)S(1)}, u32[]{:S(2)}, u32[]{:S(2)}) %collective-permute-start) | collective-permute-done | bytes 589856 | tf_op jit(solution)/shard_map/ppermute | solution.py:223
  25.0 0.0 all-to-all-done.mine4_ref
  25.0 1.9 %collective-permute-start.1 = (bf16[4,2,72,1152]{3,2,1,0:T(8,128)(2,1)S(1)}, bf16[4,2,72,1152]{3,2,1,0:T(8,128)(2,1)S(1)}, u32[]{:S(2)}, u32[]{:S(2)}) collective-permute-start(bf16[4,2,72,1152]{3,2,1,0:T(8,128)(2,1)S(1)} %all-to-all-done.mine4_ref), channel_id=1, source_target_pairs={{0,8},{8,0},{1,9},{9,1},{2,10},{10,2},{3,11},{11,3},{4,12},{12,4},... | collective-permute-start | bytes 3981320 | tf_op jit(solution)/shard_map/ppermute | solution.py:239
  26.9 0.0 copy-done.2
  26.9 1.0 %shard_map.92.mod_ref = bf16[1152,512]{1,0:T(8,128)(2,1)S(1)} custom-call(bf16[256,1152]{1,0:T(8,128)(2,1)S(1)} %bitcast.10, bf16[256,1152]{1,0:T(8,128)(2,1)S(1)} %collective-permute-done.xo_ref, f32[1,1152]{1,0:T(1,128)S(1)} %copy-done.2, f32[1,1152]{1,0:T(1,128)S(1)} %copy-done.3), custom_call_target="tpu_custom_call" | custom-call | flops 11796480 | bytes 3000000 | tf_op jit(solution)/shard_map/pallas_call | solution.py:25
  28.0 0.9 %shard_map.93.half_ref = bf16[576,512]{1,0:T(8,128)(2,1)S(1)} custom-call(bf16[1152,512]{1,0:T(8,128)(2,1)S(1)} %shard_map.92.mod_ref, bf16[576,1152]{1,0:T(8,128)(2,1)S(1)} %bitcast.8), custom_call_target="tpu_custom_call" | custom-call | flops 679477248 | bytes 2500000 | tf_op jit(solution)/shard_map/pallas_call | solution.py:25
  28.9 1.0 %collective-permute-done.1.other4_ref = bf16[4,2,72,1152]{3,2,1,0:T(8,128)(2,1)S(1)} collective-permute-done((bf16[4,2,72,1152]{3,2,1,0:T(8,128)(2,1)S(1)}, bf16[4,2,72,1152]{3,2,1,0:T(8,128)(2,1)S(1)}, u32[]{:S(2)}, u32[]{:S(2)}) %collective-permute-start.1) | collective-permute-done | bytes 1327136 | tf_op jit(solution)/shard_map/ppermute | solution.py:239
  29.9 2.6 %shard_map.94 = (bf16[4,216,512]{2,1,0:T(8,128)(2,1)}, bf16[4,72,1152]{2,1,0:T(8,128)(2,1)S(1)}) custom-call(bf16[1152,512]{1,0:T(8,128)(2,1)S(1)} %shard_map.92.mod_ref, bf16[576,512]{1,0:T(8,128)(2,1)S(1)} %shard_map.93.half_ref, bf16[576,1152]{1,0:T(8,128)(2,1)S(1)} %bitcast.13, bf16[4,2,72,1152]{3,2,1,0:T(8,128)(2,1)S(1)} %all-to-all-done.mine4_ref, ...), custom_call_target="tpu_custom_call" | custom-call | flops 679477248 | bytes 5000000 | tf_op jit(solution)/shard_map/pallas_call | solution.py:25
  32.5 4.8 %all-to-all-start.1 = ((bf16[4,216,512]{2,1,0:T(8,128)(2,1)}), bf16[4,216,512]{2,1,0:T(8,128)(2,1)S(1)}, u32[]{:S(2)}, u32[]{:S(2)}) async-start(bf16[4,216,512]{2,1,0:T(8,128)(2,1)} %get-tuple-element.13), calls=%async_computation.1 | async-start | bytes 1769472 | tf_op jit(solution)/shard_map/all_to_all | solution.py:265
  37.4 5.0 %collective-permute-start.2 = (bf16[4,72,1152]{2,1,0:T(8,128)(2,1)S(1)}, bf16[4,72,1152]{2,1,0:T(8,128)(2,1)S(1)}, u32[]{:S(2)}, u32[]{:S(2)}) collective-permute-start(bf16[4,72,1152]{2,1,0:T(8,128)(2,1)S(1)} %get-tuple-element.14), channel_id=1, source_target_pairs={{0,17},{17,0},{1,16},{16,1},{2,19},{19,2},{3,18},{18,3},{4,21},{21... | collective-permute-start | bytes 1990664 | tf_op jit(solution)/shard_map/ppermute | solution.py:264
  42.4 7.1 %all-to-all-done.1.qkv_ref = bf16[4,216,512]{2,1,0:T(8,128)(2,1)S(1)} async-done(((bf16[4,216,512]{2,1,0:T(8,128)(2,1)}), bf16[4,216,512]{2,1,0:T(8,128)(2,1)S(1)}, u32[]{:S(2)}, u32[]{:S(2)}) %all-to-all-start.1) | async-done | bytes 884768 | tf_op jit(solution)/shard_map/all_to_all | solution.py:265
  49.5 6.0 %shard_map.95 = bf16[8,72,256]{2,1,0:T(8,128)(2,1)} custom-call(bf16[4,216,512]{2,1,0:T(8,128)(2,1)S(1)} %all-to-all-done.1.qkv_ref), custom_call_target="tpu_custom_call" | custom-call | flops 2147483648 | bytes 1500000 | tf_op jit(solution)/shard_map/pallas_call | solution.py:25
  55.6 0.0 copy-start.6
  55.6 6.5 %all-to-all-start.2 = ((bf16[8,72,256]{2,1,0:T(8,128)(2,1)}), bf16[8,72,256]{2,1,0:T(8,128)(2,1)S(1)}, u32[]{:S(2)}, u32[]{:S(2)}) async-start(bf16[8,72,256]{2,1,0:T(8,128)(2,1)} %shard_map.95), calls=%async_computation.2 | async-start | bytes 589824 | tf_op jit(solution)/shard_map/all_to_all | solution.py:276
  62.1 0.0 collective-permute-done.2
  62.1 7.8 %all-to-all-done.2 = bf16[8,72,256]{2,1,0:T(8,128)(2,1)S(1)} async-done(((bf16[8,72,256]{2,1,0:T(8,128)(2,1)}), bf16[8,72,256]{2,1,0:T(8,128)(2,1)S(1)}, u32[]{:S(2)}, u32[]{:S(2)}) %all-to-all-start.2) | async-done | bytes 294944 | tf_op jit(solution)/shard_map/all_to_all | solution.py:276
  69.9 0.0 copy-done.1
  69.9 0.9 %shard_map.97 = (bf16[32,1152]{1,0:T(8,128)(2,1)S(1)}, bf16[32,1152]{1,0:T(8,128)(2,1)S(1)}) custom-call(bf16[2,288,256]{2,1,0:T(8,128)(2,1)S(1)} %bitcast.14, bf16[288,1152]{1,0:T(8,128)(2,1)S(1)} %bitcast.16, bf16[288,1152]{1,0:T(8,128)(2,1)S(1)} %bitcast.18, bf16[256,1152]{1,0:T(8,128)(2,1)S(1)} %bitcast.11, f32[1,1152]{1,0:T(1,128)S(1)} %copy-done.1, ...), custom_call_target="tpu_custom_call" | custom-call | flops 84934656 | bytes 2000000 | tf_op jit(solution)/shard_map/pallas_call | solution.py:25
  70.8 8.7 %collective-permute-start.3 = (bf16[32,1152]{1,0:T(8,128)(2,1)S(1)}, bf16[32,1152]{1,0:T(8,128)(2,1)S(1)}, u32[]{:S(2)}, u32[]{:S(2)}) collective-permute-start(bf16[32,1152]{1,0:T(8,128)(2,1)S(1)} %get-tuple-element.15.w_ref), channel_id=1, source_target_pairs={{0,504},{8,0},{16,8},{24,16},{32,24},{40,32},{48,40},{56,48},{64,5... | collective-permute-start | bytes 221192 | tf_op jit(solution)/shard_map/ppermute | solution.py:286
  79.6 1.9 %collective-permute-start.4 = (bf16[32,1152]{1,0:T(8,128)(2,1)S(1)}, bf16[32,1152]{1,0:T(8,128)(2,1)S(1)}, u32[]{:S(2)}, u32[]{:S(2)}) collective-permute-start(bf16[32,1152]{1,0:T(8,128)(2,1)S(1)} %get-tuple-element.16.e_ref), channel_id=1, source_target_pairs={{0,8},{8,16},{16,24},{24,32},{32,40},{40,48},{48,56},{56,64},{64,7... | collective-permute-start | bytes 221192 | tf_op jit(solution)/shard_map/ppermute | solution.py:287
  81.5 0.1 copy.10.bw_ref
  81.6 0.9 shard_map.96.lay_ref
  82.5 0.0 collective-permute-done.3.next_ref
  82.5 4.9 %collective-permute-done.4.prev_ref = bf16[32,1152]{1,0:T(8,128)(2,1)S(1)} collective-permute-done((bf16[32,1152]{1,0:T(8,128)(2,1)S(1)}, bf16[32,1152]{1,0:T(8,128)(2,1)S(1)}, u32[]{:S(2)}, u32[]{:S(2)}) %collective-permute-start.4) | collective-permute-done | bytes 73760 | tf_op jit(solution)/shard_map/ppermute | solution.py:287
  87.4 1.2 %shard_map.98 = bf16[256,1152]{1,0:T(8,128)(2,1)} custom-call(bf16[256,1152]{1,0:T(8,128)(2,1)S(1)} %shard_map.96.lay_ref, bf16[32,1152]{1,0:T(8,128)(2,1)S(1)} %get-tuple-element.15.w_ref, bf16[32,1152]{1,0:T(8,128)(2,1)S(1)} %get-tuple-element.16.e_ref, bf16[32,1152]{1,0:T(8,128)(2,1)S(1)} %collective-permute-done.3.next_ref, ...), custom_call_target="tpu_custom_call" | custom-call | flops 37748736 | bytes 1500000 | tf_op jit(solution)/shard_map/pallas_call | solution.py:25
  (7 shorter events, 0.0 us)
Async XLA Ops:
  2.1 9.6 %copy-start = (bf16[1,256,1152]{2,1,0:T(8,128)(2,1)S(1)}, bf16[1,256,1152]{2,1,0:T(8,128)(2,1)}, u32[]{:S(2)}) copy-start(bf16[1,256,1152]{2,1,0:T(8,128)(2,1)} %param.9) | copy-start | bytes 1769476
  2.1 24.8 %copy-start.2 = (f32[1,1152]{1,0:T(1,128)S(1)}, f32[1,1152]{1,0:T(1,128)}, u32[]{:S(2)}) copy-start(f32[1,1152]{1,0:T(1,128)} %shift_ref.1) | copy-start | bytes 13828
  2.1 24.8 %copy-start.3 = (f32[1,1152]{1,0:T(1,128)S(1)}, f32[1,1152]{1,0:T(1,128)}, u32[]{:S(2)}) copy-start(f32[1,1152]{1,0:T(1,128)} %scale_ref.1) | copy-start | bytes 13828
  2.1 22.9 %all-to-all-start = ((bf16[4,2,72,1152]{3,2,1,0:T(8,128)(2,1)}), bf16[4,2,72,1152]{3,2,1,0:T(8,128)(2,1)S(1)}, u32[]{:S(2)}, u32[]{:S(2)}) async-start(bf16[4,2,72,1152]{3,2,1,0:T(8,128)(2,1)} %shard_map.91), calls=%async_computation | async-start | bytes 2654208 | tf_op jit(solution)/shard_map/all_to_all | solution.py:237
  11.7 13.3 %collective-permute-start = (bf16[256,1152]{1,0:T(8,128)(2,1)S(1)}, bf16[256,1152]{1,0:T(8,128)(2,1)S(1)}, u32[]{:S(2)}, u32[]{:S(2)}) collective-permute-start(bf16[256,1152]{1,0:T(8,128)(2,1)S(1)} %bitcast.9), channel_id=1, source_target_pairs={{0,1},{1,0},{2,3},{3,2},{4,5},{5,4},{6,7},{7,6},{8,9},{9,8},{10,11... | collective-permute-start | bytes 1769480 | tf_op jit(solution)/shard_map/ppermute | solution.py:223
  25.0 4.9 %collective-permute-start.1 = (bf16[4,2,72,1152]{3,2,1,0:T(8,128)(2,1)S(1)}, bf16[4,2,72,1152]{3,2,1,0:T(8,128)(2,1)S(1)}, u32[]{:S(2)}, u32[]{:S(2)}) collective-permute-start(bf16[4,2,72,1152]{3,2,1,0:T(8,128)(2,1)S(1)} %all-to-all-done.mine4_ref), channel_id=1, source_target_pairs={{0,8},{8,0},{1,9},{9,1},{2,10},{10,2},{3,11},{11,3},{4,12},{12,4},... | collective-permute-start | bytes 3981320 | tf_op jit(solution)/shard_map/ppermute | solution.py:239
  32.5 17.0 %all-to-all-start.1 = ((bf16[4,216,512]{2,1,0:T(8,128)(2,1)}), bf16[4,216,512]{2,1,0:T(8,128)(2,1)S(1)}, u32[]{:S(2)}, u32[]{:S(2)}) async-start(bf16[4,216,512]{2,1,0:T(8,128)(2,1)} %get-tuple-element.13), calls=%async_computation.1 | async-start | bytes 1769472 | tf_op jit(solution)/shard_map/all_to_all | solution.py:265
  37.4 32.6 %copy-start.1 = (f32[1,1152]{1,0:T(1,128)S(1)}, f32[1,1152]{1,0:T(1,128)}, u32[]{:S(2)}) copy-start(f32[1,1152]{1,0:T(1,128)} %gate_ref.3) | copy-start | bytes 13828
  37.4 32.6 %copy-start.4 = (s32[1,32]{1,0:T(1,128)S(1)}, s32[1,32]{1,0:T(1,128)}, u32[]{:S(2)}) copy-start(s32[1,32]{1,0:T(1,128)} %east_ref.3) | copy-start | bytes 388
  37.4 32.6 %copy-start.5 = (s32[1,32]{1,0:T(1,128)S(1)}, s32[1,32]{1,0:T(1,128)}, u32[]{:S(2)}) copy-start(s32[1,32]{1,0:T(1,128)} %west_ref.3) | copy-start | bytes 388
  37.4 24.8 %collective-permute-start.2 = (bf16[4,72,1152]{2,1,0:T(8,128)(2,1)S(1)}, bf16[4,72,1152]{2,1,0:T(8,128)(2,1)S(1)}, u32[]{:S(2)}, u32[]{:S(2)}) collective-permute-start(bf16[4,72,1152]{2,1,0:T(8,128)(2,1)S(1)} %get-tuple-element.14), channel_id=1, source_target_pairs={{0,17},{17,0},{1,16},{16,1},{2,19},{19,2},{3,18},{18,3},{4,21},{21... | collective-permute-start | bytes 1990664 | tf_op jit(solution)/shard_map/ppermute | solution.py:264
  55.6 25.9 %copy-start.6 = (s32[64,32]{0,1:T(8,128)S(1)}, s32[64,32]{0,1:T(8,128)}, u32[]{:S(2)}) copy-start(s32[64,32]{0,1:T(8,128)} %param.17) | copy-start | bytes 24580
  55.6 14.3 %all-to-all-start.2 = ((bf16[8,72,256]{2,1,0:T(8,128)(2,1)}), bf16[8,72,256]{2,1,0:T(8,128)(2,1)S(1)}, u32[]{:S(2)}, u32[]{:S(2)}) async-start(bf16[8,72,256]{2,1,0:T(8,128)(2,1)} %shard_map.95), calls=%async_computation.2 | async-start | bytes 589824 | tf_op jit(solution)/shard_map/all_to_all | solution.py:276
  70.8 11.6 %collective-permute-start.3 = (bf16[32,1152]{1,0:T(8,128)(2,1)S(1)}, bf16[32,1152]{1,0:T(8,128)(2,1)S(1)}, u32[]{:S(2)}, u32[]{:S(2)}) collective-permute-start(bf16[32,1152]{1,0:T(8,128)(2,1)S(1)} %get-tuple-element.15.w_ref), channel_id=1, source_target_pairs={{0,504},{8,0},{16,8},{24,16},{32,24},{40,32},{48,40},{56,48},{64,5... | collective-permute-start | bytes 221192 | tf_op jit(solution)/shard_map/ppermute | solution.py:286
  79.6 7.8 %collective-permute-start.4 = (bf16[32,1152]{1,0:T(8,128)(2,1)S(1)}, bf16[32,1152]{1,0:T(8,128)(2,1)S(1)}, u32[]{:S(2)}, u32[]{:S(2)}) collective-permute-start(bf16[32,1152]{1,0:T(8,128)(2,1)S(1)} %get-tuple-element.16.e_ref), channel_id=1, source_target_pairs={{0,8},{8,16},{16,24},{24,32},{32,40},{40,48},{48,56},{56,64},{64,7... | collective-permute-start | bytes 221192 | tf_op jit(solution)/shard_map/ppermute | solution.py:287

commit v6 on v5

--- a/solution.py
+++ b/solution.py
@@ -92,10 +92,13 @@
         ]
         for move in moves:
             move.start()
-        other = jnp.dot(other_ref[...], mod_ref[...], preferred_element_type=F32)
+        mod = mod_ref[...]
         for h in range(4):
+            if h % 2 == 0:
+                rows = other_ref[2 * HD * h : 2 * HD * (h + 2)]
+                other = jnp.dot(rows, mod, preferred_element_type=F32)
             own = half_ref[2 * HD * h : 2 * HD * (h + 1)].astype(F32)
-            swapped = other[2 * HD * h : 2 * HD * (h + 1)]
+            swapped = other[2 * HD * (h % 2) : 2 * HD * (h % 2 + 1)]
             qk, vo = (own, swapped) if own_first else (swapped, own)
             buf[h] = jnp.concatenate([qk, vo[:HD]], axis=0).astype(BF)
             copy = pltpu.make_async_copy(buf.at[h], out_ref.at[h], sems.at[h])
@@ -177,7 +180,7 @@
     return lax.dot_general(attn, wo, (((0,), (0,)), ((), ())), preferred_element_type=F32)
 
 
-def margin_kernel(attn_ref, wo_ref, wo2_ref, x_ref, gate_ref, east_ref, west_ref, w_ref, e_ref):
+def margin_kernel(attn_ref, wo_ref, wo2_ref, x_ref, gate_ref, east_ref, west_ref, e_ref, w_ref):
     yhi = lax.axis_index("yhi")
     pick = select_rows(east_ref, west_ref)
     nt = (((1,), (1,)), ((), ()))
@@ -198,7 +201,7 @@
     out_ref[...] = (x_ref[...].astype(F32) + gate_ref[...] * proj).astype(BF)
 
 
-def blend_kernel(lay_ref, w_ref, e_ref, next_ref, prev_ref, east_ref, west_ref, bw_ref, out_ref):
+def blend_kernel(lay_ref, e_ref, w_ref, prev_ref, next_ref, east_ref, west_ref, bw_ref, out_ref):
     tile = lax.axis_index("z") * 4 + lax.axis_index("ylo") * 2 + lax.axis_index("core")
     prior = jnp.where(tile == 0, 63, tile - 1)
     a_e = column(bw_ref[pl.ds(tile, 1), :])
@@ -276,15 +279,15 @@
     attn = lax.all_to_all(attn, ("yhi", "x"), 0, 0, tiled=True).reshape(2, 4 * HD, TOK)
     wo = wo.reshape(4 * HD, D)
     wo_other = wo_other.reshape(4 * HD, D)
-    own_w, own_e = call(
+    own_e, own_w = call(
         margin_kernel,
         (sds((OV, D), BF), sds((OV, D), BF)),
         (attn, wo, wo_other, x, mod_gate, east_rows, west_rows),
         2 * 64 * 576 * D,
         2000000,
     )
+    prev_e = lax.ppermute(own_e, TILE, [(i, (i + 1) % 64) for i in range(64)])
     next_w = lax.ppermute(own_w, TILE, [(i, (i - 1) % 64) for i in range(64)])
-    prev_e = lax.ppermute(own_e, TILE, [(i, (i + 1) % 64) for i in range(64)])
     lay = call(
         out_kernel,
         sds((TOK, D), BF),
@@ -295,7 +298,7 @@
     out = call(
         blend_kernel,
         sds((TOK, D), BF),
-        (lay, own_w, own_e, next_w, prev_e, east_rows, west_rows, blend_weight),
+        (lay, own_e, own_w, prev_e, next_w, east_rows, west_rows, blend_weight),
         2 * 256 * 64 * D,
         1500000,
     )

time: 89.1 us -> 86.2 us (0.967)
  the two profiles are of different devices: /device:TPU:2 before, /device:TPU:105 now
where the time goes in v6:
time: 86.2 us; the launch traced here: 85.6 us
  waiting for transfers between devices  36.3 us (42%)
  starting transfers between devices  33.5 us (39%)
  Pallas kernels  15.6 us (18%)
    pallas_call x8, Pallas kernels, call(): pl.pallas_call(kernel, out_shape=outs, in_specs=ins or [VMEM] * len(args)...  15.6 us
    ppermute x1, waiting for transfers between devices, body(): x_other = lax.ppermute(x, 'yhi', swap)  13.3 us
    all_to_all x1, waiting for transfers between devices, body(): qkv = lax.all_to_all(qkv, 'x', 0, 0, tiled=True)  9.43 us
    ppermute x1, starting transfers between devices, body(): prev_e = lax.ppermute(own_e, TILE, [(i, (i + 1) % 64) for i in range(64)])  8.22 us
    all_to_all x1, waiting for transfers between devices, body(): lax.all_to_all(attn, ('yhi', 'x'), 0, 0, tiled=True).reshape(2, 4 * HD, TOK)  7.95 us
    ppermute x1, waiting for transfers between devices, body(): next_w = lax.ppermute(own_w, TILE, [(i, (i - 1) % 64) for i in range(64)])  4.89 us
    all_to_all x1, starting transfers between devices, body(): qkv = lax.all_to_all(qkv, 'x', 0, 0, tiled=True)  4.25 us
    all_to_all x1, starting transfers between devices, body(): mine = lax.all_to_all(packed, 'x', 0, 0, tiled=True)  4.16 us
  transfers between devices with their start and end apart: 8, of which 5 were waited for; matrix products, arithmetic and copies ran while one was open for 0% of the time, Pallas kernels for 10%

profile of v6, /device:TPU:105, one launch (start us, length us, event | category | flops | bytes accessed | tf_op | source)
XLA Modules:
  0.0 85.6 jit_solution(10524487280482907595)
XLA Ops:
  0.0 2.1 %shard_map.91 = bf16[4,2,72,1152]{3,2,1,0:T(8,128)(2,1)} custom-call(bf16[3,72,1152]{2,1,0:T(8,128)(2,1)} %bitcast.20, bf16[72,1152]{1,0:T(8,128)(2,1)} %wo_ref.1), custom_call_target="tpu_custom_call" | custom-call | flops 1000 | bytes 2000000 | tf_op jit(solution)/shard_map/pallas_call | solution.py:25
  2.1 0.0 copy-start
  2.1 0.0 copy-start.2
  2.1 0.0 copy-start.3
  2.1 4.2 %all-to-all-start = ((bf16[4,2,72,1152]{3,2,1,0:T(8,128)(2,1)}), bf16[4,2,72,1152]{3,2,1,0:T(8,128)(2,1)S(1)}, u32[]{:S(2)}, u32[]{:S(2)}) async-start(bf16[4,2,72,1152]{3,2,1,0:T(8,128)(2,1)} %shard_map.91), calls=%async_computation | async-start | bytes 2654208 | tf_op jit(solution)/shard_map/all_to_all | solution.py:240
  6.3 0.0 copy-done
  6.3 3.9 %collective-permute-start = (bf16[256,1152]{1,0:T(8,128)(2,1)S(1)}, bf16[256,1152]{1,0:T(8,128)(2,1)S(1)}, u32[]{:S(2)}, u32[]{:S(2)}) collective-permute-start(bf16[256,1152]{1,0:T(8,128)(2,1)S(1)} %bitcast.9), channel_id=1, source_target_pairs={{0,1},{1,0},{2,3},{3,2},{4,5},{5,4},{6,7},{7,6},{8,9},{9,8},{10,11... | collective-permute-start | bytes 1769480 | tf_op jit(solution)/shard_map/ppermute | solution.py:226
  10.2 13.3 %collective-permute-done.xo_ref = bf16[256,1152]{1,0:T(8,128)(2,1)S(1)} collective-permute-done((bf16[256,1152]{1,0:T(8,128)(2,1)S(1)}, bf16[256,1152]{1,0:T(8,128)(2,1)S(1)}, u32[]{:S(2)}, u32[]{:S(2)}) %collective-permute-start) | collective-permute-done | bytes 589856 | tf_op jit(solution)/shard_map/ppermute | solution.py:226
  23.6 0.0 all-to-all-done.mine4_ref
  23.6 3.8 %collective-permute-start.1 = (bf16[4,2,72,1152]{3,2,1,0:T(8,128)(2,1)S(1)}, bf16[4,2,72,1152]{3,2,1,0:T(8,128)(2,1)S(1)}, u32[]{:S(2)}, u32[]{:S(2)}) collective-permute-start(bf16[4,2,72,1152]{3,2,1,0:T(8,128)(2,1)S(1)} %all-to-all-done.mine4_ref), channel_id=1, source_target_pairs={{0,8},{8,0},{1,9},{9,1},{2,10},{10,2},{3,11},{11,3},{4,12},{12,4},... | collective-permute-start | bytes 3981320 | tf_op jit(solution)/shard_map/ppermute | solution.py:242
  27.3 0.0 copy-done.2
  27.4 1.0 %shard_map.92.mod_ref = bf16[1152,512]{1,0:T(8,128)(2,1)S(1)} custom-call(bf16[256,1152]{1,0:T(8,128)(2,1)S(1)} %bitcast.10, bf16[256,1152]{1,0:T(8,128)(2,1)S(1)} %collective-permute-done.xo_ref, f32[1,1152]{1,0:T(1,128)S(1)} %copy-done.2, f32[1,1152]{1,0:T(1,128)S(1)} %copy-done.3), custom_call_target="tpu_custom_call" | custom-call | flops 11796480 | bytes 3000000 | tf_op jit(solution)/shard_map/pallas_call | solution.py:25
  28.4 0.9 %shard_map.93.half_ref = bf16[576,512]{1,0:T(8,128)(2,1)S(1)} custom-call(bf16[1152,512]{1,0:T(8,128)(2,1)S(1)} %shard_map.92.mod_ref, bf16[576,1152]{1,0:T(8,128)(2,1)S(1)} %bitcast.8), custom_call_target="tpu_custom_call" | custom-call | flops 679477248 | bytes 2500000 | tf_op jit(solution)/shard_map/pallas_call | solution.py:25
  29.3 0.7 collective-permute-done.1.other4_ref
  30.0 2.5 %shard_map.94 = (bf16[4,216,512]{2,1,0:T(8,128)(2,1)}, bf16[4,72,1152]{2,1,0:T(8,128)(2,1)S(1)}) custom-call(bf16[1152,512]{1,0:T(8,128)(2,1)S(1)} %shard_map.92.mod_ref, bf16[576,512]{1,0:T(8,128)(2,1)S(1)} %shard_map.93.half_ref, bf16[576,1152]{1,0:T(8,128)(2,1)S(1)} %bitcast.13, bf16[4,2,72,1152]{3,2,1,0:T(8,128)(2,1)S(1)} %all-to-all-done.mine4_ref, ...), custom_call_target="tpu_custom_call" | custom-call | flops 679477248 | bytes 5000000 | tf_op jit(solution)/shard_map/pallas_call | solution.py:25
  32.5 4.2 %all-to-all-start.1 = ((bf16[4,216,512]{2,1,0:T(8,128)(2,1)}), bf16[4,216,512]{2,1,0:T(8,128)(2,1)S(1)}, u32[]{:S(2)}, u32[]{:S(2)}) async-start(bf16[4,216,512]{2,1,0:T(8,128)(2,1)} %get-tuple-element.13), calls=%async_computation.1 | async-start | bytes 1769472 | tf_op jit(solution)/shard_map/all_to_all | solution.py:268
  36.8 3.3 %collective-permute-start.2 = (bf16[4,72,1152]{2,1,0:T(8,128)(2,1)S(1)}, bf16[4,72,1152]{2,1,0:T(8,128)(2,1)S(1)}, u32[]{:S(2)}, u32[]{:S(2)}) collective-permute-start(bf16[4,72,1152]{2,1,0:T(8,128)(2,1)S(1)} %get-tuple-element.14), channel_id=1, source_target_pairs={{0,17},{17,0},{1,16},{16,1},{2,19},{19,2},{3,18},{18,3},{4,21},{21... | collective-permute-start | bytes 1990664 | tf_op jit(solution)/shard_map/ppermute | solution.py:267
  40.1 9.4 %all-to-all-done.1.qkv_ref = bf16[4,216,512]{2,1,0:T(8,128)(2,1)S(1)} async-done(((bf16[4,216,512]{2,1,0:T(8,128)(2,1)}), bf16[4,216,512]{2,1,0:T(8,128)(2,1)S(1)}, u32[]{:S(2)}, u32[]{:S(2)}) %all-to-all-start.1) | async-done | bytes 884768 | tf_op jit(solution)/shard_map/all_to_all | solution.py:268
  49.6 6.0 %shard_map.95 = bf16[8,72,256]{2,1,0:T(8,128)(2,1)} custom-call(bf16[4,216,512]{2,1,0:T(8,128)(2,1)S(1)} %all-to-all-done.1.qkv_ref), custom_call_target="tpu_custom_call" | custom-call | flops 2147483648 | bytes 1500000 | tf_op jit(solution)/shard_map/pallas_call | solution.py:25
  55.6 0.0 copy-start.6
  55.6 3.9 %all-to-all-start.2 = ((bf16[8,72,256]{2,1,0:T(8,128)(2,1)}), bf16[8,72,256]{2,1,0:T(8,128)(2,1)S(1)}, u32[]{:S(2)}, u32[]{:S(2)}) async-start(bf16[8,72,256]{2,1,0:T(8,128)(2,1)} %shard_map.95), calls=%async_computation.2 | async-start | bytes 589824 | tf_op jit(solution)/shard_map/all_to_all | solution.py:279
  59.5 0.0 collective-permute-done.2
  59.5 8.0 %all-to-all-done.2 = bf16[8,72,256]{2,1,0:T(8,128)(2,1)S(1)} async-done(((bf16[8,72,256]{2,1,0:T(8,128)(2,1)}), bf16[8,72,256]{2,1,0:T(8,128)(2,1)S(1)}, u32[]{:S(2)}, u32[]{:S(2)}) %all-to-all-start.2) | async-done | bytes 294944 | tf_op jit(solution)/shard_map/all_to_all | solution.py:279
  67.5 0.0 copy-done.5
  67.5 0.9 %shard_map.97 = (bf16[32,1152]{1,0:T(8,128)(2,1)S(1)}, bf16[32,1152]{1,0:T(8,128)(2,1)S(1)}) custom-call(bf16[2,288,256]{2,1,0:T(8,128)(2,1)S(1)} %bitcast.14, bf16[288,1152]{1,0:T(8,128)(2,1)S(1)} %bitcast.16, bf16[288,1152]{1,0:T(8,128)(2,1)S(1)} %bitcast.18, bf16[256,1152]{1,0:T(8,128)(2,1)S(1)} %bitcast.11, f32[1,1152]{1,0:T(1,128)S(1)} %copy-done.1, ...), custom_call_target="tpu_custom_call" | custom-call | flops 84934656 | bytes 2000000 | tf_op jit(solution)/shard_map/pallas_call | solution.py:25
  68.4 8.2 %collective-permute-start.3 = (bf16[32,1152]{1,0:T(8,128)(2,1)S(1)}, bf16[32,1152]{1,0:T(8,128)(2,1)S(1)}, u32[]{:S(2)}, u32[]{:S(2)}) collective-permute-start(bf16[32,1152]{1,0:T(8,128)(2,1)S(1)} %get-tuple-element.15.e_ref), channel_id=1, source_target_pairs={{0,8},{8,16},{16,24},{24,32},{32,40},{40,48},{48,56},{56,64},{64,7... | collective-permute-start | bytes 221192 | tf_op jit(solution)/shard_map/ppermute | solution.py:289
  76.6 1.9 %collective-permute-start.4 = (bf16[32,1152]{1,0:T(8,128)(2,1)S(1)}, bf16[32,1152]{1,0:T(8,128)(2,1)S(1)}, u32[]{:S(2)}, u32[]{:S(2)}) collective-permute-start(bf16[32,1152]{1,0:T(8,128)(2,1)S(1)} %get-tuple-element.16.w_ref), channel_id=1, source_target_pairs={{0,504},{8,0},{16,8},{24,16},{32,24},{40,32},{48,40},{56,48},{64,5... | collective-permute-start | bytes 221192 | tf_op jit(solution)/shard_map/ppermute | solution.py:290
  78.5 0.1 copy.10.bw_ref
  78.6 0.9 %shard_map.96.lay_ref = bf16[256,1152]{1,0:T(8,128)(2,1)S(1)} custom-call(bf16[2,288,256]{2,1,0:T(8,128)(2,1)S(1)} %bitcast.15, bf16[288,1152]{1,0:T(8,128)(2,1)S(1)} %bitcast.17, bf16[288,1152]{1,0:T(8,128)(2,1)S(1)} %bitcast.19, bf16[256,1152]{1,0:T(8,128)(2,1)S(1)} %bitcast.12, f32[1,1152]{1,0:T(1,128)S(1)} %copy-done.1), custom_call_target="tpu_custom_call" | custom-call | flops 339738624 | bytes 3000000 | tf_op jit(solution)/shard_map/pallas_call | solution.py:25
  79.5 0.0 collective-permute-done.3.prev_ref
  79.5 4.9 %collective-permute-done.4.next_ref = bf16[32,1152]{1,0:T(8,128)(2,1)S(1)} collective-permute-done((bf16[32,1152]{1,0:T(8,128)(2,1)S(1)}, bf16[32,1152]{1,0:T(8,128)(2,1)S(1)}, u32[]{:S(2)}, u32[]{:S(2)}) %collective-permute-start.4) | collective-permute-done | bytes 73760 | tf_op jit(solution)/shard_map/ppermute | solution.py:290
  84.4 1.2 %shard_map.98 = bf16[256,1152]{1,0:T(8,128)(2,1)} custom-call(bf16[256,1152]{1,0:T(8,128)(2,1)S(1)} %shard_map.96.lay_ref, bf16[32,1152]{1,0:T(8,128)(2,1)S(1)} %get-tuple-element.15.e_ref, bf16[32,1152]{1,0:T(8,128)(2,1)S(1)} %get-tuple-element.16.w_ref, bf16[32,1152]{1,0:T(8,128)(2,1)S(1)} %collective-permute-done.3.prev_ref, ...), custom_call_target="tpu_custom_call" | custom-call | flops 37748736 | bytes 1500000 | tf_op jit(solution)/shard_map/pallas_call | solution.py:25
  (7 shorter events, 0.0 us)
Async XLA Ops:
  2.1 4.2 %copy-start = (bf16[1,256,1152]{2,1,0:T(8,128)(2,1)S(1)}, bf16[1,256,1152]{2,1,0:T(8,128)(2,1)}, u32[]{:S(2)}) copy-start(bf16[1,256,1152]{2,1,0:T(8,128)(2,1)} %param.9) | copy-start | bytes 1769476
  2.1 25.2 %copy-start.2 = (f32[1,1152]{1,0:T(1,128)S(1)}, f32[1,1152]{1,0:T(1,128)}, u32[]{:S(2)}) copy-start(f32[1,1152]{1,0:T(1,128)} %shift_ref.1) | copy-start | bytes 13828
  2.1 25.2 %copy-start.3 = (f32[1,1152]{1,0:T(1,128)S(1)}, f32[1,1152]{1,0:T(1,128)}, u32[]{:S(2)}) copy-start(f32[1,1152]{1,0:T(1,128)} %scale_ref.1) | copy-start | bytes 13828
  2.1 21.4 %all-to-all-start = ((bf16[4,2,72,1152]{3,2,1,0:T(8,128)(2,1)}), bf16[4,2,72,1152]{3,2,1,0:T(8,128)(2,1)S(1)}, u32[]{:S(2)}, u32[]{:S(2)}) async-start(bf16[4,2,72,1152]{3,2,1,0:T(8,128)(2,1)} %shard_map.91), calls=%async_computation | async-start | bytes 2654208 | tf_op jit(solution)/shard_map/all_to_all | solution.py:240
  6.3 17.3 %collective-permute-start = (bf16[256,1152]{1,0:T(8,128)(2,1)S(1)}, bf16[256,1152]{1,0:T(8,128)(2,1)S(1)}, u32[]{:S(2)}, u32[]{:S(2)}) collective-permute-start(bf16[256,1152]{1,0:T(8,128)(2,1)S(1)} %bitcast.9), channel_id=1, source_target_pairs={{0,1},{1,0},{2,3},{3,2},{4,5},{5,4},{6,7},{7,6},{8,9},{9,8},{10,11... | collective-permute-start | bytes 1769480 | tf_op jit(solution)/shard_map/ppermute | solution.py:226
  23.6 6.4 %collective-permute-start.1 = (bf16[4,2,72,1152]{3,2,1,0:T(8,128)(2,1)S(1)}, bf16[4,2,72,1152]{3,2,1,0:T(8,128)(2,1)S(1)}, u32[]{:S(2)}, u32[]{:S(2)}) collective-permute-start(bf16[4,2,72,1152]{3,2,1,0:T(8,128)(2,1)S(1)} %all-to-all-done.mine4_ref), channel_id=1, source_target_pairs={{0,8},{8,0},{1,9},{9,1},{2,10},{10,2},{3,11},{11,3},{4,12},{12,4},... | collective-permute-start | bytes 3981320 | tf_op jit(solution)/shard_map/ppermute | solution.py:242
  32.5 17.0 %all-to-all-start.1 = ((bf16[4,216,512]{2,1,0:T(8,128)(2,1)}), bf16[4,216,512]{2,1,0:T(8,128)(2,1)S(1)}, u32[]{:S(2)}, u32[]{:S(2)}) async-start(bf16[4,216,512]{2,1,0:T(8,128)(2,1)} %get-tuple-element.13), calls=%async_computation.1 | async-start | bytes 1769472 | tf_op jit(solution)/shard_map/all_to_all | solution.py:268
  36.8 30.7 %copy-start.1 = (f32[1,1152]{1,0:T(1,128)S(1)}, f32[1,1152]{1,0:T(1,128)}, u32[]{:S(2)}) copy-start(f32[1,1152]{1,0:T(1,128)} %gate_ref.3) | copy-start | bytes 13828
  36.8 30.7 %copy-start.4 = (s32[1,32]{1,0:T(1,128)S(1)}, s32[1,32]{1,0:T(1,128)}, u32[]{:S(2)}) copy-start(s32[1,32]{1,0:T(1,128)} %east_ref.3) | copy-start | bytes 388
  36.8 30.7 %copy-start.5 = (s32[1,32]{1,0:T(1,128)S(1)}, s32[1,32]{1,0:T(1,128)}, u32[]{:S(2)}) copy-start(s32[1,32]{1,0:T(1,128)} %west_ref.3) | copy-start | bytes 388
  36.8 22.7 %collective-permute-start.2 = (bf16[4,72,1152]{2,1,0:T(8,128)(2,1)S(1)}, bf16[4,72,1152]{2,1,0:T(8,128)(2,1)S(1)}, u32[]{:S(2)}, u32[]{:S(2)}) collective-permute-start(bf16[4,72,1152]{2,1,0:T(8,128)(2,1)S(1)} %get-tuple-element.14), channel_id=1, source_target_pairs={{0,17},{17,0},{1,16},{16,1},{2,19},{19,2},{3,18},{18,3},{4,21},{21... | collective-permute-start | bytes 1990664 | tf_op jit(solution)/shard_map/ppermute | solution.py:267
  55.6 23.0 %copy-start.6 = (s32[64,32]{0,1:T(8,128)S(1)}, s32[64,32]{0,1:T(8,128)}, u32[]{:S(2)}) copy-start(s32[64,32]{0,1:T(8,128)} %param.17) | copy-start | bytes 24580
  55.6 11.9 %all-to-all-start.2 = ((bf16[8,72,256]{2,1,0:T(8,128)(2,1)}), bf16[8,72,256]{2,1,0:T(8,128)(2,1)S(1)}, u32[]{:S(2)}, u32[]{:S(2)}) async-start(bf16[8,72,256]{2,1,0:T(8,128)(2,1)} %shard_map.95), calls=%async_computation.2 | async-start | bytes 589824 | tf_op jit(solution)/shard_map/all_to_all | solution.py:279
  68.4 11.1 %collective-permute-start.3 = (bf16[32,1152]{1,0:T(8,128)(2,1)S(1)}, bf16[32,1152]{1,0:T(8,128)(2,1)S(1)}, u32[]{:S(2)}, u32[]{:S(2)}) collective-permute-start(bf16[32,1152]{1,0:T(8,128)(2,1)S(1)} %get-tuple-element.15.e_ref), channel_id=1, source_target_pairs={{0,8},{8,16},{16,24},{24,32},{32,40},{40,48},{48,56},{56,64},{64,7... | collective-permute-start | bytes 221192 | tf_op jit(solution)/shard_map/ppermute | solution.py:289
  76.6 7.8 %collective-permute-start.4 = (bf16[32,1152]{1,0:T(8,128)(2,1)S(1)}, bf16[32,1152]{1,0:T(8,128)(2,1)S(1)}, u32[]{:S(2)}, u32[]{:S(2)}) collective-permute-start(bf16[32,1152]{1,0:T(8,128)(2,1)S(1)} %get-tuple-element.16.w_ref), channel_id=1, source_target_pairs={{0,504},{8,0},{16,8},{24,16},{32,24},{40,32},{48,40},{56,48},{64,5... | collective-permute-start | bytes 221192 | tf_op jit(solution)/shard_map/ppermute | solution.py:290

commit v7 on v6

--- a/solution.py
+++ b/solution.py
@@ -130,31 +130,32 @@
         lo = q - hi
         k = block[HD : 2 * HD]
         both = jnp.concatenate([hi, lo], axis=0).astype(BF)
-        queries.append((both[:, :TOK], b, 0))
-        queries.append((both[:, TOK:], b, 1))
+        queries.append(both)
         kt = k.T.astype(BF)
         keys.append(jnp.concatenate([kt, kt], axis=1))
         values.append(jnp.concatenate([block[2 * HD :], ones], axis=0).astype(BF))
 
     def score(i):
-        return [jnp.dot(k, queries[i][0], preferred_element_type=F32) for k in keys]
+        return [jnp.dot(k, queries[i], preferred_element_type=F32) for k in keys]
 
     copies = []
     ahead = score(0)
-    for i in range(8):
+    for b in range(4):
         s = ahead
-        if i < 7:
-            ahead = score(i + 1)
+        if b < 3:
+            ahead = score(b + 1)
         peak = functools.reduce(jnp.maximum, [jnp.max(c, axis=0, keepdims=True) for c in s])
         o = sum(
             jnp.dot(v, jnp.exp2(c - peak).astype(BF), preferred_element_type=F32)
             for c, v in zip(s, values)
         )
-        _, b, half = queries[i]
-        slot = (yhi if half == 0 else 1 - yhi) * 4 + b
-        buf[i] = (o[:HD] / o[HD : HD + 1]).astype(BF)
-        copies.append(pltpu.make_async_copy(buf.at[i], out_ref.at[slot], sems.at[i]))
-        copies[-1].start()
+        res = (o[:HD] / o[HD : HD + 1]).astype(BF)
+        for half in range(2):
+            i = 2 * b + half
+            slot = (yhi if half == 0 else 1 - yhi) * 4 + b
+            buf[i] = res[:, half * TOK : (half + 1) * TOK]
+            copies.append(pltpu.make_async_copy(buf.at[i], out_ref.at[slot], sems.at[i]))
+            copies[-1].start()
     for copy in copies:
         copy.wait()
 

time: 86.2 us -> 86.7 us (level)
  transfers between devices with their start and end apart: 8 -> 8, of which waited for: 5 -> 5; matrix products, arithmetic and copies ran while one was open for 0% -> 0% of each run, Pallas kernels for 10% -> 11%
where the time goes in v7:
time: 86.7 us; the launch traced here: 86.2 us
  waiting for transfers between devices  36.3 us (42%)
  starting transfers between devices  33.5 us (39%)
  Pallas kernels  16.1 us (19%)
    pallas_call x8, Pallas kernels, call(): pl.pallas_call(kernel, out_shape=outs, in_specs=ins or [VMEM] * len(args)...  16.1 us
    ppermute x1, waiting for transfers between devices, body(): x_other = lax.ppermute(x, 'yhi', swap)  13.3 us
    all_to_all x1, waiting for transfers between devices, body(): qkv = lax.all_to_all(qkv, 'x', 0, 0, tiled=True)  9.43 us
    ppermute x1, starting transfers between devices, body(): prev_e = lax.ppermute(own_e, TILE, [(i, (i + 1) % 64) for i in range(64)])  8.2 us
    all_to_all x1, waiting for transfers between devices, body(): lax.all_to_all(attn, ('yhi', 'x'), 0, 0, tiled=True).reshape(2, 4 * HD, TOK)  7.97 us
    ppermute x1, waiting for transfers between devices, body(): next_w = lax.ppermute(own_w, TILE, [(i, (i - 1) % 64) for i in range(64)])  4.89 us
    all_to_all x1, starting transfers between devices, body(): qkv = lax.all_to_all(qkv, 'x', 0, 0, tiled=True)  4.25 us
    all_to_all x1, starting transfers between devices, body(): mine = lax.all_to_all(packed, 'x', 0, 0, tiled=True)  4.16 us
  transfers between devices with their start and end apart: 8, of which 5 were waited for; matrix products, arithmetic and copies ran while one was open for 0% of the time, Pallas kernels for 11%

profile of v7, /device:TPU:105, one launch (start us, length us, event | category | flops | bytes accessed | tf_op | source)
XLA Modules:
  0.0 86.2 jit_solution(13869532469206783692)
XLA Ops:
  0.0 2.1 %shard_map.91 = bf16[4,2,72,1152]{3,2,1,0:T(8,128)(2,1)} custom-call(bf16[3,72,1152]{2,1,0:T(8,128)(2,1)} %bitcast.20, bf16[72,1152]{1,0:T(8,128)(2,1)} %wo_ref.1), custom_call_target="tpu_custom_call" | custom-call | flops 1000 | bytes 2000000 | tf_op jit(solution)/shard_map/pallas_call | solution.py:25
  2.1 0.0 copy-start
  2.1 0.0 copy-start.2
  2.1 0.0 copy-start.3
  2.1 4.2 %all-to-all-start = ((bf16[4,2,72,1152]{3,2,1,0:T(8,128)(2,1)}), bf16[4,2,72,1152]{3,2,1,0:T(8,128)(2,1)S(1)}, u32[]{:S(2)}, u32[]{:S(2)}) async-start(bf16[4,2,72,1152]{3,2,1,0:T(8,128)(2,1)} %shard_map.91), calls=%async_computation | async-start | bytes 2654208 | tf_op jit(solution)/shard_map/all_to_all | solution.py:241
  6.3 0.0 copy-done
  6.3 3.9 %collective-permute-start = (bf16[256,1152]{1,0:T(8,128)(2,1)S(1)}, bf16[256,1152]{1,0:T(8,128)(2,1)S(1)}, u32[]{:S(2)}, u32[]{:S(2)}) collective-permute-start(bf16[256,1152]{1,0:T(8,128)(2,1)S(1)} %bitcast.9), channel_id=1, source_target_pairs={{0,1},{1,0},{2,3},{3,2},{4,5},{5,4},{6,7},{7,6},{8,9},{9,8},{10,11... | collective-permute-start | bytes 1769480 | tf_op jit(solution)/shard_map/ppermute | solution.py:227
  10.2 13.3 %collective-permute-done.xo_ref = bf16[256,1152]{1,0:T(8,128)(2,1)S(1)} collective-permute-done((bf16[256,1152]{1,0:T(8,128)(2,1)S(1)}, bf16[256,1152]{1,0:T(8,128)(2,1)S(1)}, u32[]{:S(2)}, u32[]{:S(2)}) %collective-permute-start) | collective-permute-done | bytes 589856 | tf_op jit(solution)/shard_map/ppermute | solution.py:227
  23.6 0.0 all-to-all-done.mine4_ref
  23.6 3.8 %collective-permute-start.1 = (bf16[4,2,72,1152]{3,2,1,0:T(8,128)(2,1)S(1)}, bf16[4,2,72,1152]{3,2,1,0:T(8,128)(2,1)S(1)}, u32[]{:S(2)}, u32[]{:S(2)}) collective-permute-start(bf16[4,2,72,1152]{3,2,1,0:T(8,128)(2,1)S(1)} %all-to-all-done.mine4_ref), channel_id=1, source_target_pairs={{0,8},{8,0},{1,9},{9,1},{2,10},{10,2},{3,11},{11,3},{4,12},{12,4},... | collective-permute-start | bytes 3981320 | tf_op jit(solution)/shard_map/ppermute | solution.py:243
  27.3 0.0 copy-done.2
  27.4 1.0 %shard_map.92.mod_ref = bf16[1152,512]{1,0:T(8,128)(2,1)S(1)} custom-call(bf16[256,1152]{1,0:T(8,128)(2,1)S(1)} %bitcast.10, bf16[256,1152]{1,0:T(8,128)(2,1)S(1)} %collective-permute-done.xo_ref, f32[1,1152]{1,0:T(1,128)S(1)} %copy-done.2, f32[1,1152]{1,0:T(1,128)S(1)} %copy-done.3), custom_call_target="tpu_custom_call" | custom-call | flops 11796480 | bytes 3000000 | tf_op jit(solution)/shard_map/pallas_call | solution.py:25
  28.4 0.9 %shard_map.93.half_ref = bf16[576,512]{1,0:T(8,128)(2,1)S(1)} custom-call(bf16[1152,512]{1,0:T(8,128)(2,1)S(1)} %shard_map.92.mod_ref, bf16[576,1152]{1,0:T(8,128)(2,1)S(1)} %bitcast.8), custom_call_target="tpu_custom_call" | custom-call | flops 679477248 | bytes 2500000 | tf_op jit(solution)/shard_map/pallas_call | solution.py:25
  29.3 0.7 collective-permute-done.1.other4_ref
  30.0 2.5 %shard_map.94 = (bf16[4,216,512]{2,1,0:T(8,128)(2,1)}, bf16[4,72,1152]{2,1,0:T(8,128)(2,1)S(1)}) custom-call(bf16[1152,512]{1,0:T(8,128)(2,1)S(1)} %shard_map.92.mod_ref, bf16[576,512]{1,0:T(8,128)(2,1)S(1)} %shard_map.93.half_ref, bf16[576,1152]{1,0:T(8,128)(2,1)S(1)} %bitcast.13, bf16[4,2,72,1152]{3,2,1,0:T(8,128)(2,1)S(1)} %all-to-all-done.mine4_ref, ...), custom_call_target="tpu_custom_call" | custom-call | flops 679477248 | bytes 5000000 | tf_op jit(solution)/shard_map/pallas_call | solution.py:25
  32.5 4.2 %all-to-all-start.1 = ((bf16[4,216,512]{2,1,0:T(8,128)(2,1)}), bf16[4,216,512]{2,1,0:T(8,128)(2,1)S(1)}, u32[]{:S(2)}, u32[]{:S(2)}) async-start(bf16[4,216,512]{2,1,0:T(8,128)(2,1)} %get-tuple-element.13), calls=%async_computation.1 | async-start | bytes 1769472 | tf_op jit(solution)/shard_map/all_to_all | solution.py:269
  36.8 3.3 %collective-permute-start.2 = (bf16[4,72,1152]{2,1,0:T(8,128)(2,1)S(1)}, bf16[4,72,1152]{2,1,0:T(8,128)(2,1)S(1)}, u32[]{:S(2)}, u32[]{:S(2)}) collective-permute-start(bf16[4,72,1152]{2,1,0:T(8,128)(2,1)S(1)} %get-tuple-element.14), channel_id=1, source_target_pairs={{0,17},{17,0},{1,16},{16,1},{2,19},{19,2},{3,18},{18,3},{4,21},{21... | collective-permute-start | bytes 1990664 | tf_op jit(solution)/shard_map/ppermute | solution.py:268
  40.1 9.4 %all-to-all-done.1.qkv_ref = bf16[4,216,512]{2,1,0:T(8,128)(2,1)S(1)} async-done(((bf16[4,216,512]{2,1,0:T(8,128)(2,1)}), bf16[4,216,512]{2,1,0:T(8,128)(2,1)S(1)}, u32[]{:S(2)}, u32[]{:S(2)}) %all-to-all-start.1) | async-done | bytes 884768 | tf_op jit(solution)/shard_map/all_to_all | solution.py:269
  49.6 6.6 %shard_map.95 = bf16[8,72,256]{2,1,0:T(8,128)(2,1)} custom-call(bf16[4,216,512]{2,1,0:T(8,128)(2,1)S(1)} %all-to-all-done.1.qkv_ref), custom_call_target="tpu_custom_call" | custom-call | flops 2147483648 | bytes 1500000 | tf_op jit(solution)/shard_map/pallas_call | solution.py:25
  56.1 0.0 copy-start.6
  56.1 3.9 %all-to-all-start.2 = ((bf16[8,72,256]{2,1,0:T(8,128)(2,1)}), bf16[8,72,256]{2,1,0:T(8,128)(2,1)S(1)}, u32[]{:S(2)}, u32[]{:S(2)}) async-start(bf16[8,72,256]{2,1,0:T(8,128)(2,1)} %shard_map.95), calls=%async_computation.2 | async-start | bytes 589824 | tf_op jit(solution)/shard_map/all_to_all | solution.py:280
  60.0 0.0 collective-permute-done.2
  60.1 8.0 %all-to-all-done.2 = bf16[8,72,256]{2,1,0:T(8,128)(2,1)S(1)} async-done(((bf16[8,72,256]{2,1,0:T(8,128)(2,1)}), bf16[8,72,256]{2,1,0:T(8,128)(2,1)S(1)}, u32[]{:S(2)}, u32[]{:S(2)}) %all-to-all-start.2) | async-done | bytes 294944 | tf_op jit(solution)/shard_map/all_to_all | solution.py:280
  68.0 0.0 copy-done.1
  68.0 0.9 %shard_map.97 = (bf16[32,1152]{1,0:T(8,128)(2,1)S(1)}, bf16[32,1152]{1,0:T(8,128)(2,1)S(1)}) custom-call(bf16[2,288,256]{2,1,0:T(8,128)(2,1)S(1)} %bitcast.14, bf16[288,1152]{1,0:T(8,128)(2,1)S(1)} %bitcast.16, bf16[288,1152]{1,0:T(8,128)(2,1)S(1)} %bitcast.18, bf16[256,1152]{1,0:T(8,128)(2,1)S(1)} %bitcast.11, f32[1,1152]{1,0:T(1,128)S(1)} %copy-done.1, ...), custom_call_target="tpu_custom_call" | custom-call | flops 84934656 | bytes 2000000 | tf_op jit(solution)/shard_map/pallas_call | solution.py:25
  68.9 8.2 %collective-permute-start.3 = (bf16[32,1152]{1,0:T(8,128)(2,1)S(1)}, bf16[32,1152]{1,0:T(8,128)(2,1)S(1)}, u32[]{:S(2)}, u32[]{:S(2)}) collective-permute-start(bf16[32,1152]{1,0:T(8,128)(2,1)S(1)} %get-tuple-element.15.e_ref), channel_id=1, source_target_pairs={{0,8},{8,16},{16,24},{24,32},{32,40},{40,48},{48,56},{56,64},{64,7... | collective-permute-start | bytes 221192 | tf_op jit(solution)/shard_map/ppermute | solution.py:290
  77.2 1.9 %collective-permute-start.4 = (bf16[32,1152]{1,0:T(8,128)(2,1)S(1)}, bf16[32,1152]{1,0:T(8,128)(2,1)S(1)}, u32[]{:S(2)}, u32[]{:S(2)}) collective-permute-start(bf16[32,1152]{1,0:T(8,128)(2,1)S(1)} %get-tuple-element.16.w_ref), channel_id=1, source_target_pairs={{0,504},{8,0},{16,8},{24,16},{32,24},{40,32},{48,40},{56,48},{64,5... | collective-permute-start | bytes 221192 | tf_op jit(solution)/shard_map/ppermute | solution.py:291
  79.1 0.1 copy.10.bw_ref
  79.2 0.9 shard_map.96.lay_ref
  80.0 0.0 collective-permute-done.3.prev_ref
  80.1 4.9 %collective-permute-done.4.next_ref = bf16[32,1152]{1,0:T(8,128)(2,1)S(1)} collective-permute-done((bf16[32,1152]{1,0:T(8,128)(2,1)S(1)}, bf16[32,1152]{1,0:T(8,128)(2,1)S(1)}, u32[]{:S(2)}, u32[]{:S(2)}) %collective-permute-start.4) | collective-permute-done | bytes 73760 | tf_op jit(solution)/shard_map/ppermute | solution.py:291
  84.9 1.2 %shard_map.98 = bf16[256,1152]{1,0:T(8,128)(2,1)} custom-call(bf16[256,1152]{1,0:T(8,128)(2,1)S(1)} %shard_map.96.lay_ref, bf16[32,1152]{1,0:T(8,128)(2,1)S(1)} %get-tuple-element.15.e_ref, bf16[32,1152]{1,0:T(8,128)(2,1)S(1)} %get-tuple-element.16.w_ref, bf16[32,1152]{1,0:T(8,128)(2,1)S(1)} %collective-permute-done.3.prev_ref, ...), custom_call_target="tpu_custom_call" | custom-call | flops 37748736 | bytes 1500000 | tf_op jit(solution)/shard_map/pallas_call | solution.py:25
  (7 shorter events, 0.0 us)
Async XLA Ops:
  2.1 4.2 %copy-start = (bf16[1,256,1152]{2,1,0:T(8,128)(2,1)S(1)}, bf16[1,256,1152]{2,1,0:T(8,128)(2,1)}, u32[]{:S(2)}) copy-start(bf16[1,256,1152]{2,1,0:T(8,128)(2,1)} %param.9) | copy-start | bytes 1769476
  2.1 25.2 %copy-start.2 = (f32[1,1152]{1,0:T(1,128)S(1)}, f32[1,1152]{1,0:T(1,128)}, u32[]{:S(2)}) copy-start(f32[1,1152]{1,0:T(1,128)} %shift_ref.1) | copy-start | bytes 13828
  2.1 25.2 %copy-start.3 = (f32[1,1152]{1,0:T(1,128)S(1)}, f32[1,1152]{1,0:T(1,128)}, u32[]{:S(2)}) copy-start(f32[1,1152]{1,0:T(1,128)} %scale_ref.1) | copy-start | bytes 13828
  2.1 21.4 %all-to-all-start = ((bf16[4,2,72,1152]{3,2,1,0:T(8,128)(2,1)}), bf16[4,2,72,1152]{3,2,1,0:T(8,128)(2,1)S(1)}, u32[]{:S(2)}, u32[]{:S(2)}) async-start(bf16[4,2,72,1152]{3,2,1,0:T(8,128)(2,1)} %shard_map.91), calls=%async_computation | async-start | bytes 2654208 | tf_op jit(solution)/shard_map/all_to_all | solution.py:241
  6.3 17.3 %collective-permute-start = (bf16[256,1152]{1,0:T(8,128)(2,1)S(1)}, bf16[256,1152]{1,0:T(8,128)(2,1)S(1)}, u32[]{:S(2)}, u32[]{:S(2)}) collective-permute-start(bf16[256,1152]{1,0:T(8,128)(2,1)S(1)} %bitcast.9), channel_id=1, source_target_pairs={{0,1},{1,0},{2,3},{3,2},{4,5},{5,4},{6,7},{7,6},{8,9},{9,8},{10,11... | collective-permute-start | bytes 1769480 | tf_op jit(solution)/shard_map/ppermute | solution.py:227
  23.6 6.4 %collective-permute-start.1 = (bf16[4,2,72,1152]{3,2,1,0:T(8,128)(2,1)S(1)}, bf16[4,2,72,1152]{3,2,1,0:T(8,128)(2,1)S(1)}, u32[]{:S(2)}, u32[]{:S(2)}) collective-permute-start(bf16[4,2,72,1152]{3,2,1,0:T(8,128)(2,1)S(1)} %all-to-all-done.mine4_ref), channel_id=1, source_target_pairs={{0,8},{8,0},{1,9},{9,1},{2,10},{10,2},{3,11},{11,3},{4,12},{12,4},... | collective-permute-start | bytes 3981320 | tf_op jit(solution)/shard_map/ppermute | solution.py:243
  32.5 17.0 %all-to-all-start.1 = ((bf16[4,216,512]{2,1,0:T(8,128)(2,1)}), bf16[4,216,512]{2,1,0:T(8,128)(2,1)S(1)}, u32[]{:S(2)}, u32[]{:S(2)}) async-start(bf16[4,216,512]{2,1,0:T(8,128)(2,1)} %get-tuple-element.13), calls=%async_computation.1 | async-start | bytes 1769472 | tf_op jit(solution)/shard_map/all_to_all | solution.py:269
  36.8 31.3 %copy-start.1 = (f32[1,1152]{1,0:T(1,128)S(1)}, f32[1,1152]{1,0:T(1,128)}, u32[]{:S(2)}) copy-start(f32[1,1152]{1,0:T(1,128)} %gate_ref.3) | copy-start | bytes 13828
  36.8 31.3 %copy-start.4 = (s32[1,32]{1,0:T(1,128)S(1)}, s32[1,32]{1,0:T(1,128)}, u32[]{:S(2)}) copy-start(s32[1,32]{1,0:T(1,128)} %east_ref.3) | copy-start | bytes 388
  36.8 31.3 %copy-start.5 = (s32[1,32]{1,0:T(1,128)S(1)}, s32[1,32]{1,0:T(1,128)}, u32[]{:S(2)}) copy-start(s32[1,32]{1,0:T(1,128)} %west_ref.3) | copy-start | bytes 388
  36.8 23.3 %collective-permute-start.2 = (bf16[4,72,1152]{2,1,0:T(8,128)(2,1)S(1)}, bf16[4,72,1152]{2,1,0:T(8,128)(2,1)S(1)}, u32[]{:S(2)}, u32[]{:S(2)}) collective-permute-start(bf16[4,72,1152]{2,1,0:T(8,128)(2,1)S(1)} %get-tuple-element.14), channel_id=1, source_target_pairs={{0,17},{17,0},{1,16},{16,1},{2,19},{19,2},{3,18},{18,3},{4,21},{21... | collective-permute-start | bytes 1990664 | tf_op jit(solution)/shard_map/ppermute | solution.py:268
  56.1 23.0 %copy-start.6 = (s32[64,32]{0,1:T(8,128)S(1)}, s32[64,32]{0,1:T(8,128)}, u32[]{:S(2)}) copy-start(s32[64,32]{0,1:T(8,128)} %param.17) | copy-start | bytes 24580
  56.1 11.9 %all-to-all-start.2 = ((bf16[8,72,256]{2,1,0:T(8,128)(2,1)}), bf16[8,72,256]{2,1,0:T(8,128)(2,1)S(1)}, u32[]{:S(2)}, u32[]{:S(2)}) async-start(bf16[8,72,256]{2,1,0:T(8,128)(2,1)} %shard_map.95), calls=%async_computation.2 | async-start | bytes 589824 | tf_op jit(solution)/shard_map/all_to_all | solution.py:280
  68.9 11.1 %collective-permute-start.3 = (bf16[32,1152]{1,0:T(8,128)(2,1)S(1)}, bf16[32,1152]{1,0:T(8,128)(2,1)S(1)}, u32[]{:S(2)}, u32[]{:S(2)}) collective-permute-start(bf16[32,1152]{1,0:T(8,128)(2,1)S(1)} %get-tuple-element.15.e_ref), channel_id=1, source_target_pairs={{0,8},{8,16},{16,24},{24,32},{32,40},{40,48},{48,56},{56,64},{64,7... | collective-permute-start | bytes 221192 | tf_op jit(solution)/shard_map/ppermute | solution.py:290
  77.2 7.8 %collective-permute-start.4 = (bf16[32,1152]{1,0:T(8,128)(2,1)S(1)}, bf16[32,1152]{1,0:T(8,128)(2,1)S(1)}, u32[]{:S(2)}, u32[]{:S(2)}) collective-permute-start(bf16[32,1152]{1,0:T(8,128)(2,1)S(1)} %get-tuple-element.16.w_ref), channel_id=1, source_target_pairs={{0,504},{8,0},{16,8},{24,16},{32,24},{40,32},{48,40},{56,48},{64,5... | collective-permute-start | bytes 221192 | tf_op jit(solution)/shard_map/ppermute | solution.py:291
